TPU v7x, 32 devices: a whole 2x2x4 slice. The times are simulated.
32 devices in a mesh: space: 8 (over z, x), chan: 4 (over y, core).
Axes of the slice: x: 2, y: 2, z: 4, core: 2. Of those that a mesh axis runs over, the one named last changes fastest.
Arguments:
- volume: bfloat16 [16, 256, 8, 128], P('space', 'chan'), may hold values from -6 to 6
- kernel: bfloat16 [27, 256, 256], P(None, 'chan'), may hold values from -0.078125 to 0.078125
- cotangent: bfloat16 [16, 256, 8, 128], P('space', 'chan'), may hold values from -6 to 6
Outputs:
- output_map: bfloat16 [16, 256, 8, 128], P('space', 'chan')
- input_grad: bfloat16 [16, 256, 8, 128], P('space', 'chan')
- kernel_grad: float32 [27, 256, 256], P(None, 'chan')
All inputs are finite; a program needn't handle non-finite values.
Results may differ from a plain program's by a relative error of at most 0.001.
Values may be sent and summed in bfloat16 or wider, within the bound.
No kernel may reach another device: no remote copies, remote signals or barrier semaphores. Data moves between devices by JAX's collectives and lax.ppermute only.
A program may use at most 128 MiB of HBM per device.

v0:
```python
import math

import jax
import jax.numpy as jnp
from jax import lax
from jax.sharding import PartitionSpec as P


def with_halo(block, sides, width):
    for axis, dim in sides:
        count = lax.axis_size(axis)
        forward = [(i, i + 1) for i in range(count - 1)]
        backward = [(target, source) for source, target in forward]
        low = lax.ppermute(
            lax.slice_in_dim(block, block.shape[dim] - width, None, axis=dim), axis, forward
        )
        high = lax.ppermute(lax.slice_in_dim(block, 0, width, axis=dim), axis, backward)
        block = jnp.concatenate([low, block, high], axis=dim)
    return block


def plane_stack(piece, height, width, flipped):
    cells = height * width
    padded = jnp.pad(piece, ((0, 0), (0, 0), (width + 1, width + 1)))
    column = lax.broadcasted_iota(jnp.int32, (1, 1, cells), 2) % width
    windows = []
    for row_step in range(3):
        for col_step in range(3):
            row_from = 2 - row_step if flipped else row_step
            col_from = 2 - col_step if flipped else col_step
            offset = width + 1 + (row_from - 1) * width + (col_from - 1)
            shifted = padded[:, :, offset : offset + cells]
            target = column + (col_from - 1)
            inside = ((target >= 0) & (target < width)).astype(piece.dtype)
            windows.append(shifted * inside)
    return jnp.concatenate(windows, axis=1)


def on_device(volume, kernel, cotangent):
    depth, chans_local, height, width = volume.shape
    filters_local = cotangent.shape[1]
    cells = height * width
    scale_factor = 1.0 / math.sqrt(depth * lax.axis_size("space") * height * width)
    volume_flat = volume.reshape(depth, chans_local, cells)
    grad_flat = cotangent.reshape(depth, filters_local, cells)
    columns = lax.all_to_all(kernel, "chan", split_axis=2, concat_axis=1, tiled=True)
    init_output = jnp.zeros((depth, filters_local, cells), jnp.float32)
    init_input = jnp.zeros((depth, chans_local, cells), jnp.float32)
    rims = with_halo(volume_flat, (("space", 0),), 1)
    piece = lax.all_gather(rims, "chan", axis=1, tiled=True)
    output_acc = init_output
    count = piece.shape[1]
    stacked = plane_stack(piece, height, width, False)
    grads = []
    for depth_step in range(3):
        window = stacked[depth_step : depth_step + depth]
        taps = kernel[9 * depth_step : 9 * depth_step + 9]
        weights = jnp.transpose(taps, (1, 0, 2)).reshape(filters_local, 9 * count)
        output_acc = output_acc + jnp.einsum(
            "fj,zjp->zfp", weights, window, preferred_element_type=jnp.float32
        )
        term = jnp.einsum("zfp,zjp->fj", grad_flat, window, preferred_element_type=jnp.float32)
        grads.append(jnp.transpose(term.reshape(filters_local, 9, count), (1, 0, 2)))
    kernel_acc = jnp.concatenate(grads, axis=0)
    output_acc, kernel_acc = (output_acc, kernel_acc)
    grad_ext = with_halo(grad_flat, (("space", 0),), 1)
    total = init_input
    piece = lax.all_gather(grad_ext, "chan", axis=1, tiled=True)
    count = piece.shape[1]
    stacked = plane_stack(piece, height, width, True)
    for depth_step in range(3):
        window = stacked[2 - depth_step : 2 - depth_step + depth]
        taps = columns[9 * depth_step : 9 * depth_step + 9]
        weights = jnp.transpose(taps, (2, 0, 1)).reshape(chans_local, 9 * count)
        total = total + jnp.einsum(
            "kj,zjp->zkp", weights, window, preferred_element_type=jnp.float32
        )
    kernel_grad = lax.psum(kernel_acc, "space") * scale_factor
    output_map = output_acc.astype(jnp.bfloat16).reshape(depth, filters_local, height, width)
    input_grad = total.astype(jnp.bfloat16).reshape(depth, chans_local, height, width)
    return (output_map, input_grad, kernel_grad)


def solution(mesh):
    return jax.shard_map(
        on_device,
        mesh=mesh,
        in_specs=(
            P("space", "chan", None, None),
            P(None, "chan", None),
            P("space", "chan", None, None),
        ),
        out_specs=(
            P("space", "chan", None, None),
            P("space", "chan", None, None),
            P(None, "chan", None),
        ),
        check_vma=False,
    )
```

profile of v0, /device:TPU:0, one launch (start us, length us, event | category | flops | bytes accessed | tf_op | source)
XLA Modules:
  0.0 226.6 jit_solution(10698282163954191732)
XLA Ops:
  8.4 4.8 %collective-permute-start.2 = (bf16[1,64,1024]{2,1,0:T(8,128)(2,1)S(1)}, bf16[1,64,1024]{2,1,0:T(8,128)(2,1)S(1)}, u32[]{:S(2)}, u32[]{:S(2)}) collective-permute-start(bf16[1,64,1024]{2,1,0:T(8,128)(2,1)S(1)} %slice.138), channel_id=1, source_target_pairs={{0,4},{4,8},{8,12},{12,16},{16,20},{20,24},{24,28},{1,5},{5,9},{9,... | collective-permute-start | bytes 393224 | tf_op jit(solution)/shard_map/ppermute | solution.py:14
  16.0 4.2 %collective-permute-done.3 = bf16[1,64,1024]{2,1,0:T(8,128)(2,1)S(1)} collective-permute-done((bf16[1,64,1024]{2,1,0:T(8,128)(2,1)S(1)}, bf16[1,64,1024]{2,1,0:T(8,128)(2,1)S(1)}, u32[]{:S(2)}, u32[]{:S(2)}) %collective-permute-start.3) | collective-permute-done | bytes 131104 | tf_op jit(solution)/shard_map/ppermute | solution.py:17
  22.2 4.4 %collective-permute-start = (bf16[1,64,1024]{2,1,0:T(8,128)(2,1)S(1)}, bf16[1,64,1024]{2,1,0:T(8,128)(2,1)S(1)}, u32[]{:S(2)}, u32[]{:S(2)}) collective-permute-start(bf16[1,64,1024]{2,1,0:T(8,128)(2,1)S(1)} %slice.120), channel_id=1, source_target_pairs={{0,4},{4,8},{8,12},{12,16},{16,20},{20,24},{24,28},{1,5},{5,9},{9,... | collective-permute-start | bytes 393224 | tf_op jit(solution)/shard_map/ppermute | solution.py:14
  29.0 4.4 %collective-permute-done.1 = bf16[1,64,1024]{2,1,0:T(8,128)(2,1)S(1)} collective-permute-done((bf16[1,64,1024]{2,1,0:T(8,128)(2,1)S(1)}, bf16[1,64,1024]{2,1,0:T(8,128)(2,1)S(1)}, u32[]{:S(2)}, u32[]{:S(2)}) %collective-permute-start.1) | collective-permute-done | bytes 131104 | tf_op jit(solution)/shard_map/ppermute | solution.py:17
  34.4 3.1 %copy.26 = bf16[27,64,256]{1,0,2:T(8,128)(2,1)S(1)} copy(bf16[27,64,256]{2,1,0:T(8,128)(2,1)S(1)} %copy-done.3) | data formatting | bytes 1769472 | tf_op args[1]
  37.4 2.4 %reshape.125 = bf16[4,2,55296]{2,1,0:T(2,128)(2,1)} reshape(bf16[256,27,64]{2,1,0:T(8,128)(2,1)S(1)} %bitcast.73) | data formatting | bytes 1769472
  39.8 4.2 %all-to-all-start = ((bf16[4,2,55296]{2,1,0:T(2,128)(2,1)}), bf16[4,2,55296]{2,1,0:T(2,128)(2,1)}, u32[]{:S(2)}, u32[]{:S(2)}) async-start(bf16[4,2,55296]{2,1,0:T(2,128)(2,1)} %reshape.125), calls=%async_computation | async-start | bytes 1769472 | tf_op jit(solution)/shard_map/all_to_all | solution.py:46
  46.8 10.6 %all-to-all-done = bf16[4,2,55296]{2,1,0:T(2,128)(2,1)} async-done(((bf16[4,2,55296]{2,1,0:T(2,128)(2,1)}), bf16[4,2,55296]{2,1,0:T(2,128)(2,1)}, u32[]{:S(2)}, u32[]{:S(2)}) %all-to-all-start) | async-done | bytes 884768 | tf_op jit(solution)/shard_map/all_to_all | solution.py:46
  57.3 3.5 %reshape.126 = bf16[256,27,64]{2,1,0:T(8,128)(2,1)S(1)} reshape(bf16[4,2,55296]{2,1,0:T(2,128)(2,1)} %all-to-all-done) | data formatting | bytes 1769472
  67.4 3.8 %fusion.29 = bf16[4,2304,1024]{2,1,0:T(8,128)(2,1)} fusion(bf16[4,256,1024]{2,1,0:T(8,128)(2,1)} %all-gather.5.cloned.1.call-done, bf16[1024]{0:T(1024)(128)(2,1)S(1)} %fusion.73), kind=kLoop, calls=%fused_computation.48 | loop fusion | flops 4194303 | bytes 4196352
  73.1 2.6 %fusion.33 = bf16[4,2304,1024]{2,1,0:T(8,128)(2,1)} fusion(bf16[4,2304,1024]{2,1,0:T(8,128)(2,1)} %fusion.31, bf16[4,256,1024]{2,1,0:T(8,128)(2,1)S(1)} %copy-done, bf16[1024]{0:T(1024)(128)(2,1)S(1)} %fusion.75), kind=kLoop, calls=%fused_computation.52 | loop fusion | flops 4194304 | bytes 4196352
  75.7 2.5 %fusion.35 = bf16[4,2304,1024]{2,1,0:T(8,128)(2,1)} fusion(bf16[4,2304,1024]{2,1,0:T(8,128)(2,1)} %fusion.33, bf16[4,256,1024]{2,1,0:T(8,128)(2,1)S(1)} %copy-done, bf16[1024]{0:T(1024)(128)(2,1)S(1)} %fusion.73), kind=kLoop, calls=%fused_computation.54 | loop fusion | flops 4194304 | bytes 4196352
  80.1 4.5 %fusion.37 = (bf16[4,2304,1024]{2,1,0:T(8,128)(2,1)}, bf16[4,2304,1024]{2,1,0:T(8,128)(2,1)S(1)}) fusion(bf16[4,2304,1024]{2,1,0:T(8,128)(2,1)} %multiply_dynamic-update-slice_fusion, bf16[4,256,1024]{2,1,0:T(8,128)(2,1)S(1)} %copy-done, bf16[1024]{0:T(1024)(128)(2,1)S(1)} %fusion.75, bf16[4,256,1024]{2,1,0:T(8,128)(2,1)} %all-gather.3.cloned.1.call-done), kind=kLoop, calls=%fused_computation.56 | loop fusion | flops 7340031 | bytes 8390656
  84.5 2.6 %fusion.39 = bf16[4,2304,1024]{2,1,0:T(8,128)(2,1)} fusion(bf16[4,2304,1024]{2,1,0:T(8,128)(2,1)} %get-tuple-element.23, bf16[4,256,1024]{2,1,0:T(8,128)(2,1)S(1)} %copy-done, bf16[1024]{0:T(1024)(128)(2,1)S(1)} %fusion.73), kind=kLoop, calls=%fused_computation.58 | loop fusion | flops 4194304 | bytes 4196352
  87.2 2.6 %fusion.41 = (bf16[4,2304,1024]{2,1,0:T(8,128)(2,1)}, bf16[4,2304,1024]{2,1,0:T(8,128)(2,1)S(1)}) fusion(bf16[4,2304,1024]{2,1,0:T(8,128)(2,1)} %fusion.39, bf16[4,256,1024]{2,1,0:T(8,128)(2,1)S(1)} %copy-done, bf16[1024]{0:T(1024)(128)(2,1)S(1)} %fusion.77, bf16[4,2304,1024]{2,1,0:T(8,128)(2,1)S(1)} %get-tuple-element.24, bf16[4,256,1024]{2,1,0:T(8,128)(2,1)S(1)} %copy-done.1), kind=kLoop, calls=%fused_computation.60 | loop fusion | flops 7340032 | bytes 8390656
  91.2 3.9 %fusion.43 = (bf16[4,2304,1024]{2,1,0:T(8,128)(2,1)}, bf16[4,2304,1024]{2,1,0:T(8,128)(2,1)S(1)}) fusion(bf16[4,2304,1024]{2,1,0:T(8,128)(2,1)} %get-tuple-element.21, bf16[4,256,1024]{2,1,0:T(8,128)(2,1)S(1)} %copy-done, bf16[1024]{0:T(1024)(128)(2,1)S(1)} %fusion.75, bf16[4,2304,1024]{2,1,0:T(8,128)(2,1)S(1)} %fusion.17, bf16[4,256,1024]{2,1,0:T(8,128)(2,1)S(1)} %copy-done.1), kind=kLoop, calls=%fused_computation.62 | loop fusion | flops 7340032 | bytes 8390656 | tf_op jit(solution)/shard_map/concatenate | solution.py:36
  99.8 3.0 %convolution_bitcast_fusion.2 = f32[64,2304]{1,0:T(8,128)S(1)} fusion(bf16[4,2304,1024]{2,1,0:T(8,128)(2,1)S(1)} %fusion.27, bf16[2,64,1024]{2,1,0:T(8,128)(2,1)S(1)} %reshape.102), kind=kOutput, calls=%fused_computation.14 | convolution fusion | flops 603979776 | bytes 19726336 | tf_op jit(solution)/shard_map/zfp,zjp->fj/dot_general | solution.py:62
  102.8 3.1 %convolution_bitcast_fusion.1 = f32[64,2304]{1,0:T(8,128)S(1)} fusion(bf16[4,2304,1024]{2,1,0:T(8,128)(2,1)S(1)} %fusion.27, bf16[2,64,1024]{2,1,0:T(8,128)(2,1)S(1)} %reshape.102), kind=kOutput, calls=%fused_computation.13 | convolution fusion | flops 603979776 | bytes 19726336 | tf_op jit(solution)/shard_map/zfp,zjp->fj/dot_general | solution.py:62
  106.2 3.8 %convolution_bitcast_fusion = f32[64,2304]{1,0:T(8,128)} fusion(bf16[4,2304,1024]{2,1,0:T(8,128)(2,1)S(1)} %fusion.27, bf16[2,64,1024]{2,1,0:T(8,128)(2,1)S(1)} %reshape.102), kind=kOutput, calls=%fused_computation.12 | convolution fusion | flops 603979776 | bytes 19726336 | tf_op jit(solution)/shard_map/zfp,zjp->fj/dot_general | solution.py:62
  113.2 5.7 %fusion = f32[2,1024,64]{1,2,0:T(8,128)S(1)} fusion(bf16[64,2304,1]{1,0,2:T(8,128)(2,1)} %reshape.115, bf16[4,2304,1024]{2,1,0:T(8,128)(2,1)} %get-tuple-element.19), kind=kOutput, calls=%fused_computation | convolution fusion | flops 603979776 | bytes 10256384 | tf_op jit(solution)/shard_map/kj,zjp->zkp/dot_general | solution.py:75
  118.9 5.7 %fusion.2 = f32[2,1024,64]{1,2,0:T(8,128)S(1)} fusion(bf16[64,2304,1]{1,0,2:T(8,128)(2,1)S(1)} %copy-done.8, bf16[4,2304,1024]{2,1,0:T(8,128)(2,1)} %get-tuple-element.19), kind=kOutput, calls=%fused_computation.2 | convolution fusion | flops 603979776 | bytes 10256384 | tf_op jit(solution)/shard_map/kj,zjp->zkp/dot_general | solution.py:75
  124.7 5.7 %fusion.59 = bf16[2,1024,64]{1,2,0:T(8,128)(2,1)S(1)} fusion(f32[2,1024,64]{1,2,0:T(8,128)S(1)} %fusion, f32[2,1024,64]{1,2,0:T(8,128)S(1)} %fusion.2, bf16[64,2304,1]{1,0,2:T(8,128)(2,1)S(1)} %copy-done.4, bf16[4,2304,1024]{2,1,0:T(8,128)(2,1)} %get-tuple-element.19), kind=kOutput, calls=%fused_computation.72 | convolution fusion | flops 604372992 | bytes 11042816 | tf_op jit(solution)/shard_map/kj,zjp->zkp/dot_general | solution.py:75
  137.3 78.6 %all-reduce.4.cloned.1.call-done = f32[27,64,256]{2,0,1:T(8,128)} async-done(((f32[27,64,256]{2,0,1:T(8,128)}), f32[27,64,256]{2,0,1:T(8,128)}) %all-reduce.4.cloned.1.call-update) | async-done | bytes 1769488 | tf_op jit(solution)/shard_map/psum | solution.py:78
  217.7 2.2 copy.31
  (90 shorter events, 40.2 us)
Async XLA Ops:
  7.2 20.7 %copy-start.5 = (bf16[2,64,8,128]{3,2,1,0:T(8,128)(2,1)S(1)}, bf16[2,64,8,128]{3,2,1,0:T(8,128)(2,1)}, u32[]{:S(2)}) copy-start(bf16[2,64,8,128]{3,2,1,0:T(8,128)(2,1)} %param.3) | copy-start | bytes 786436
  7.2 27.2 %copy-start.3 = (bf16[27,64,256]{2,1,0:T(8,128)(2,1)S(1)}, bf16[27,64,256]{2,1,0:T(8,128)(2,1)}, u32[]{:S(2)}) copy-start(bf16[27,64,256]{2,1,0:T(8,128)(2,1)} %param.4) | copy-start | bytes 2654212
  7.2 60.2 %all-gather.5.cloned.1.call-start = ((), (), s32[]{:S(2)}) async-start(), calls=%async_computation.2 | async-start | bytes 2621440 | tf_op jit(solution)/shard_map/all_gather | solution.py:68
  8.4 7.6 %collective-permute-start.2 = (bf16[1,64,1024]{2,1,0:T(8,128)(2,1)S(1)}, bf16[1,64,1024]{2,1,0:T(8,128)(2,1)S(1)}, u32[]{:S(2)}, u32[]{:S(2)}) collective-permute-start(bf16[1,64,1024]{2,1,0:T(8,128)(2,1)S(1)} %slice.138), channel_id=1, source_target_pairs={{0,4},{4,8},{8,12},{12,16},{16,20},{20,24},{24,28},{1,5},{5,9},{9,... | collective-permute-start | bytes 393224 | tf_op jit(solution)/shard_map/ppermute | solution.py:14
  13.3 6.9 %collective-permute-start.3 = (bf16[1,64,1024]{2,1,0:T(8,128)(2,1)S(1)}, bf16[1,64,1024]{2,1,0:T(8,128)(2,1)S(1)}, u32[]{:S(2)}, u32[]{:S(2)}) collective-permute-start(bf16[1,64,1024]{2,1,0:T(8,128)(2,1)S(1)} %slice.140), channel_id=1, source_target_pairs={{4,0},{8,4},{12,8},{16,12},{20,16},{24,20},{28,24},{5,1},{9,5},{13... | collective-permute-start | bytes 393224 | tf_op jit(solution)/shard_map/ppermute | solution.py:17
  21.1 59.0 %all-gather.3.cloned.1.call-start = ((), (), s32[]{:S(2)}) async-start(), calls=%async_computation.1 | async-start | bytes 2621440 | tf_op jit(solution)/shard_map/all_gather | solution.py:50
  22.2 6.9 %collective-permute-start = (bf16[1,64,1024]{2,1,0:T(8,128)(2,1)S(1)}, bf16[1,64,1024]{2,1,0:T(8,128)(2,1)S(1)}, u32[]{:S(2)}, u32[]{:S(2)}) collective-permute-start(bf16[1,64,1024]{2,1,0:T(8,128)(2,1)S(1)} %slice.120), channel_id=1, source_target_pairs={{0,4},{4,8},{8,12},{12,16},{16,20},{20,24},{24,28},{1,5},{5,9},{9,... | collective-permute-start | bytes 393224 | tf_op jit(solution)/shard_map/ppermute | solution.py:14
  26.6 6.9 %collective-permute-start.1 = (bf16[1,64,1024]{2,1,0:T(8,128)(2,1)S(1)}, bf16[1,64,1024]{2,1,0:T(8,128)(2,1)S(1)}, u32[]{:S(2)}, u32[]{:S(2)}) collective-permute-start(bf16[1,64,1024]{2,1,0:T(8,128)(2,1)S(1)} %slice.122), channel_id=1, source_target_pairs={{4,0},{8,4},{12,8},{16,12},{20,16},{24,20},{28,24},{5,1},{9,5},{13... | collective-permute-start | bytes 393224 | tf_op jit(solution)/shard_map/ppermute | solution.py:17
  39.8 17.5 %all-to-all-start = ((bf16[4,2,55296]{2,1,0:T(2,128)(2,1)}), bf16[4,2,55296]{2,1,0:T(2,128)(2,1)}, u32[]{:S(2)}, u32[]{:S(2)}) async-start(bf16[4,2,55296]{2,1,0:T(2,128)(2,1)} %reshape.125), calls=%async_computation | async-start | bytes 1769472 | tf_op jit(solution)/shard_map/all_to_all | solution.py:46
  44.1 171.8 %all-reduce.4.cloned.1.call-start = ((), (), s32[]{:S(2)}) async-start(), calls=%async_computation.3 | async-start | bytes 4194304 | tf_op jit(solution)/shard_map/psum | solution.py:78
  67.4 3.8 %copy-start = (bf16[4,256,1024]{2,1,0:T(8,128)(2,1)S(1)}, bf16[4,256,1024]{2,1,0:T(8,128)(2,1)}, u32[]{:S(2)}) copy-start(bf16[4,256,1024]{2,1,0:T(8,128)(2,1)} %all-gather.5.cloned.1.call-done) | copy-start | bytes 6291460
  84.5 2.7 %copy-start.1 = (bf16[4,256,1024]{2,1,0:T(8,128)(2,1)S(1)}, bf16[4,256,1024]{2,1,0:T(8,128)(2,1)}, u32[]{:S(2)}) copy-start(bf16[4,256,1024]{2,1,0:T(8,128)(2,1)} %all-gather.3.cloned.1.call-done) | copy-start | bytes 6291460
  99.8 6.4 %copy-start.2 = (bf16[4,2304,1024]{2,1,0:T(8,128)(2,1)}, bf16[4,2304,1024]{2,1,0:T(8,128)(2,1)S(1)}, u32[]{:S(2)}) copy-start(bf16[4,2304,1024]{2,1,0:T(8,128)(2,1)S(1)} %fusion.27) | copy-start | bytes 56623108
  113.2 5.7 %copy-start.8 = (bf16[64,2304,1]{1,0,2:T(8,128)(2,1)S(1)}, bf16[64,2304,1]{1,0,2:T(8,128)(2,1)}, u32[]{:S(2)}) copy-start(bf16[64,2304,1]{1,0,2:T(8,128)(2,1)} %reshape.114) | copy-start | bytes 884740
  113.2 18.0 %slice-start = ((s8[18874368]{0:T(1024)(128)(4,1)}), s8[4194304]{0:T(1024)(128)(4,1)S(1)}, s32[]{:S(2)}) async-start(s8[18874368]{0:T(1024)(128)(4,1)} %bitcast.70), calls=%async_computation.4 | async-start | bytes 8388608
  113.2 18.0 %slice-start.1 = ((s8[18874368]{0:T(1024)(128)(4,1)}), s8[4194304]{0:T(1024)(128)(4,1)S(1)}, s32[]{:S(2)}) async-start(s8[18874368]{0:T(1024)(128)(4,1)} %bitcast.70), calls=%async_computation.5 | async-start | bytes 8388608
  118.9 5.8 %copy-start.4 = (bf16[64,2304,1]{1,0,2:T(8,128)(2,1)S(1)}, bf16[64,2304,1]{1,0,2:T(8,128)(2,1)}, u32[]{:S(2)}) copy-start(bf16[64,2304,1]{1,0,2:T(8,128)(2,1)} %reshape.113) | copy-start | bytes 884740
  118.9 12.3 %slice-start.2 = ((s8[18874368]{0:T(1024)(128)(4,1)}), s8[4194304]{0:T(1024)(128)(4,1)S(1)}, s32[]{:S(2)}) async-start(s8[18874368]{0:T(1024)(128)(4,1)} %bitcast.70), calls=%async_computation.6 | async-start | bytes 8388608
  118.9 12.3 %slice-start.3 = ((s8[18874368]{0:T(1024)(128)(4,1)}), s8[4194304]{0:T(1024)(128)(4,1)S(1)}, s32[]{:S(2)}) async-start(s8[18874368]{0:T(1024)(128)(4,1)} %bitcast.70), calls=%async_computation.7 | async-start | bytes 8388608
  124.7 6.5 %slice-start.4 = ((s8[18874368]{0:T(1024)(128)(4,1)}), s8[2097152]{0:T(1024)(128)(4,1)S(1)}, s32[]{:S(2)}) async-start(s8[18874368]{0:T(1024)(128)(4,1)} %bitcast.70), calls=%async_computation.8 | async-start | bytes 4194304
  124.7 6.5 %copy-start.6 = (bf16[64,2304,1]{1,0,2:T(8,128)(2,1)S(1)}, bf16[64,2304,1]{1,0,2:T(8,128)(2,1)}, u32[]{:S(2)}) copy-start(bf16[64,2304,1]{1,0,2:T(8,128)(2,1)} %reshape.111) | copy-start | bytes 884740
  131.2 1.8 copy-start.7
Sparse Core Ops, SparseCore 0:
  21.2 23.7 all-gather.4
  46.6 22.8 all-gather.2
  113.3 102.5 all-reduce.3
where the time goes:
time: 231 us; the launch traced here: 227 us
  waiting for transfers between devices  99.1 us (43%)
  other arithmetic  37.6 us (16%)
  matrix products  32.3 us (14%)
  local copies, waits for them, and re-layouts  27 us (12%)
  starting transfers between devices  16.1 us (7%)
  between operations  14.4 us (6%)
    psum x1, waiting for transfers between devices, on_device(): kernel_grad = lax.psum(kernel_acc, 'space') * scale_factor  78.6 us
    unnamed x14, other arithmetic  27.3 us
    dot_general x3, matrix products, on_device(): jnp.einsum('kj,zjp->zkp', weights, window, preferred_element_type=jnp.flo...  17.1 us
    unnamed x34, local copies, waits for them, and re-layouts  13 us
    all_to_all x1, waiting for transfers between devices, on_device(): lax.all_to_all(kernel, 'chan', split_axis=2, concat_axis=1, tiled=True)  10.6 us
    dot_general x3, matrix products, on_device(): jnp.einsum('zfp,zjp->fj', grad_flat, window, preferred_element_type=jnp.f...  9.88 us
    ppermute x2, starting transfers between devices, with_halo(): lax.ppermute(lax.slice_in_dim(block, block.shape[dim] - width, None, axis...  9.21 us
    ppermute x2, waiting for transfers between devices, with_halo(): lax.ppermute(lax.slice_in_dim(block, 0, width, axis=dim), axis, backward)  8.63 us
  transfers between devices with their start and end apart: 8, of which 6 were waited for; matrix products, arithmetic and copies ran while one was open for 26% of the time, Pallas kernels for 0%

commit v1 on v0

--- a/solution.py
+++ b/solution.py
@@ -1,9 +1,354 @@
+import functools
 import math
 
 import jax
 import jax.numpy as jnp
 from jax import lax
+from jax.experimental import pallas as pl
+from jax.experimental.pallas import tpu as pltpu
 from jax.sharding import PartitionSpec as P
+
+VMEM_LIMIT = 48 * 1024 * 1024
+
+
+def vmem_specs(count):
+    return [pl.BlockSpec(memory_space=pltpu.VMEM)] * count
+
+
+def shifted(block, step, width):
+    if step == 0:
+        return block
+    lane = lax.broadcasted_iota(jnp.int32, block.shape, 1)
+    rolled = pltpu.roll(block.astype(jnp.float32), (-step) % width, 1)
+    kept = (lane + step >= 0) & (lane + step < width)
+    return jnp.where(kept, rolled, 0.0).astype(block.dtype)
+
+
+def kernel_grad_kernel(
+    scale, order, place, own, other, grad, grad_low, grad_high, out_ref, bound_ref, left, right
+):
+    depth, height, chans, width = own.shape
+    filters = grad.shape[2]
+    cells = height * width
+    span = 2 * chans
+
+    def grad_row(plane, row):
+        if plane == 0:
+            return grad_low[row]
+        if plane == depth + 1:
+            return grad_high[row]
+        return grad[plane - 1, row]
+
+    for source, at in ((own, place[0]), (other, 1 - place[0])):
+        for plane in range(depth):
+            for row in range(height):
+                lanes = slice(plane * cells + row * width, plane * cells + (row + 1) * width)
+                block = source[plane, row]
+                for col_step in range(3):
+                    start = pl.multiple_of(col_step * span + at * chans, chans)
+                    right[pl.ds(start, chans), lanes] = shifted(block, col_step - 1, width)
+    for a in range(3):
+        for b in range(3):
+            rows = slice((3 * a + b) * filters, (3 * a + b + 1) * filters)
+            for plane in range(depth):
+                for row in range(height):
+                    lanes = slice(plane * cells + row * width, plane * cells + (row + 1) * width)
+                    at = row - b + 1
+                    if 0 <= at < height:
+                        left[rows, lanes] = grad_row(plane - a + 2, at)
+                    else:
+                        left[rows, lanes] = jnp.zeros((filters, width), left.dtype)
+    total = lax.dot_general(
+        left[...], right[...], (((1,), (1,)), ((), ())), preferred_element_type=jnp.float32
+    )
+    total = total * scale
+    peak = jnp.maximum(jnp.max(jnp.abs(total)), 1e-30)
+    bound_ref[...] = jnp.ceil(jnp.log2(jnp.full(bound_ref.shape, peak, jnp.float32))) + 1.0
+    rows = out_ref.shape[1]
+    for tap in range(27):
+        a, b, c = tap // 9, tap // 3 % 3, tap % 3
+        block = total[(3 * a + b) * filters : (3 * a + b + 1) * filters, c * span : (c + 1) * span]
+        for shard, at in enumerate(order):
+            out_ref[at * 27 + tap] = block[shard * rows : (shard + 1) * rows]
+
+
+def kernel_grad_part(place, own, other, grad, grad_low, grad_high, scale, order):
+    depth, height, chans, width = own.shape
+    filters = grad.shape[2]
+    cells = depth * height * width
+    rows = filters // len(order)
+    return pl.pallas_call(
+        functools.partial(kernel_grad_kernel, scale, order),
+        out_shape=[
+            jax.ShapeDtypeStruct((27 * len(order), rows, 2 * chans), jnp.float32),
+            jax.ShapeDtypeStruct((rows, 2 * chans), jnp.float32),
+        ],
+        in_specs=[pl.BlockSpec(memory_space=pltpu.SMEM)] + vmem_specs(5),
+        out_specs=vmem_specs(2),
+        scratch_shapes=[
+            pltpu.VMEM((9 * filters, cells), jnp.bfloat16),
+            pltpu.VMEM((6 * chans, cells), jnp.bfloat16),
+        ],
+        compiler_params=pltpu.CompilerParams(vmem_limit_bytes=VMEM_LIMIT),
+        cost_estimate=pl.CostEstimate(
+            flops=2 * 27 * filters * 2 * chans * cells, bytes_accessed=4 << 20, transcendentals=0
+        ),
+        name="kernel_grad",
+    )(place, own, other, grad, grad_low, grad_high)
+
+
+def output_kernel(place, own, other, far_own, far_other, rims, taps, out_ref, weights, stack, acc):
+    depth, height, chans, width = own.shape
+    filters, total = taps.shape[1], taps.shape[2]
+    cells = height * width
+    for tap in range(27):
+        a, b, c = tap // 9, tap // 3 % 3, tap % 3
+        weights[(3 * a + b) * filters : (3 * a + b + 1) * filters, c * total : (c + 1) * total] = taps[tap]
+    core, row_of = place[0], place[1]
+    parts = (
+        (own, 2 * row_of + core),
+        (other, 2 * row_of + 1 - core),
+        (far_own, 2 * (1 - row_of) + core),
+        (far_other, 2 * (1 - row_of) + 1 - core),
+    )
+    acc[...] = jnp.zeros_like(acc)
+    for plane in range(depth + 2):
+        inner = 0 < plane < depth + 1
+        for row in range(height):
+            lanes = slice(row * width, (row + 1) * width)
+            if inner:
+                for source, at in parts:
+                    block = source[plane - 1, row]
+                    for c in range(3):
+                        start = pl.multiple_of(c * total + at * chans, chans)
+                        stack[pl.ds(start, chans), lanes] = shifted(block, c - 1, width)
+            else:
+                block = rims[min(plane, 1), row]
+                for c in range(3):
+                    stack[c * total : (c + 1) * total, lanes] = shifted(block, c - 1, width)
+        steps = [a for a in range(3) if 0 <= plane - a < depth]
+        low, high = steps[0], steps[-1] + 1
+        for row in range(0, height, 2):
+            part = jnp.dot(
+                weights[low * 3 * filters : high * 3 * filters, :],
+                stack[:, row * width : (row + 2) * width],
+                preferred_element_type=jnp.float32,
+            )
+            for a in steps:
+                for b in range(3):
+                    block = part[((a - low) * 3 + b) * filters : ((a - low) * 3 + b + 1) * filters]
+                    for k in range(2):
+                        at = row + k - b + 1
+                        if 0 <= at < height:
+                            acc[plane - a, at] += block[:, k * width : (k + 1) * width]
+    out_ref[...] = acc[...].astype(out_ref.dtype)
+
+
+def output_part(place, own, other, far_own, far_other, rims, taps):
+    depth, height, chans, width = own.shape
+    filters, total = taps.shape[1], taps.shape[2]
+    return pl.pallas_call(
+        output_kernel,
+        out_shape=jax.ShapeDtypeStruct((depth, height, filters, width), jnp.bfloat16),
+        in_specs=[pl.BlockSpec(memory_space=pltpu.SMEM)] + vmem_specs(6),
+        out_specs=pl.BlockSpec(memory_space=pltpu.VMEM),
+        scratch_shapes=[
+            pltpu.VMEM((9 * filters, 3 * total), jnp.bfloat16),
+            pltpu.VMEM((3 * total, height * width), jnp.bfloat16),
+            pltpu.VMEM((depth, height, filters, width), jnp.float32),
+        ],
+        compiler_params=pltpu.CompilerParams(vmem_limit_bytes=VMEM_LIMIT),
+        cost_estimate=pl.CostEstimate(
+            flops=2 * 27 * filters * total * depth * height * width, bytes_accessed=4 << 20, transcendentals=0
+        ),
+        name="output_map",
+    )(place, own, other, far_own, far_other, rims, taps)
+
+
+def input_grad_kernel(grad, grad_low, grad_high, taps, out_ref, weights, stack):
+    depth, height, filters, width = grad.shape
+    total = taps.shape[2]
+    span = 3 * filters
+    weights[...] = jnp.transpose(taps[...].reshape(27 * filters, total))
+    zero = jnp.zeros((span, width), stack.dtype)
+    for plane in range(depth + 2):
+        stack[plane, 0] = zero
+        stack[plane, height + 1] = zero
+        for row in range(height):
+            if plane == 0:
+                block = grad_low[row]
+            elif plane == depth + 1:
+                block = grad_high[row]
+            else:
+                block = grad[plane - 1, row]
+            for c in range(3):
+                stack[plane, row + 1, c * filters : (c + 1) * filters] = shifted(block, 1 - c, width)
+    chans = out_ref.shape[4]
+    for plane in range(depth):
+        for row in range(0, height, 2):
+            halves = []
+            for k in range(2):
+                pieces = [stack[plane - a + 2, row + k - b + 2] for a in range(3) for b in range(3)]
+                halves.append(jnp.concatenate(pieces, axis=0))
+            part = jnp.dot(weights[...], jnp.concatenate(halves, axis=1), preferred_element_type=jnp.float32)
+            for k in range(2):
+                for block in range(total // chans):
+                    out_ref[block // 2, block % 2, plane, row + k] = part[
+                        block * chans : (block + 1) * chans, k * width : (k + 1) * width
+                    ]
+
+
+def input_grad_part(grad, grad_low, grad_high, taps, chans):
+    depth, height, filters, width = grad.shape
+    total = taps.shape[2]
+    return pl.pallas_call(
+        input_grad_kernel,
+        out_shape=jax.ShapeDtypeStruct((2, 2, depth, height, chans, width), jnp.float32),
+        in_specs=vmem_specs(4),
+        out_specs=pl.BlockSpec(memory_space=pltpu.VMEM),
+        scratch_shapes=[
+            pltpu.VMEM((total, 27 * filters), jnp.bfloat16),
+            pltpu.VMEM((depth + 2, height + 2, 3 * filters, width), jnp.bfloat16),
+        ],
+        compiler_params=pltpu.CompilerParams(vmem_limit_bytes=VMEM_LIMIT),
+        cost_estimate=pl.CostEstimate(
+            flops=2 * 27 * filters * total * depth * height * width, bytes_accessed=4 << 20, transcendentals=0
+        ),
+        name="input_grad",
+    )(grad, grad_low, grad_high, taps)
+
+
+def swap(value, axis, bit):
+    count = lax.axis_size(axis)
+    return lax.ppermute(value, axis, [(i, i ^ (1 << bit)) for i in range(count)])
+
+
+def message(values, exponent):
+    coded = (values * jnp.exp2(14.0 - exponent)).astype(jnp.float16)
+    return jnp.concatenate([coded, exponent.astype(jnp.float16)[None]], axis=0)
+
+
+def opened(received):
+    exponent = received[-1].astype(jnp.float32)
+    return received[:-1].astype(jnp.float32) * jnp.exp2(exponent - 14.0), exponent
+
+
+def shard_places(bits):
+    edges = len(bits)
+    return tuple(
+        sum((shard >> bit & 1) << (edges - 1 - step) for step, bit in enumerate(bits))
+        for shard in range(1 << edges)
+    )
+
+
+def reduced(values, exponent, bits):
+    here = lax.axis_index("space")
+    for bit in bits:
+        mine = (here >> bit) & 1
+        halves = values.reshape((2, values.shape[0] // 2) + values.shape[1:])
+        away = lax.dynamic_index_in_dim(halves, 1 - mine, 0, keepdims=False)
+        kept = lax.dynamic_index_in_dim(halves, mine, 0, keepdims=False)
+        received, bound = opened(swap(message(away, exponent), "space", bit))
+        values = kept + received
+        exponent = jnp.maximum(exponent, bound) + 1.0
+    return message(values, exponent)
+
+
+def gathered(coded, bits):
+    flips = [0]
+    for bit in reversed(bits[1:]):
+        coded = jnp.concatenate([coded, swap(coded, "space", bit)], axis=0)
+        flips = flips + [flip ^ (1 << bit) for flip in flips]
+    others = [flip ^ (1 << bits[0]) for flip in flips]
+    return [(coded, flips), (swap(coded, "space", bits[0]), others)]
+
+
+def decoded(coded, count):
+    parts = coded.reshape((count, coded.shape[0] // count) + coded.shape[1:]).astype(jnp.float32)
+    return parts[:, :-1] * jnp.exp2(parts[:, -1:] - 14.0)
+
+
+def assemble_kernel(flips, place, *refs):
+    parts, out_ref = refs[:-1], refs[-1]
+    for index, (part, part_flips) in enumerate(zip(parts, flips)):
+        rows, lanes = part.shape[2:]
+        side = place[1] if index < len(parts) // 2 else 1 - place[1]
+        for at, flip in enumerate(part_flips):
+            start = pl.multiple_of((place[2] ^ flip) * rows, rows)
+            for half in range(2):
+
+                @pl.when(side == half)
+                def _():
+                    out_ref[:, pl.ds(start, rows), half * lanes : (half + 1) * lanes] = part[at]
+
+
+def assembled(place, near, far, filters):
+    parts = [decoded(coded, len(flips)) for coded, flips in near + far]
+    flips = [flips for _, flips in near + far]
+    lanes = parts[0].shape[-1]
+    return pl.pallas_call(
+        functools.partial(assemble_kernel, flips),
+        out_shape=jax.ShapeDtypeStruct((27, filters, 2 * lanes), jnp.float32),
+        in_specs=[pl.BlockSpec(memory_space=pltpu.SMEM)] + vmem_specs(len(parts)),
+        out_specs=pl.BlockSpec(memory_space=pltpu.VMEM),
+        compiler_params=pltpu.CompilerParams(vmem_limit_bytes=VMEM_LIMIT),
+        name="assemble",
+    )(place, *parts)
+
+
+def cube_on_device(volume, kernel, cotangent):
+    depth, chans, height, width = volume.shape
+    filters = cotangent.shape[1]
+    count = lax.axis_size("space")
+    scale = 1.0 / math.sqrt(depth * count * height * width)
+    here = lax.axis_index("chan")
+    place = jnp.stack([here & 1, here >> 1, lax.axis_index("space")]).astype(jnp.int32)
+    edges = count.bit_length() - 1
+    near_bits = tuple(range(edges))
+    far_bits = (1, 0) + tuple(range(2, edges))
+    forward = [(i, i + 1) for i in range(count - 1)]
+    backward = [(i + 1, i) for i in range(count - 1)]
+
+    own = jnp.transpose(volume, (0, 2, 1, 3))
+    far_own = swap(own, "chan", 1)
+    other = swap(own, "chan", 0)
+    grad = jnp.transpose(cotangent, (0, 2, 1, 3))
+    low = lax.ppermute(jnp.stack([grad[-1], own[-1]]), "space", forward)
+    high = lax.ppermute(jnp.stack([grad[0], own[0]]), "space", backward)
+    grad_low, grad_high = low[0], high[0]
+
+    near, near_bound = kernel_grad_part(
+        place, own, other, grad, grad_low, grad_high, scale, shard_places(near_bits)
+    )
+    far_other = swap(far_own, "chan", 0)
+    far, far_bound = kernel_grad_part(
+        place, far_own, far_other, grad, grad_low, grad_high, scale, shard_places(far_bits)
+    )
+
+    rims = jnp.stack([low[1], high[1]])
+    rims = pair(rims, swap(rims, "chan", 0), place[0])
+    rims = pair(rims, swap(rims, "chan", 1), place[1])
+
+    terms = input_grad_part(grad, grad_low, grad_high, kernel, chans)
+    kept = lax.dynamic_index_in_dim(terms, place[0], 1, keepdims=False)
+    away = lax.dynamic_index_in_dim(terms, 1 - place[0], 1, keepdims=False)
+    terms = kept + swap(away, "chan", 0)
+    kept = lax.dynamic_index_in_dim(terms, place[1], 0, keepdims=False)
+    away = lax.dynamic_index_in_dim(terms, 1 - place[1], 0, keepdims=False)
+    terms = kept + swap(away, "chan", 1)
+    input_grad = jnp.transpose(terms.astype(jnp.bfloat16), (0, 2, 1, 3))
+
+    output = output_part(place, own, other, far_own, far_other, rims, kernel)
+    output_map = jnp.transpose(output, (0, 2, 1, 3))
+
+    near = gathered(reduced(near, near_bound, near_bits), near_bits)
+    far = gathered(reduced(far, far_bound, far_bits), far_bits)
+    kernel_grad = assembled(place, near, far, filters)
+    return output_map, input_grad, kernel_grad
+
+
+def pair(own, other, at):
+    return jnp.where(at == 0, jnp.concatenate([own, other], 2), jnp.concatenate([other, own], 2))
 
 
 def with_halo(block, sides, width):
@@ -36,7 +381,7 @@
     return jnp.concatenate(windows, axis=1)
 
 
-def on_device(volume, kernel, cotangent):
+def plain_on_device(volume, kernel, cotangent):
     depth, chans_local, height, width = volume.shape
     filters_local = cotangent.shape[1]
     cells = height * width
@@ -80,6 +425,15 @@
     input_grad = total.astype(jnp.bfloat16).reshape(depth, chans_local, height, width)
     return (output_map, input_grad, kernel_grad)
 
+def on_device(volume, kernel, cotangent):
+    count, ways = lax.axis_size("space"), lax.axis_size("chan")
+    chans, width = volume.shape[1], volume.shape[3]
+    filters = cotangent.shape[1]
+    cube = ways == 4 and count >= 4 and count & (count - 1) == 0
+    if cube and width == 128 and (2 * chans) % 128 == 0 and filters % (8 * count) == 0:
+        return cube_on_device(volume, kernel, cotangent)
+    return plain_on_device(volume, kernel, cotangent)
+
 
 def solution(mesh):
     return jax.shard_map(

time: 231 us -> 82.6 us (0.36); the launches traced: 227 us -> 82.4 us
  waiting for transfers between devices: 99.1 us -> 32.6 us
  other arithmetic: 37.6 us -> 3.21 us
  matrix products: 32.3 us -> 0 us
  local copies, waits for them, and re-layouts: 27 us -> 3.44 us
  Pallas kernels: 0 us -> 13.6 us
  between operations: 14.4 us -> 1.12 us
  starting transfers between devices: 16.1 us -> 28.5 us
    psum x1 -> x0, waiting for transfers between devices: 78.6 us -> none  [on_device(): kernel_grad = lax.psum(kernel_acc, 'space') * scale_factor]
    dot_general x9 -> x0, matrix products: 32.3 us -> none  [the longest x3 17.1 us: on_device(): jnp.einsum('kj,zjp->zkp', weights, window, preferred_element_type=jnp.flo...]
    unnamed x14 -> x0, other arithmetic: 27.3 us -> none
    ppermute x4 -> x21, waiting for transfers between devices: 9.92 us -> 32.6 us  [the longest x19 24.7 us: swap(): return lax.ppermute(value, axis, [(i, i ^ 1 << bit) for i in range(count)])]
    ppermute x4 -> x21, starting transfers between devices: 11.8 us -> 28.5 us  [the longest x19 22.6 us: swap(): return lax.ppermute(value, axis, [(i, i ^ 1 << bit) for i in range(count)])]
    pallas_call x0 -> x5, Pallas kernels: none -> 13.6 us  [the longest x2 5.21 us: kernel_grad_part(): pl.pallas_call(functools.partial(kernel_grad_kernel, scale, order), out_s...]
    all_to_all x1 -> x0, waiting for transfers between devices: 10.6 us -> none  [on_device(): lax.all_to_all(kernel, 'chan', split_axis=2, concat_axis=1, tiled=True)]
    unnamed x34 -> x5, local copies, waits for them, and re-layouts: 13 us -> 2.87 us
  transfers between devices with their start and end apart: 8 -> 21, of which waited for: 6 -> 11; matrix products, arithmetic and copies ran while one was open for 26% -> 4% of each run, Pallas kernels for 0% -> 16%
where the time goes in v1:
time: 82.6 us; the launch traced here: 82.4 us
  waiting for transfers between devices  32.6 us (39%)
  starting transfers between devices  28.5 us (35%)
  Pallas kernels  13.6 us (16%)
  local copies, waits for them, and re-layouts  3.44 us (4%)
  other arithmetic  3.21 us (4%)
  between operations  1.12 us (1%)
    ppermute x19, waiting for transfers between devices, swap(): return lax.ppermute(value, axis, [(i, i ^ 1 << bit) for i in range(count)])  24.7 us
    ppermute x19, starting transfers between devices, swap(): return lax.ppermute(value, axis, [(i, i ^ 1 << bit) for i in range(count)])  22.6 us
    ppermute x1, waiting for transfers between devices, cube_on_device(): low = lax.ppermute(jnp.stack([grad[-1], own[-1]]), 'space', forward)  5.76 us
    pallas_call x2, Pallas kernels, kernel_grad_part(): pl.pallas_call(functools.partial(kernel_grad_kernel, scale, order), out_s...  5.21 us
    ppermute x1, starting transfers between devices, cube_on_device(): low = lax.ppermute(jnp.stack([grad[-1], own[-1]]), 'space', forward)  4.56 us
    pallas_call x1, Pallas kernels, output_part(): pl.pallas_call(output_kernel, out_shape=jax.ShapeDtypeStruct((depth, heig...  4.03 us
    unnamed x5, local copies, waits for them, and re-layouts  2.87 us
    pallas_call x1, Pallas kernels, input_grad_part(): pl.pallas_call(input_grad_kernel, out_shape=jax.ShapeDtypeStruct((2, 2, d...  2.3 us
  transfers between devices with their start and end apart: 21, of which 11 were waited for; matrix products, arithmetic and copies ran while one was open for 4% of the time, Pallas kernels for 16%

profile of v1, /device:TPU:0, one launch (start us, length us, event | category | flops | bytes accessed | tf_op | source)
XLA Modules:
  0.0 82.4 jit_solution(4522758971537531588)
XLA Ops:
  4.5 2.6 %collective-permute-start.1 = (bf16[2,8,64,128]{3,2,1,0:T(8,128)(2,1)S(1)}, bf16[2,8,64,128]{3,2,1,0:T(8,128)(2,1)S(1)}, u32[]{:S(2)}, u32[]{:S(2)}) collective-permute-start(bf16[2,8,64,128]{3,2,1,0:T(8,128)(2,1)S(1)} %bitcast.189), channel_id=1, source_target_pairs={{0,2},{1,3},{2,0},{3,1},{4,6},{5,7},{6,4},{7,5},{8,10},{9,11},{10,... | collective-permute-start | bytes 786440 | tf_op jit(solution)/shard_map/ppermute | solution.py:223
  7.2 4.6 %collective-permute-start.3 = (bf16[2,8,64,128]{3,2,1,0:T(8,128)(2,1)S(1)}, bf16[2,8,64,128]{3,2,1,0:T(8,128)(2,1)S(1)}, u32[]{:S(2)}, u32[]{:S(2)}) collective-permute-start(bf16[2,8,64,128]{3,2,1,0:T(8,128)(2,1)S(1)} %pad_maximum_fusion), channel_id=1, source_target_pairs={{0,4},{4,8},{8,12},{12,16},{16,20},{20,24},{24,28},{1,5},{5,9},{9,... | collective-permute-start | bytes 786440 | tf_op jit(solution)/shard_map/ppermute | solution.py:316
  11.8 2.0 %collective-permute-done.4 = bf16[2,8,64,128]{3,2,1,0:T(8,128)(2,1)S(1)} collective-permute-done((bf16[2,8,64,128]{3,2,1,0:T(8,128)(2,1)S(1)}, bf16[2,8,64,128]{3,2,1,0:T(8,128)(2,1)S(1)}, u32[]{:S(2)}, u32[]{:S(2)}) %collective-permute-start.4) | collective-permute-done | bytes 262176 | tf_op jit(solution)/shard_map/ppermute | solution.py:317
  13.9 5.8 %collective-permute-done.3 = bf16[2,8,64,128]{3,2,1,0:T(8,128)(2,1)S(1)} collective-permute-done((bf16[2,8,64,128]{3,2,1,0:T(8,128)(2,1)S(1)}, bf16[2,8,64,128]{3,2,1,0:T(8,128)(2,1)S(1)}, u32[]{:S(2)}, u32[]{:S(2)}) %collective-permute-start.3) | collective-permute-done | bytes 262176 | tf_op jit(solution)/shard_map/ppermute | solution.py:316
  19.8 2.6 %kernel_grad.2 = (f32[216,8,128]{2,1,0:T(8,128)S(1)}, f32[8,128]{1,0:T(8,128)S(1)}) custom-call(s32[3]{0:T(128)S(1)} %pad_add_fusion.place, bf16[2,8,64,128]{3,2,1,0:T(8,128)(2,1)S(1)} %bitcast.190, bf16[2,8,64,128]{3,2,1,0:T(8,128)(2,1)S(1)} %collective-permute-done.other, bf16[2,8,64,128]{3,2,1,0:T(8,128)(2,1)S(1)} %bitcast.193, ...), custom_call_target="tpu_custom_call" | custom-call | flops 905969664 | bytes 4194304 | tf_op jit(solution)/shard_map/kernel_grad/pallas_call | solution.py:80
  22.6 2.5 %collective-permute-start.9 = (f16[109,8,128]{2,1,0:T(8,128)(2,1)S(1)}, f16[109,8,128]{2,1,0:T(8,128)(2,1)S(1)}, u32[]{:S(2)}, u32[]{:S(2)}) collective-permute-start(f16[109,8,128]{2,1,0:T(8,128)(2,1)S(1)} %pad_maximum_fusion.5), channel_id=1, source_target_pairs={{0,4},{4,0},{8,12},{12,8},{16,20},{20,16},{24,28},{28,24},{1,5},{5... | collective-permute-start | bytes 669704 | tf_op jit(solution)/shard_map/ppermute | solution.py:223
  25.1 2.3 %input_grad.1 = f32[2,2,2,8,64,128]{5,4,3,2,1,0:T(8,128)S(1)} custom-call(bf16[2,8,64,128]{3,2,1,0:T(8,128)(2,1)S(1)} %bitcast.194, bf16[8,64,128]{2,1,0:T(8,128)(2,1)S(1)} %get-tuple-element.22.grad_low, bf16[8,64,128]{2,1,0:T(8,128)(2,1)S(1)} %get-tuple-element.20.grad_high, bf16[27,64,256]{2,1,0:T(8,128)(2,1)S(1)} %copy-done), custom_call_target="tpu_custom_call" | custom-call | flops 1811939328 | bytes 4194304 | tf_op jit(solution)/shard_map/input_grad/pallas_call | solution.py:204
  28.1 3.1 %collective-permute-done.9 = f16[109,8,128]{2,1,0:T(8,128)(2,1)S(1)} collective-permute-done((f16[109,8,128]{2,1,0:T(8,128)(2,1)S(1)}, f16[109,8,128]{2,1,0:T(8,128)(2,1)S(1)}, u32[]{:S(2)}, u32[]{:S(2)}) %collective-permute-start.9) | collective-permute-done | bytes 223264 | tf_op jit(solution)/shard_map/ppermute | solution.py:223
  31.4 1.6 %collective-permute-start.10 = (f16[55,8,128]{2,1,0:T(8,128)(2,1)S(1)}, f16[55,8,128]{2,1,0:T(8,128)(2,1)S(1)}, u32[]{:S(2)}, u32[]{:S(2)}) collective-permute-start(f16[55,8,128]{2,1,0:T(8,128)(2,1)S(1)} %pad_maximum_fusion.9), channel_id=1, source_target_pairs={{0,8},{4,12},{8,0},{12,4},{16,24},{20,28},{24,16},{28,20},{1,9},{5... | collective-permute-start | bytes 337928 | tf_op jit(solution)/shard_map/ppermute | solution.py:223
  33.2 1.6 %collective-permute-start.6 = (bf16[2,8,128,128]{3,2,1,0:T(8,128)(2,1)S(1)}, bf16[2,8,128,128]{3,2,1,0:T(8,128)(2,1)S(1)}, u32[]{:S(2)}, u32[]{:S(2)}) collective-permute-start(bf16[2,8,128,128]{3,2,1,0:T(8,128)(2,1)S(1)} %maximum_select_fusion.1), channel_id=1, source_target_pairs={{0,2},{1,3},{2,0},{3,1},{4,6},{5,7},{6,4},{7,5},{8,10},{9,11},{10,... | collective-permute-start | bytes 1572872 | tf_op jit(solution)/shard_map/ppermute | solution.py:223
  34.8 2.6 %kernel_grad.3 = (f32[216,8,128]{2,1,0:T(8,128)S(1)}, f32[8,128]{1,0:T(8,128)S(1)}) custom-call(s32[3]{0:T(128)S(1)} %pad_add_fusion.place, bf16[2,8,64,128]{3,2,1,0:T(8,128)(2,1)S(1)} %collective-permute-done.1.far_own.own, bf16[2,8,64,128]{3,2,1,0:T(8,128)(2,1)S(1)} %collective-permute-done.2.far_other.other, bf16[2,8,64,128]{3,2,1,0:T(8,128)(2,1)S(1)} %bitcast.195, ...), custom_call_target="tpu_custom_call" | custom-call | flops 905969664 | bytes 4194304 | tf_op jit(solution)/shard_map/kernel_grad/pallas_call | solution.py:80
  37.6 2.0 %collective-permute-start.11 = (f16[28,8,128]{2,1,0:T(8,128)(2,1)S(1)}, f16[28,8,128]{2,1,0:T(8,128)(2,1)S(1)}, u32[]{:S(2)}, u32[]{:S(2)}) collective-permute-start(f16[28,8,128]{2,1,0:T(8,128)(2,1)S(1)} %pad_maximum_fusion.11), channel_id=1, source_target_pairs={{0,16},{4,20},{8,24},{12,28},{16,0},{20,4},{24,8},{28,12},{1,17},{... | collective-permute-start | bytes 172040 | tf_op jit(solution)/shard_map/ppermute | solution.py:223
  40.9 2.6 %collective-permute-done.11 = f16[28,8,128]{2,1,0:T(8,128)(2,1)S(1)} collective-permute-done((f16[28,8,128]{2,1,0:T(8,128)(2,1)S(1)}, f16[28,8,128]{2,1,0:T(8,128)(2,1)S(1)}, u32[]{:S(2)}, u32[]{:S(2)}) %collective-permute-start.11) | collective-permute-done | bytes 57376 | tf_op jit(solution)/shard_map/ppermute | solution.py:223
  43.5 1.9 %collective-permute-start.12 = (f16[28,8,128]{2,1,0:T(8,128)(2,1)S(1)}, f16[28,8,128]{2,1,0:T(8,128)(2,1)S(1)}, u32[]{:S(2)}, u32[]{:S(2)}) collective-permute-start(f16[28,8,128]{2,1,0:T(8,128)(2,1)S(1)} %pad_maximum_fusion.12), channel_id=1, source_target_pairs={{0,16},{4,20},{8,24},{12,28},{16,0},{20,4},{24,8},{28,12},{1,17},{... | collective-permute-start | bytes 172040 | tf_op jit(solution)/shard_map/ppermute | solution.py:223
  45.5 2.2 %collective-permute-done.15 = f16[109,8,128]{2,1,0:T(8,128)(2,1)S(1)} collective-permute-done((f16[109,8,128]{2,1,0:T(8,128)(2,1)S(1)}, f16[109,8,128]{2,1,0:T(8,128)(2,1)S(1)}, u32[]{:S(2)}, u32[]{:S(2)}) %collective-permute-start.15) | collective-permute-done | bytes 223264 | tf_op jit(solution)/shard_map/ppermute | solution.py:223
  47.8 1.4 %collective-permute-start.16 = (f16[55,8,128]{2,1,0:T(8,128)(2,1)S(1)}, f16[55,8,128]{2,1,0:T(8,128)(2,1)S(1)}, u32[]{:S(2)}, u32[]{:S(2)}) collective-permute-start(f16[55,8,128]{2,1,0:T(8,128)(2,1)S(1)} %pad_maximum_fusion.10), channel_id=1, source_target_pairs={{0,4},{4,0},{8,12},{12,8},{16,20},{20,16},{24,28},{28,24},{1,5},{5... | collective-permute-start | bytes 337928 | tf_op jit(solution)/shard_map/ppermute | solution.py:223
  50.4 2.2 %collective-permute-done.16 = f16[55,8,128]{2,1,0:T(8,128)(2,1)S(1)} collective-permute-done((f16[55,8,128]{2,1,0:T(8,128)(2,1)S(1)}, f16[55,8,128]{2,1,0:T(8,128)(2,1)S(1)}, u32[]{:S(2)}, u32[]{:S(2)}) %collective-permute-start.16) | collective-permute-done | bytes 112672 | tf_op jit(solution)/shard_map/ppermute | solution.py:223
  54.2 2.1 %collective-permute-start.14 = (f16[112,8,128]{2,1,0:T(8,128)(2,1)S(1)}, f16[112,8,128]{2,1,0:T(8,128)(2,1)S(1)}, u32[]{:S(2)}, u32[]{:S(2)}) collective-permute-start(f16[112,8,128]{2,1,0:T(8,128)(2,1)S(1)} %pad_maximum_fusion.3), channel_id=1, source_target_pairs={{0,4},{4,0},{8,12},{12,8},{16,20},{20,16},{24,28},{28,24},{1,5},{5... | collective-permute-start | bytes 688136 | tf_op jit(solution)/shard_map/ppermute | solution.py:223
  56.3 3.0 %collective-permute-done.17 = f16[28,8,128]{2,1,0:T(8,128)(2,1)S(1)} collective-permute-done((f16[28,8,128]{2,1,0:T(8,128)(2,1)S(1)}, f16[28,8,128]{2,1,0:T(8,128)(2,1)S(1)}, u32[]{:S(2)}, u32[]{:S(2)}) %collective-permute-start.17) | collective-permute-done | bytes 57376 | tf_op jit(solution)/shard_map/ppermute | solution.py:223
  59.5 5.0 %collective-permute-done.18 = f16[28,8,128]{2,1,0:T(8,128)(2,1)S(1)} collective-permute-done((f16[28,8,128]{2,1,0:T(8,128)(2,1)S(1)}, f16[28,8,128]{2,1,0:T(8,128)(2,1)S(1)}, u32[]{:S(2)}, u32[]{:S(2)}) %collective-permute-start.18) | collective-permute-done | bytes 57376 | tf_op jit(solution)/shard_map/ppermute | solution.py:223
  65.0 4.0 %output_map.1 = bf16[2,8,64,128]{3,2,1,0:T(8,128)(2,1)S(1)} custom-call(s32[3]{0:T(128)S(1)} %pad_add_fusion.place, bf16[2,8,64,128]{3,2,1,0:T(8,128)(2,1)S(1)} %bitcast.191, bf16[2,8,64,128]{3,2,1,0:T(8,128)(2,1)S(1)} %collective-permute-done.other, bf16[2,8,64,128]{3,2,1,0:T(8,128)(2,1)S(1)} %collective-permute-done.1.far_own.own, ...), custom_call_target="tpu_custom_call" | custom-call | flops 1811939328 | bytes 4194304 | tf_op jit(solution)/shard_map/output_map/pallas_call | solution.py:150
  73.1 3.1 %collective-permute-done.20 = f16[112,8,128]{2,1,0:T(8,128)(2,1)S(1)} collective-permute-done((f16[112,8,128]{2,1,0:T(8,128)(2,1)S(1)}, f16[112,8,128]{2,1,0:T(8,128)(2,1)S(1)}, u32[]{:S(2)}, u32[]{:S(2)}) %collective-permute-start.20) | collective-permute-done | bytes 229408 | tf_op jit(solution)/shard_map/ppermute | solution.py:223
  76.3 2.0 %assemble.1 = f32[27,64,256]{2,1,0:T(8,128)} custom-call(s32[3]{0:T(128)S(1)} %pad_add_fusion.place, f32[4,27,8,128]{3,2,1,0:T(8,128)S(1)} %get-tuple-element.43.refs_0_, f32[4,27,8,128]{3,2,1,0:T(8,128)S(1)} %get-tuple-element.42.refs_1_, f32[4,27,8,128]{3,2,1,0:T(8,128)S(1)} %get-tuple-element.41.refs_2_, f32[4,27,8,128]{3,2,1,0:T(8,128)S(1)} %get-tuple-element.40.refs_3_), custom_call_target="tpu_custom_call" | custom-call | tf_op jit(solution)/shard_map/assemble/pallas_call | solution.py:289
  78.3 3.0 %collective-permute-done.8 = f32[2,8,64,128]{3,1,2,0:T(8,128)S(1)} collective-permute-done((f32[2,8,64,128]{3,1,2,0:T(8,128)S(1)}, f32[2,8,64,128]{3,1,2,0:T(8,128)S(1)}, u32[]{:S(2)}, u32[]{:S(2)}) %collective-permute-start.8) | collective-permute-done | bytes 524320 | tf_op jit(solution)/shard_map/ppermute | solution.py:223
  (93 shorter events, 15.3 us)
Async XLA Ops:
  2.7 11.1 %collective-permute-start.4 = (bf16[2,8,64,128]{3,2,1,0:T(8,128)(2,1)S(1)}, bf16[2,8,64,128]{3,2,1,0:T(8,128)(2,1)S(1)}, u32[]{:S(2)}, u32[]{:S(2)}) collective-permute-start(bf16[2,8,64,128]{3,2,1,0:T(8,128)(2,1)S(1)} %pad_maximum_fusion.1), channel_id=1, source_target_pairs={{4,0},{8,4},{12,8},{16,12},{20,16},{24,20},{28,24},{5,1},{9,5},{13... | collective-permute-start | bytes 786440 | tf_op jit(solution)/shard_map/ppermute | solution.py:317
  4.0 15.8 %collective-permute-start = (bf16[2,8,64,128]{3,2,1,0:T(8,128)(2,1)S(1)}, bf16[2,8,64,128]{3,2,1,0:T(8,128)(2,1)S(1)}, u32[]{:S(2)}, u32[]{:S(2)}) collective-permute-start(bf16[2,8,64,128]{3,2,1,0:T(8,128)(2,1)S(1)} %bitcast.188), channel_id=1, source_target_pairs={{0,1},{1,0},{2,3},{3,2},{4,5},{5,4},{6,7},{7,6},{8,9},{9,8},{10,11... | collective-permute-start | bytes 786440 | tf_op jit(solution)/shard_map/ppermute | solution.py:223
  4.5 23.2 %collective-permute-start.1 = (bf16[2,8,64,128]{3,2,1,0:T(8,128)(2,1)S(1)}, bf16[2,8,64,128]{3,2,1,0:T(8,128)(2,1)S(1)}, u32[]{:S(2)}, u32[]{:S(2)}) collective-permute-start(bf16[2,8,64,128]{3,2,1,0:T(8,128)(2,1)S(1)} %bitcast.189), channel_id=1, source_target_pairs={{0,2},{1,3},{2,0},{3,1},{4,6},{5,7},{6,4},{7,5},{8,10},{9,11},{10,... | collective-permute-start | bytes 786440 | tf_op jit(solution)/shard_map/ppermute | solution.py:223
  7.2 12.5 %collective-permute-start.3 = (bf16[2,8,64,128]{3,2,1,0:T(8,128)(2,1)S(1)}, bf16[2,8,64,128]{3,2,1,0:T(8,128)(2,1)S(1)}, u32[]{:S(2)}, u32[]{:S(2)}) collective-permute-start(bf16[2,8,64,128]{3,2,1,0:T(8,128)(2,1)S(1)} %pad_maximum_fusion), channel_id=1, source_target_pairs={{0,4},{4,8},{8,12},{12,16},{16,20},{20,24},{24,28},{1,5},{5,9},{9,... | collective-permute-start | bytes 786440 | tf_op jit(solution)/shard_map/ppermute | solution.py:316
  19.7 13.3 %collective-permute-start.5 = (bf16[2,8,64,128]{3,2,1,0:T(8,128)(2,1)S(1)}, bf16[2,8,64,128]{3,2,1,0:T(8,128)(2,1)S(1)}, u32[]{:S(2)}, u32[]{:S(2)}) collective-permute-start(bf16[2,8,64,128]{3,2,1,0:T(8,128)(2,1)S(1)} %pad_maximum_fusion.2), channel_id=1, source_target_pairs={{0,1},{1,0},{2,3},{3,2},{4,5},{5,4},{6,7},{7,6},{8,9},{9,8},{10,11... | collective-permute-start | bytes 786440 | tf_op jit(solution)/shard_map/ppermute | solution.py:223
  19.8 5.3 %copy-start = (bf16[27,64,256]{2,1,0:T(8,128)(2,1)S(1)}, bf16[27,64,256]{2,1,0:T(8,128)(2,1)}, u32[]{:S(2)}) copy-start(bf16[27,64,256]{2,1,0:T(8,128)(2,1)} %taps.3) | copy-start | bytes 2654212
  22.6 8.6 %collective-permute-start.9 = (f16[109,8,128]{2,1,0:T(8,128)(2,1)S(1)}, f16[109,8,128]{2,1,0:T(8,128)(2,1)S(1)}, u32[]{:S(2)}, u32[]{:S(2)}) collective-permute-start(f16[109,8,128]{2,1,0:T(8,128)(2,1)S(1)} %pad_maximum_fusion.5), channel_id=1, source_target_pairs={{0,4},{4,0},{8,12},{12,8},{16,20},{20,16},{24,28},{28,24},{1,5},{5... | collective-permute-start | bytes 669704 | tf_op jit(solution)/shard_map/ppermute | solution.py:223
  27.5 44.0 %collective-permute-start.7 = (f32[2,2,8,64,128]{4,3,2,1,0:T(8,128)S(1)}, f32[2,2,8,64,128]{4,3,2,1,0:T(8,128)S(1)}, u32[]{:S(2)}, u32[]{:S(2)}) collective-permute-start(f32[2,2,8,64,128]{4,3,2,1,0:T(8,128)S(1)} %dynamic-slice_bitcast_fusion), channel_id=1, source_target_pairs={{0,1},{1,0},{2,3},{3,2},{4,5},{5,4},{6,7},{7,6},{8,9},{9,8},{10,11... | collective-permute-start | bytes 3145736 | tf_op jit(solution)/shard_map/ppermute | solution.py:223
  27.8 7.0 %collective-permute-start.2 = (bf16[2,8,64,128]{3,2,1,0:T(8,128)(2,1)S(1)}, bf16[2,8,64,128]{3,2,1,0:T(8,128)(2,1)S(1)}, u32[]{:S(2)}, u32[]{:S(2)}) collective-permute-start(bf16[2,8,64,128]{3,2,1,0:T(8,128)(2,1)S(1)} %collective-permute-done.1.far_own.own), channel_id=1, source_target_pairs={{0,1},{1,0},{2,3},{3,2},{4,5},{5,4},{6,7},{7,6},{8,9},{9,8},{10,11... | collective-permute-start | bytes 786440 | tf_op jit(solution)/shard_map/ppermute | solution.py:223
  31.4 6.1 %collective-permute-start.10 = (f16[55,8,128]{2,1,0:T(8,128)(2,1)S(1)}, f16[55,8,128]{2,1,0:T(8,128)(2,1)S(1)}, u32[]{:S(2)}, u32[]{:S(2)}) collective-permute-start(f16[55,8,128]{2,1,0:T(8,128)(2,1)S(1)} %pad_maximum_fusion.9), channel_id=1, source_target_pairs={{0,8},{4,12},{8,0},{12,4},{16,24},{20,28},{24,16},{28,20},{1,9},{5... | collective-permute-start | bytes 337928 | tf_op jit(solution)/shard_map/ppermute | solution.py:223
  33.2 31.4 %collective-permute-start.6 = (bf16[2,8,128,128]{3,2,1,0:T(8,128)(2,1)S(1)}, bf16[2,8,128,128]{3,2,1,0:T(8,128)(2,1)S(1)}, u32[]{:S(2)}, u32[]{:S(2)}) collective-permute-start(bf16[2,8,128,128]{3,2,1,0:T(8,128)(2,1)S(1)} %maximum_select_fusion.1), channel_id=1, source_target_pairs={{0,2},{1,3},{2,0},{3,1},{4,6},{5,7},{6,4},{7,5},{8,10},{9,11},{10,... | collective-permute-start | bytes 1572872 | tf_op jit(solution)/shard_map/ppermute | solution.py:223
  37.6 5.8 %collective-permute-start.11 = (f16[28,8,128]{2,1,0:T(8,128)(2,1)S(1)}, f16[28,8,128]{2,1,0:T(8,128)(2,1)S(1)}, u32[]{:S(2)}, u32[]{:S(2)}) collective-permute-start(f16[28,8,128]{2,1,0:T(8,128)(2,1)S(1)} %pad_maximum_fusion.11), channel_id=1, source_target_pairs={{0,16},{4,20},{8,24},{12,28},{16,0},{20,4},{24,8},{28,12},{1,17},{... | collective-permute-start | bytes 172040 | tf_op jit(solution)/shard_map/ppermute | solution.py:223
  39.7 7.9 %collective-permute-start.15 = (f16[109,8,128]{2,1,0:T(8,128)(2,1)S(1)}, f16[109,8,128]{2,1,0:T(8,128)(2,1)S(1)}, u32[]{:S(2)}, u32[]{:S(2)}) collective-permute-start(f16[109,8,128]{2,1,0:T(8,128)(2,1)S(1)} %pad_maximum_fusion.6), channel_id=1, source_target_pairs={{0,8},{4,12},{8,0},{12,4},{16,24},{20,28},{24,16},{28,20},{1,9},{5... | collective-permute-start | bytes 669704 | tf_op jit(solution)/shard_map/ppermute | solution.py:223
  43.5 5.6 %collective-permute-start.12 = (f16[28,8,128]{2,1,0:T(8,128)(2,1)S(1)}, f16[28,8,128]{2,1,0:T(8,128)(2,1)S(1)}, u32[]{:S(2)}, u32[]{:S(2)}) collective-permute-start(f16[28,8,128]{2,1,0:T(8,128)(2,1)S(1)} %pad_maximum_fusion.12), channel_id=1, source_target_pairs={{0,16},{4,20},{8,24},{12,28},{16,0},{20,4},{24,8},{28,12},{1,17},{... | collective-permute-start | bytes 172040 | tf_op jit(solution)/shard_map/ppermute | solution.py:223
  47.8 4.8 %collective-permute-start.16 = (f16[55,8,128]{2,1,0:T(8,128)(2,1)S(1)}, f16[55,8,128]{2,1,0:T(8,128)(2,1)S(1)}, u32[]{:S(2)}, u32[]{:S(2)}) collective-permute-start(f16[55,8,128]{2,1,0:T(8,128)(2,1)S(1)} %pad_maximum_fusion.10), channel_id=1, source_target_pairs={{0,4},{4,0},{8,12},{12,8},{16,20},{20,16},{24,28},{28,24},{1,5},{5... | collective-permute-start | bytes 337928 | tf_op jit(solution)/shard_map/ppermute | solution.py:223
  49.2 4.9 %collective-permute-start.13 = (f16[56,8,128]{2,1,0:T(8,128)(2,1)S(1)}, f16[56,8,128]{2,1,0:T(8,128)(2,1)S(1)}, u32[]{:S(2)}, u32[]{:S(2)}) collective-permute-start(f16[56,8,128]{2,1,0:T(8,128)(2,1)S(1)} %pad_maximum_fusion.7), channel_id=1, source_target_pairs={{0,8},{4,12},{8,0},{12,4},{16,24},{20,28},{24,16},{28,20},{1,9},{5... | collective-permute-start | bytes 344072 | tf_op jit(solution)/shard_map/ppermute | solution.py:223
  52.8 6.5 %collective-permute-start.17 = (f16[28,8,128]{2,1,0:T(8,128)(2,1)S(1)}, f16[28,8,128]{2,1,0:T(8,128)(2,1)S(1)}, u32[]{:S(2)}, u32[]{:S(2)}) collective-permute-start(f16[28,8,128]{2,1,0:T(8,128)(2,1)S(1)} %pad_maximum_fusion.13), channel_id=1, source_target_pairs={{0,16},{4,20},{8,24},{12,28},{16,0},{20,4},{24,8},{28,12},{1,17},{... | collective-permute-start | bytes 172040 | tf_op jit(solution)/shard_map/ppermute | solution.py:223
  54.2 15.7 %collective-permute-start.14 = (f16[112,8,128]{2,1,0:T(8,128)(2,1)S(1)}, f16[112,8,128]{2,1,0:T(8,128)(2,1)S(1)}, u32[]{:S(2)}, u32[]{:S(2)}) collective-permute-start(f16[112,8,128]{2,1,0:T(8,128)(2,1)S(1)} %pad_maximum_fusion.3), channel_id=1, source_target_pairs={{0,4},{4,0},{8,12},{12,8},{16,20},{20,16},{24,28},{28,24},{1,5},{5... | collective-permute-start | bytes 688136 | tf_op jit(solution)/shard_map/ppermute | solution.py:223
  59.4 5.1 %collective-permute-start.18 = (f16[28,8,128]{2,1,0:T(8,128)(2,1)S(1)}, f16[28,8,128]{2,1,0:T(8,128)(2,1)S(1)}, u32[]{:S(2)}, u32[]{:S(2)}) collective-permute-start(f16[28,8,128]{2,1,0:T(8,128)(2,1)S(1)} %pad_maximum_fusion.14), channel_id=1, source_target_pairs={{0,16},{4,20},{8,24},{12,28},{16,0},{20,4},{24,8},{28,12},{1,17},{... | collective-permute-start | bytes 172040 | tf_op jit(solution)/shard_map/ppermute | solution.py:223
  64.6 5.4 %collective-permute-start.19 = (f16[56,8,128]{2,1,0:T(8,128)(2,1)S(1)}, f16[56,8,128]{2,1,0:T(8,128)(2,1)S(1)}, u32[]{:S(2)}, u32[]{:S(2)}) collective-permute-start(f16[56,8,128]{2,1,0:T(8,128)(2,1)S(1)} %pad_maximum_fusion.8), channel_id=1, source_target_pairs={{0,4},{4,0},{8,12},{12,8},{16,20},{20,16},{24,28},{28,24},{1,5},{5... | collective-permute-start | bytes 344072 | tf_op jit(solution)/shard_map/ppermute | solution.py:223
  70.1 6.1 %collective-permute-start.20 = (f16[112,8,128]{2,1,0:T(8,128)(2,1)S(1)}, f16[112,8,128]{2,1,0:T(8,128)(2,1)S(1)}, u32[]{:S(2)}, u32[]{:S(2)}) collective-permute-start(f16[112,8,128]{2,1,0:T(8,128)(2,1)S(1)} %pad_maximum_fusion.4), channel_id=1, source_target_pairs={{0,8},{4,12},{8,0},{12,4},{16,24},{20,28},{24,16},{28,20},{1,9},{5... | collective-permute-start | bytes 688136 | tf_op jit(solution)/shard_map/ppermute | solution.py:223
  72.1 9.2 %collective-permute-start.8 = (f32[2,8,64,128]{3,1,2,0:T(8,128)S(1)}, f32[2,8,64,128]{3,1,2,0:T(8,128)S(1)}, u32[]{:S(2)}, u32[]{:S(2)}) collective-permute-start(f32[2,8,64,128]{3,1,2,0:T(8,128)S(1)} %bitcast.211), channel_id=1, source_target_pairs={{0,2},{1,3},{2,0},{3,1},{4,6},{5,7},{6,4},{7,5},{8,10},{9,11},{10,... | collective-permute-start | bytes 1572872 | tf_op jit(solution)/shard_map/ppermute | solution.py:223

commit v2 on v0

--- a/solution.py
+++ b/solution.py
@@ -1,9 +1,389 @@
+import functools
 import math
 
 import jax
 import jax.numpy as jnp
 from jax import lax
+from jax.experimental import pallas as pl
+from jax.experimental.pallas import tpu as pltpu
 from jax.sharding import PartitionSpec as P
+
+VMEM_LIMIT = 48 * 1024 * 1024
+SMALL_COST = pl.CostEstimate(flops=1, bytes_accessed=1, transcendentals=0)
+
+
+def specs(count):
+    return [pl.BlockSpec(memory_space=pltpu.SMEM)] + [pl.BlockSpec(memory_space=pltpu.VMEM)] * count
+
+
+def shifted(block, step):
+    if step:
+        width = block.shape[1]
+        lane = lax.broadcasted_iota(jnp.int32, block.shape, 1)
+        rolled = pltpu.roll(block.astype(jnp.float32), (-step) % width, 1)
+        block = jnp.where((lane + step >= 0) & (lane + step < width), rolled, 0.0)
+    return block.astype(jnp.bfloat16)
+
+
+def edge_row(odd, beside, across, low, row):
+    if low:
+        return jnp.where(odd == 0, across[row], beside[row])
+    return jnp.where(odd == 0, beside[row], across[row])
+
+
+def kernel_grad_kernel(
+    scale, order, place, own, other, grad, beside, across, out_ref, left, right
+):
+    depth, height, chans, width = own.shape
+    filters = grad.shape[2]
+    cells = height * width
+    span = 2 * chans
+    odd = place[2] & 1
+
+    for source, at in ((own, place[0]), (other, 1 - place[0])):
+        for plane in range(depth):
+            for row in range(height):
+                lanes = slice(plane * cells + row * width, plane * cells + (row + 1) * width)
+                block = source[plane, row]
+                for c in range(3):
+                    start = pl.multiple_of(c * span + at * chans, chans)
+                    right[pl.ds(start, chans), lanes] = shifted(block, c - 1)
+
+    for plane in range(-1, depth + 1):
+        for row in range(height):
+            if 0 <= plane < depth:
+                block = grad[plane, row]
+            else:
+                block = edge_row(odd, beside, across, plane < 0, row)
+            for a in range(3):
+                target = plane + a - 1
+                if 0 <= target < depth:
+                    for b in range(3):
+                        at = row + b - 1
+                        if 0 <= at < height:
+                            rows = slice((3 * a + b) * filters, (3 * a + b + 1) * filters)
+                            left[rows, target * cells + at * width : target * cells + (at + 1) * width] = block
+    zero = jnp.zeros((filters, width), left.dtype)
+    for a in range(3):
+        for plane in range(depth):
+            last = plane * cells + cells - width
+            left[3 * a * filters : (3 * a + 1) * filters, last : last + width] = zero
+            left[(3 * a + 2) * filters : (3 * a + 3) * filters, plane * cells : plane * cells + width] = zero
+
+    total = lax.dot_general(
+        left[...], right[...], (((1,), (1,)), ((), ())), preferred_element_type=jnp.float32
+    )
+    total = total * scale
+    peak = jnp.maximum(jnp.max(jnp.abs(total)), 1e-30)
+    exponent = jnp.ceil(jnp.log2(jnp.full(out_ref.shape[2:], peak, jnp.float32))) + 1.0
+    rows = out_ref.shape[2]
+    for shard, at in enumerate(order):
+        for tap in range(27):
+            a, b, c = tap // 9, tap // 3 % 3, tap % 3
+            first = (3 * a + b) * filters + shard * rows
+            out_ref[at, tap] = total[first : first + rows, c * span : (c + 1) * span]
+        out_ref[at, 27] = exponent
+
+
+def kernel_grad_part(place, own, other, grad, beside, across, scale, order):
+    depth, height, chans, width = own.shape
+    filters = grad.shape[2]
+    cells = depth * height * width
+    rows = filters // len(order)
+    return pl.pallas_call(
+        functools.partial(kernel_grad_kernel, scale, order),
+        out_shape=jax.ShapeDtypeStruct((len(order), 28, rows, 2 * chans), jnp.float32),
+        in_specs=specs(5),
+        out_specs=specs(1)[1],
+        scratch_shapes=[
+            pltpu.VMEM((9 * filters, cells), jnp.bfloat16),
+            pltpu.VMEM((6 * chans, cells), jnp.bfloat16),
+        ],
+        compiler_params=pltpu.CompilerParams(vmem_limit_bytes=VMEM_LIMIT),
+        cost_estimate=SMALL_COST,
+        name="kernel_grad",
+    )(place, own, other, grad, beside, across)
+
+
+def output_kernel(place, own, other, far_own, far_other, taps, out_ref, beside_ref, across_ref, weights, stack, acc):
+    depth, height, chans, width = own.shape
+    filters, total = taps.shape[1], taps.shape[2]
+    for tap in range(27):
+        a, b, c = tap // 9, tap // 3 % 3, tap % 3
+        weights[(3 * a + b) * filters : (3 * a + b + 1) * filters, c * total : (c + 1) * total] = taps[tap]
+    core, row_of, odd = place[0], place[1], place[2] & 1
+    homes = (
+        2 * row_of + core,
+        2 * row_of + 1 - core,
+        2 * (1 - row_of) + core,
+        2 * (1 - row_of) + 1 - core,
+    )
+    acc[...] = jnp.zeros_like(acc)
+    for plane in range(depth):
+        for block, home in zip((own, other, far_own, far_other), homes):
+            for row in range(height):
+                lanes = slice(row * width, (row + 1) * width)
+                for c in range(3):
+                    start = pl.multiple_of(c * total + home * chans, chans)
+                    stack[pl.ds(start, chans), lanes] = shifted(block[plane, row], c - 1)
+        for row in range(0, height, 2):
+            part = jnp.dot(
+                weights[...], stack[:, row * width : (row + 2) * width], preferred_element_type=jnp.float32
+            )
+            for a in range(3):
+                for b in range(3):
+                    block = part[(3 * a + b) * filters : (3 * a + b + 1) * filters]
+                    for k in range(2):
+                        at = row + k - b + 1
+                        if 0 <= at < height:
+                            acc[plane - a + 2, at] += block[:, k * width : (k + 1) * width]
+    out_ref[...] = acc[1 : depth + 1]
+    low, high = acc[0], acc[depth + 1]
+    beside_ref[...] = jnp.where(odd == 0, high, low)
+    across_ref[...] = jnp.where(odd == 0, low, high)
+
+
+def output_part(place, own, other, far_own, far_other, taps):
+    depth, height, chans, width = own.shape
+    filters, total = taps.shape[1], taps.shape[2]
+    plane = jax.ShapeDtypeStruct((height, filters, width), jnp.float32)
+    return pl.pallas_call(
+        output_kernel,
+        out_shape=[jax.ShapeDtypeStruct((depth, height, filters, width), jnp.float32), plane, plane],
+        in_specs=specs(5),
+        out_specs=specs(3)[1:],
+        scratch_shapes=[
+            pltpu.VMEM((9 * filters, 3 * total), jnp.bfloat16),
+            pltpu.VMEM((3 * total, height * width), jnp.bfloat16),
+            pltpu.VMEM((depth + 2, height, filters, width), jnp.float32),
+        ],
+        compiler_params=pltpu.CompilerParams(vmem_limit_bytes=VMEM_LIMIT),
+        cost_estimate=SMALL_COST,
+        name="output_map",
+    )(place, own, other, far_own, far_other, taps)
+
+
+def input_grad_kernel(place, grad, beside, across, taps, out_ref, weights, stack):
+    depth, height, filters, width = grad.shape
+    total = taps.shape[2]
+    chans = out_ref.shape[4]
+    span = 3 * filters
+    odd = place[2] & 1
+    weights[...] = jnp.transpose(taps[...].reshape(27 * filters, total))
+    zero = jnp.zeros((span, width), stack.dtype)
+    for plane in range(depth + 2):
+        stack[plane, 0] = zero
+        stack[plane, height + 1] = zero
+        for row in range(height):
+            if 0 < plane < depth + 1:
+                block = grad[plane - 1, row]
+            else:
+                block = edge_row(odd, beside, across, plane == 0, row)
+            for c in range(3):
+                stack[plane, row + 1, c * filters : (c + 1) * filters] = shifted(block, 1 - c)
+    for plane in range(depth):
+        for row in range(0, height, 2):
+            halves = []
+            for k in range(2):
+                pieces = [stack[plane - a + 2, row + k - b + 2] for a in range(3) for b in range(3)]
+                halves.append(jnp.concatenate(pieces, axis=0))
+            part = jnp.dot(weights[...], jnp.concatenate(halves, axis=1), preferred_element_type=jnp.float32)
+            for k in range(2):
+                for block in range(total // chans):
+                    out_ref[block // 2, block % 2, plane, row + k] = part[
+                        block * chans : (block + 1) * chans, k * width : (k + 1) * width
+                    ]
+
+
+def input_grad_part(place, grad, beside, across, taps, chans):
+    depth, height, filters, width = grad.shape
+    total = taps.shape[2]
+    return pl.pallas_call(
+        input_grad_kernel,
+        out_shape=jax.ShapeDtypeStruct((2, 2, depth, height, chans, width), jnp.float32),
+        in_specs=specs(4),
+        out_specs=specs(1)[1],
+        scratch_shapes=[
+            pltpu.VMEM((total, 27 * filters), jnp.bfloat16),
+            pltpu.VMEM((depth + 2, height + 2, 3 * filters, width), jnp.bfloat16),
+        ],
+        compiler_params=pltpu.CompilerParams(vmem_limit_bytes=VMEM_LIMIT),
+        cost_estimate=SMALL_COST,
+        name="input_grad",
+    )(place, grad, beside, across, taps)
+
+
+def after(value, *others):
+    return lax.optimization_barrier((value,) + others)[0]
+
+
+def swap(value, axis, bit):
+    count = lax.axis_size(axis)
+    return lax.ppermute(value, axis, [(i, i ^ (1 << bit)) for i in range(count)])
+
+
+def across_swap(plane):
+    count = lax.axis_size("space")
+    pairs = [(i, i + 1) for i in range(1, count - 1, 2)]
+    return lax.ppermute(plane, "space", pairs + [(j, i) for i, j in pairs])
+
+
+def is_head(shards):
+    return lax.broadcasted_iota(jnp.int32, shards.shape, 1) == shards.shape[1] - 1
+
+
+def message(shards):
+    factor = jnp.where(is_head(shards), 1.0, jnp.exp2(14.0 - shards[:, -1:]))
+    return (shards * factor).astype(jnp.float16)
+
+
+def opened(received):
+    shards = received.astype(jnp.float32)
+    return shards * jnp.where(is_head(shards), 1.0, jnp.exp2(shards[:, -1:] - 14.0))
+
+
+def summed(kept, received):
+    terms = opened(received)
+    return jnp.where(is_head(kept), jnp.maximum(kept, terms) + 1.0, kept + terms)
+
+
+def cut(shards, bit):
+    mine = (lax.axis_index("space") >> bit) & 1
+    halves = shards.reshape((2, shards.shape[0] // 2) + shards.shape[1:])
+    away = lax.dynamic_index_in_dim(halves, 1 - mine, 0, keepdims=False)
+    kept = lax.dynamic_index_in_dim(halves, mine, 0, keepdims=False)
+    return kept, message(away)
+
+
+def shard_places(bits):
+    edges = len(bits)
+    return tuple(
+        sum((shard >> bit & 1) << (edges - 1 - step) for step, bit in enumerate(bits))
+        for shard in range(1 << edges)
+    )
+
+
+def assemble_kernel(flips, place, *refs):
+    parts, out_ref = refs[:-1], refs[-1]
+    for index, (part, part_flips) in enumerate(zip(parts, flips)):
+        rows, lanes = part.shape[2:]
+        side = place[1] if index < len(parts) // 2 else 1 - place[1]
+        for at, flip in enumerate(part_flips):
+            start = pl.multiple_of((place[2] ^ flip) * rows, rows)
+            for half in range(2):
+
+                @pl.when(side == half)
+                def _():
+                    out_ref[:, pl.ds(start, rows), half * lanes : (half + 1) * lanes] = part[at, :27]
+
+
+def assembled(place, parts, flips, filters):
+    lanes = parts[0].shape[-1]
+    return pl.pallas_call(
+        functools.partial(assemble_kernel, flips),
+        out_shape=jax.ShapeDtypeStruct((27, filters, 2 * lanes), jnp.float32),
+        in_specs=specs(len(parts)),
+        out_specs=specs(1)[1],
+        compiler_params=pltpu.CompilerParams(vmem_limit_bytes=VMEM_LIMIT),
+        cost_estimate=SMALL_COST,
+        name="assemble",
+    )(place, *parts)
+
+
+def cube_on_device(volume, kernel, cotangent):
+    depth, chans, height, width = volume.shape
+    filters = cotangent.shape[1]
+    count = lax.axis_size("space")
+    scale = 1.0 / math.sqrt(depth * count * height * width)
+    here = lax.axis_index("chan")
+    place = jnp.stack([here & 1, here >> 1, lax.axis_index("space")]).astype(jnp.int32)
+    edges = count.bit_length() - 1
+    near_bits = tuple(range(edges))
+    far_bits = (1, 0) + tuple(range(2, edges))
+
+    own = jnp.transpose(volume, (0, 2, 1, 3))
+    grad = jnp.transpose(cotangent, (0, 2, 1, 3))
+    odd = lax.axis_index("space") & 1
+    grad_beside = swap(
+        lax.dynamic_index_in_dim(grad, (1 - odd) * (depth - 1), 0, keepdims=False), "space", 0
+    )
+    grad_across = across_swap(
+        lax.dynamic_index_in_dim(grad, odd * (depth - 1), 0, keepdims=False)
+    )
+    far_own = swap(own, "chan", 1)
+    other = swap(own, "chan", 0)
+    far_other = swap(after(far_own, grad_beside, grad_across), "chan", 0)
+    near = kernel_grad_part(
+        place, own, other, grad, grad_beside, grad_across, scale, shard_places(near_bits)
+    )
+    far = kernel_grad_part(
+        place, after(far_own, near), far_other, grad, grad_beside, grad_across, scale, shard_places(far_bits)
+    )
+    chains = [Chain(after(near, far), near_bits), Chain(far, far_bits)]
+    last = after(chains[0].sent, chains[1].sent)
+
+    terms = input_grad_part(place, after(grad, last), grad_beside, grad_across, kernel, chans)
+    kept = lax.dynamic_index_in_dim(terms, place[0], 1, keepdims=False)
+    away = lax.dynamic_index_in_dim(terms, 1 - place[0], 1, keepdims=False)
+    received_terms = swap(away, "chan", 0)
+
+    due = {2: [away]}
+    for turn in range(2, 4 * edges):
+        chain = chains[turn % 2]
+        chain.step([last] + due.get(turn, []))
+        last = chain.sent
+        if turn == 3:
+            half_terms = kept + after(received_terms, last)
+            kept = lax.dynamic_index_in_dim(half_terms, place[1], 0, keepdims=False)
+            away = lax.dynamic_index_in_dim(half_terms, 1 - place[1], 0, keepdims=False)
+            received_terms = swap(away, "chan", 1)
+            due[turn + 1] = [away]
+        if turn == 5:
+            inner, beside, across = output_part(place, after(own, last), other, far_own, far_other, kernel)
+            beside, across = swap(beside, "space", 0), across_swap(across)
+            due[turn + 1] = [inner]
+        if turn == 2 * edges + 1:
+            total = kept + after(received_terms, last)
+            input_grad = jnp.transpose(total.astype(jnp.bfloat16), (0, 2, 1, 3))
+            due[turn + 1] = [input_grad]
+        if turn == 2 * edges + 3:
+            beside, across = after(beside, last), after(across, last)
+            rims = [jnp.where(odd == 0, across, beside), jnp.where(odd == 0, beside, across)]
+            rims = jnp.stack(rims[:1] + [jnp.zeros_like(beside)] * (depth - 2) + rims[1:])
+            output_map = jnp.transpose((inner + rims).astype(jnp.bfloat16), (0, 2, 1, 3))
+            due[turn + 2] = [output_map]
+    parts, flips = [], []
+    for chain in chains:
+        parts += [opened(chain.sent), opened(chain.received)]
+        flips += [chain.whose, [flip ^ (1 << chain.bits[0]) for flip in chain.whose]]
+    kernel_grad = assembled(place, parts, flips, filters)
+    return output_map, input_grad, kernel_grad
+
+
+class Chain:
+    def __init__(self, shards, bits):
+        self.bits, self.at, self.whose = bits, 0, [0]
+        self.kept, self.sent = cut(shards, bits[0])
+        self.received = swap(self.sent, "space", bits[0])
+
+    def step(self, earlier):
+        received = after(self.received, *earlier)
+        self.at += 1
+        edges = len(self.bits)
+        if self.at <= edges:
+            shards = summed(self.kept, received)
+            if self.at < edges:
+                bit = self.bits[self.at]
+                self.kept, self.sent = cut(shards, bit)
+            else:
+                bit = self.bits[-1]
+                self.sent = message(shards)
+        else:
+            bit = self.bits[2 * edges - 1 - self.at]
+            self.sent = jnp.concatenate([self.sent, received], axis=0)
+            flip = 1 << self.bits[2 * edges - self.at]
+            self.whose = self.whose + [whose ^ flip for whose in self.whose]
+        self.received = swap(self.sent, "space", bit)
 
 
 def with_halo(block, sides, width):
@@ -36,7 +416,7 @@
     return jnp.concatenate(windows, axis=1)
 
 
-def on_device(volume, kernel, cotangent):
+def plain_on_device(volume, kernel, cotangent):
     depth, chans_local, height, width = volume.shape
     filters_local = cotangent.shape[1]
     cells = height * width
@@ -80,6 +460,15 @@
     input_grad = total.astype(jnp.bfloat16).reshape(depth, chans_local, height, width)
     return (output_map, input_grad, kernel_grad)
 
+def on_device(volume, kernel, cotangent):
+    count, ways = lax.axis_size("space"), lax.axis_size("chan")
+    chans, width = volume.shape[1], volume.shape[3]
+    filters = cotangent.shape[1]
+    cube = ways == 4 and count >= 4 and count & (count - 1) == 0 and volume.shape[0] >= 2
+    if cube and width == 128 and (2 * chans) % 128 == 0 and filters % (8 * count) == 0:
+        return cube_on_device(volume, kernel, cotangent)
+    return plain_on_device(volume, kernel, cotangent)
+
 
 def solution(mesh):
     return jax.shard_map(

time: 231 us -> 74.6 us (0.32); the launches traced: 227 us -> 74.3 us
  waiting for transfers between devices: 99.1 us -> 19.8 us
  matrix products: 32.3 us -> 0 us
  other arithmetic: 37.6 us -> 6.59 us
  local copies, waits for them, and re-layouts: 27 us -> 4.25 us
  Pallas kernels: 0 us -> 13.5 us
  between operations: 14.4 us -> 1.18 us
  starting transfers between devices: 16.1 us -> 29 us
    psum x1 -> x0, waiting for transfers between devices: 78.6 us -> none  [on_device(): kernel_grad = lax.psum(kernel_acc, 'space') * scale_factor]
    dot_general x9 -> x0, matrix products: 32.3 us -> none  [the longest x3 17.1 us: on_device(): jnp.einsum('kj,zjp->zkp', weights, window, preferred_element_type=jnp.flo...]
    unnamed x14 -> x0, other arithmetic: 27.3 us -> none
    ppermute x4 -> x21, starting transfers between devices: 11.8 us -> 29 us  [the longest x19 27.5 us: swap(): return lax.ppermute(value, axis, [(i, i ^ 1 << bit) for i in range(count)])]
    pallas_call x0 -> x5, Pallas kernels: none -> 13.5 us  [the longest x2 5.23 us: kernel_grad_part(): pl.pallas_call(functools.partial(kernel_grad_kernel, scale, order), out_s...]
    all_to_all x1 -> x0, waiting for transfers between devices: 10.6 us -> none  [on_device(): lax.all_to_all(kernel, 'chan', split_axis=2, concat_axis=1, tiled=True)]
    ppermute x4 -> x21, waiting for transfers between devices: 9.92 us -> 19.8 us  [the longest x19 19.8 us: swap(): return lax.ppermute(value, axis, [(i, i ^ 1 << bit) for i in range(count)])]
    unnamed x34 -> x17, local copies, waits for them, and re-layouts: 13 us -> 3.59 us
  transfers between devices with their start and end apart: 8 -> 21, of which waited for: 6 -> 10; matrix products, arithmetic and copies ran while one was open for 26% -> 10% of each run, Pallas kernels for 0% -> 12%
where the time goes in v2:
time: 74.6 us; the launch traced here: 74.3 us
  starting transfers between devices  29 us (39%)
  waiting for transfers between devices  19.8 us (27%)
  Pallas kernels  13.5 us (18%)
  other arithmetic  6.59 us (9%)
  local copies, waits for them, and re-layouts  4.25 us (6%)
  between operations  1.18 us (2%)
    ppermute x19, starting transfers between devices, swap(): return lax.ppermute(value, axis, [(i, i ^ 1 << bit) for i in range(count)])  27.5 us
    ppermute x19, waiting for transfers between devices, swap(): return lax.ppermute(value, axis, [(i, i ^ 1 << bit) for i in range(count)])  19.8 us
    pallas_call x2, Pallas kernels, kernel_grad_part(): pl.pallas_call(functools.partial(kernel_grad_kernel, scale, order), out_s...  5.23 us
    unnamed x17, local copies, waits for them, and re-layouts  3.59 us
    pallas_call x1, Pallas kernels, output_part(): pl.pallas_call(output_kernel, out_shape=[jax.ShapeDtypeStruct((depth, hei...  3.44 us
    pallas_call x1, Pallas kernels, input_grad_part(): pl.pallas_call(input_grad_kernel, out_shape=jax.ShapeDtypeStruct((2, 2, d...  2.84 us
    pallas_call x1, Pallas kernels, assembled(): pl.pallas_call(functools.partial(assemble_kernel, flips), out_shape=jax.S...  2.02 us
    select_n x6, other arithmetic, summed(): jnp.where(is_head(kept), jnp.maximum(kept, terms) + 1.0, kept + terms)  1.75 us
  transfers between devices with their start and end apart: 21, of which 10 were waited for; matrix products, arithmetic and copies ran while one was open for 10% of the time, Pallas kernels for 12%

profile of v2, /device:TPU:0, one launch (start us, length us, event | category | flops | bytes accessed | tf_op | source)
XLA Modules:
  0.0 74.3 jit_solution(13877412527094520288)
XLA Ops:
  1.6 3.0 %collective-permute-start = (bf16[2,8,64,128]{3,2,1,0:T(8,128)(2,1)S(1)}, bf16[2,8,64,128]{3,2,1,0:T(8,128)(2,1)S(1)}, u32[]{:S(2)}, u32[]{:S(2)}) collective-permute-start(bf16[2,8,64,128]{3,2,1,0:T(8,128)(2,1)S(1)} %bitcast.132), channel_id=1, source_target_pairs={{0,2},{1,3},{2,0},{3,1},{4,6},{5,7},{6,4},{7,5},{8,10},{9,11},{10,... | collective-permute-start | bytes 786440 | tf_op jit(solution)/shard_map/ppermute | solution.py:222
  5.7 1.6 %collective-permute-start.2 = (bf16[8,64,128]{2,1,0:T(8,128)(2,1)S(1)}, bf16[8,64,128]{2,1,0:T(8,128)(2,1)S(1)}, u32[]{:S(2)}, u32[]{:S(2)}) collective-permute-start(bf16[8,64,128]{2,1,0:T(8,128)(2,1)S(1)} %get-tuple-element.57), channel_id=1, source_target_pairs={{0,4},{4,0},{8,12},{12,8},{16,20},{20,16},{24,28},{28,24},{1,5},{5... | collective-permute-start | bytes 393224 | tf_op jit(solution)/shard_map/ppermute | solution.py:222
  8.0 2.7 %collective-permute-done.2.beside = bf16[8,64,128]{2,1,0:T(8,128)(2,1)S(1)} collective-permute-done((bf16[8,64,128]{2,1,0:T(8,128)(2,1)S(1)}, bf16[8,64,128]{2,1,0:T(8,128)(2,1)S(1)}, u32[]{:S(2)}, u32[]{:S(2)}) %collective-permute-start.2) | collective-permute-done | bytes 131104 | tf_op jit(solution)/shard_map/ppermute | solution.py:222
  11.1 2.6 %kernel_grad.2 = f32[8,28,8,128]{3,2,1,0:T(8,128)S(1)} custom-call(s32[3]{0:T(128)S(1)} %pad_add_fusion.place, bf16[2,8,64,128]{3,2,1,0:T(8,128)(2,1)S(1)} %bitcast.134, bf16[2,8,64,128]{3,2,1,0:T(8,128)(2,1)S(1)} %collective-permute-done.1.other, bf16[2,8,64,128]{3,2,1,0:T(8,128)(2,1)S(1)} %bitcast.125, ...), custom_call_target="tpu_custom_call" | custom-call | flops 1 | bytes 1 | tf_op jit(solution)/shard_map/kernel_grad/pallas_call | solution.py:93
  13.7 2.6 %kernel_grad.3 = f32[8,28,8,128]{3,2,1,0:T(8,128)S(1)} custom-call(s32[3]{0:T(128)S(1)} %pad_add_fusion.place, bf16[2,8,64,128]{3,2,1,0:T(8,128)(2,1)S(1)} %collective-permute-done.own.far_own, bf16[2,8,64,128]{3,2,1,0:T(8,128)(2,1)S(1)} %collective-permute-done.4.other.far_other, bf16[2,8,64,128]{3,2,1,0:T(8,128)(2,1)S(1)} %bitcast.126, ...), custom_call_target="tpu_custom_call" | custom-call | flops 1 | bytes 1 | tf_op jit(solution)/shard_map/kernel_grad/pallas_call | solution.py:93
  18.1 4.6 %collective-permute-start.6 = (f16[4,28,8,128]{3,2,1,0:T(8,128)(2,1)}, f16[4,28,8,128]{3,2,1,0:T(8,128)(2,1)}, u32[]{:S(2)}, u32[]{:S(2)}) collective-permute-start(f16[4,28,8,128]{3,2,1,0:T(8,128)(2,1)} %get-tuple-element.68), channel_id=1, source_target_pairs={{0,4},{4,0},{8,12},{12,8},{16,20},{20,16},{24,28},{28,24},{1,5},{5... | collective-permute-start | bytes 688136 | tf_op jit(solution)/shard_map/ppermute | solution.py:222
  22.7 1.6 %collective-permute-start.5 = (f16[4,28,8,128]{3,2,1,0:T(8,128)(2,1)}, f16[4,28,8,128]{3,2,1,0:T(8,128)(2,1)S(1)}, u32[]{:S(2)}, u32[]{:S(2)}) collective-permute-start(f16[4,28,8,128]{3,2,1,0:T(8,128)(2,1)} %get-tuple-element.69), channel_id=1, source_target_pairs={{0,8},{4,12},{8,0},{12,4},{16,24},{20,28},{24,16},{28,20},{1,9},{5... | collective-permute-start | bytes 688136 | tf_op jit(solution)/shard_map/ppermute | solution.py:222
  24.3 2.8 %input_grad.1 = f32[2,2,2,8,64,128]{5,4,3,2,1,0:T(8,128)S(1)} custom-call(s32[3]{0:T(128)S(1)} %pad_add_fusion.place, bf16[2,8,64,128]{3,2,1,0:T(8,128)(2,1)S(1)} %bitcast.127, bf16[8,64,128]{2,1,0:T(8,128)(2,1)S(1)} %collective-permute-done.2.beside, bf16[8,64,128]{2,1,0:T(8,128)(2,1)S(1)} %collective-permute-done.3.across, bf16[27,64,256]{2,1,0:T(8,128)(2,1)S(1)} %copy-done), custom_call_target="tpu_custom_call" | custom-call | flops 1 | bytes 1 | tf_op jit(solution)/shard_map/input_grad/pallas_call | solution.py:201
  27.3 1.9 %collective-permute-done.6 = f16[4,28,8,128]{3,2,1,0:T(8,128)(2,1)} collective-permute-done((f16[4,28,8,128]{3,2,1,0:T(8,128)(2,1)}, f16[4,28,8,128]{3,2,1,0:T(8,128)(2,1)}, u32[]{:S(2)}, u32[]{:S(2)}) %collective-permute-start.6) | collective-permute-done | bytes 229408 | tf_op jit(solution)/shard_map/ppermute | solution.py:222
  30.3 1.1 %fusion.3 = f32[4,28,8,128]{3,2,1,0:T(8,128)S(1)} fusion(f32[2,4,28,8,128]{4,3,2,1,0:T(8,128)S(1)} %bitcast.131, s32[]{:T(128)S(6)} %select_n.191, f32[4,8,128]{2,1,0:T(8,128)S(1)} %fusion.29, pred[28]{0:T(512)(128)(4,1)S(1)} %iota_compare_fusion, f16[4,28,8,128]{3,2,1,0:T(8,128)(2,1)} %collective-permute-done.6), kind=kLoop, calls=%fused_computation.10 | loop fusion | flops 802816 | bytes 1163296 | tf_op jit(solution)/shard_map/jit(_where)/select_n | solution.py:247
  31.6 2.9 %collective-permute-start.8 = (f16[2,28,8,128]{3,2,1,0:T(8,128)(2,1)S(1)}, f16[2,28,8,128]{3,2,1,0:T(8,128)(2,1)S(1)}, u32[]{:S(2)}, u32[]{:S(2)}) collective-permute-start(f16[2,28,8,128]{3,2,1,0:T(8,128)(2,1)S(1)} %multiply_convert_fusion.3), channel_id=1, source_target_pairs={{0,8},{4,12},{8,0},{12,4},{16,24},{20,28},{24,16},{28,20},{1,9},{5... | collective-permute-start | bytes 344072 | tf_op jit(solution)/shard_map/ppermute | solution.py:222
  36.1 1.3 %collective-permute-done.8 = f16[2,28,8,128]{3,2,1,0:T(8,128)(2,1)S(1)} collective-permute-done((f16[2,28,8,128]{3,2,1,0:T(8,128)(2,1)S(1)}, f16[2,28,8,128]{3,2,1,0:T(8,128)(2,1)S(1)}, u32[]{:S(2)}, u32[]{:S(2)}) %collective-permute-start.8) | collective-permute-done | bytes 114720 | tf_op jit(solution)/shard_map/ppermute | solution.py:222
  37.7 2.9 %collective-permute-start.12 = (f16[1,28,8,128]{3,2,1,0:T(8,128)(2,1)S(1)}, f16[1,28,8,128]{3,2,1,0:T(8,128)(2,1)S(1)}, u32[]{:S(2)}, u32[]{:S(2)}) collective-permute-start(f16[1,28,8,128]{3,2,1,0:T(8,128)(2,1)S(1)} %multiply_convert_fusion.7), channel_id=1, source_target_pairs={{0,16},{4,20},{8,24},{12,28},{16,0},{20,4},{24,8},{28,12},{1,17},{... | collective-permute-start | bytes 172040 | tf_op jit(solution)/shard_map/ppermute | solution.py:222
  40.9 1.8 %collective-permute-start.11 = (f16[1,28,8,128]{3,2,1,0:T(8,128)(2,1)S(1)}, f16[1,28,8,128]{3,2,1,0:T(8,128)(2,1)S(1)}, u32[]{:S(2)}, u32[]{:S(2)}) collective-permute-start(f16[1,28,8,128]{3,2,1,0:T(8,128)(2,1)S(1)} %multiply_convert_fusion.6), channel_id=1, source_target_pairs={{0,16},{4,20},{8,24},{12,28},{16,0},{20,4},{24,8},{28,12},{1,17},{... | collective-permute-start | bytes 172040 | tf_op jit(solution)/shard_map/ppermute | solution.py:222
  43.2 3.4 %output_map.1 = (f32[2,8,64,128]{3,2,1,0:T(8,128)S(1)}, f32[8,64,128]{2,1,0:T(8,128)S(1)}, f32[8,64,128]{2,1,0:T(8,128)S(1)}) custom-call(s32[3]{0:T(128)S(1)} %pad_add_fusion.place, bf16[2,8,64,128]{3,2,1,0:T(8,128)(2,1)S(1)} %bitcast.135, bf16[2,8,64,128]{3,2,1,0:T(8,128)(2,1)S(1)} %copy-done.4, bf16[2,8,64,128]{3,2,1,0:T(8,128)(2,1)S(1)} %copy-done.2, ...), custom_call_target="tpu_custom_call" | custom-call | flops 1 | bytes 1 | tf_op jit(solution)/shard_map/output_map/pallas_call | solution.py:150
  47.5 3.2 %collective-permute-start.16 = (f32[8,64,128]{2,1,0:T(8,128)S(1)}, f32[8,64,128]{2,1,0:T(8,128)S(1)}, u32[]{:S(2)}, u32[]{:S(2)}) collective-permute-start(f32[8,64,128]{2,1,0:T(8,128)S(1)} %get-tuple-element.45), channel_id=1, source_target_pairs={{0,4},{4,0},{8,12},{12,8},{16,20},{20,16},{24,28},{28,24},{1,5},{5... | collective-permute-start | bytes 786440 | tf_op jit(solution)/shard_map/ppermute | solution.py:222
  50.9 2.4 %collective-permute-start.14 = (f16[1,28,8,128]{3,2,1,0:T(8,128)(2,1)S(1)}, f16[1,28,8,128]{3,2,1,0:T(8,128)(2,1)S(1)}, u32[]{:S(2)}, u32[]{:S(2)}) collective-permute-start(f16[1,28,8,128]{3,2,1,0:T(8,128)(2,1)S(1)} %multiply_convert_fusion.5), channel_id=1, source_target_pairs={{0,16},{4,20},{8,24},{12,28},{16,0},{20,4},{24,8},{28,12},{1,17},{... | collective-permute-start | bytes 172040 | tf_op jit(solution)/shard_map/ppermute | solution.py:222
  54.5 1.0 %fusion.6 = bf16[2,64,8,128]{3,2,1,0:T(8,128)(2,1)} fusion(f32[2,8,64,128]{3,1,2,0:T(8,128)S(1)} %collective-permute-done.15, f32[1,2,8,64,128]{4,3,2,1,0:T(8,128)S(1)} %get-tuple-element.52), kind=kLoop, calls=%fused_computation.23 | loop fusion | flops 262144 | bytes 1310720 | tf_op jit(solution)/shard_map/transpose | solution.py:347
  55.5 3.5 %collective-permute-done.14 = f16[1,28,8,128]{3,2,1,0:T(8,128)(2,1)S(1)} collective-permute-done((f16[1,28,8,128]{3,2,1,0:T(8,128)(2,1)S(1)}, f16[1,28,8,128]{3,2,1,0:T(8,128)(2,1)S(1)}, u32[]{:S(2)}, u32[]{:S(2)}) %collective-permute-start.14) | collective-permute-done | bytes 57376 | tf_op jit(solution)/shard_map/ppermute | solution.py:222
  60.8 3.1 %collective-permute-done.17 = f16[2,28,8,128]{3,2,1,0:T(8,128)(2,1)S(1)} collective-permute-done((f16[2,28,8,128]{3,2,1,0:T(8,128)(2,1)S(1)}, f16[2,28,8,128]{3,2,1,0:T(8,128)(2,1)S(1)}, u32[]{:S(2)}, u32[]{:S(2)}) %collective-permute-start.17) | collective-permute-done | bytes 114720 | tf_op jit(solution)/shard_map/ppermute | solution.py:222
  64.1 1.6 %collective-permute-done.19 = f16[2,28,8,128]{3,2,1,0:T(8,128)(2,1)S(1)} collective-permute-done((f16[2,28,8,128]{3,2,1,0:T(8,128)(2,1)S(1)}, f16[2,28,8,128]{3,2,1,0:T(8,128)(2,1)S(1)}, u32[]{:S(2)}, u32[]{:S(2)}) %collective-permute-start.19) | collective-permute-done | bytes 114720 | tf_op jit(solution)/shard_map/ppermute | solution.py:222
  65.7 1.5 %collective-permute-start.20 = (f16[4,28,8,128]{3,2,1,0:T(8,128)(2,1)S(1)}, f16[4,28,8,128]{3,2,1,0:T(8,128)(2,1)S(1)}, u32[]{:S(2)}, u32[]{:S(2)}) collective-permute-start(f16[4,28,8,128]{3,2,1,0:T(8,128)(2,1)S(1)} %get-tuple-element.60), channel_id=1, source_target_pairs={{0,8},{4,12},{8,0},{12,4},{16,24},{20,28},{24,16},{28,20},{1,9},{5... | collective-permute-start | bytes 688136 | tf_op jit(solution)/shard_map/ppermute | solution.py:222
  67.3 4.5 %collective-permute-done.20 = f16[4,28,8,128]{3,2,1,0:T(8,128)(2,1)S(1)} collective-permute-done((f16[4,28,8,128]{3,2,1,0:T(8,128)(2,1)S(1)}, f16[4,28,8,128]{3,2,1,0:T(8,128)(2,1)S(1)}, u32[]{:S(2)}, u32[]{:S(2)}) %collective-permute-start.20) | collective-permute-done | bytes 229408 | tf_op jit(solution)/shard_map/ppermute | solution.py:222
  72.3 2.0 %assemble.1 = f32[27,64,256]{2,1,0:T(8,128)} custom-call(s32[3]{0:T(128)S(1)} %pad_add_fusion.place, f32[4,28,8,128]{3,2,1,0:T(8,128)S(1)} %get-tuple-element.66.refs_0_, f32[4,28,8,128]{3,2,1,0:T(8,128)S(1)} %get-tuple-element.67.refs_1_, f32[4,28,8,128]{3,2,1,0:T(8,128)S(1)} %get-tuple-element.65.refs_2_, f32[4,28,8,128]{3,2,1,0:T(8,128)S(1)} %get-tuple-element.64.refs_3_), custom_call_target="tpu_custom_call" | custom-call | flops 1 | bytes 1 | tf_op jit(solution)/shard_map/assemble/pallas_call | solution.py:282
  (97 shorter events, 13.3 us)
Async XLA Ops:
  1.6 9.3 %collective-permute-start = (bf16[2,8,64,128]{3,2,1,0:T(8,128)(2,1)S(1)}, bf16[2,8,64,128]{3,2,1,0:T(8,128)(2,1)S(1)}, u32[]{:S(2)}, u32[]{:S(2)}) collective-permute-start(bf16[2,8,64,128]{3,2,1,0:T(8,128)(2,1)S(1)} %bitcast.132), channel_id=1, source_target_pairs={{0,2},{1,3},{2,0},{3,1},{4,6},{5,7},{6,4},{7,5},{8,10},{9,11},{10,... | collective-permute-start | bytes 786440 | tf_op jit(solution)/shard_map/ppermute | solution.py:222
  5.7 5.0 %collective-permute-start.2 = (bf16[8,64,128]{2,1,0:T(8,128)(2,1)S(1)}, bf16[8,64,128]{2,1,0:T(8,128)(2,1)S(1)}, u32[]{:S(2)}, u32[]{:S(2)}) collective-permute-start(bf16[8,64,128]{2,1,0:T(8,128)(2,1)S(1)} %get-tuple-element.57), channel_id=1, source_target_pairs={{0,4},{4,0},{8,12},{12,8},{16,20},{20,16},{24,28},{28,24},{1,5},{5... | collective-permute-start | bytes 393224 | tf_op jit(solution)/shard_map/ppermute | solution.py:222
  7.3 3.5 %collective-permute-start.3 = (bf16[8,64,128]{2,1,0:T(8,128)(2,1)S(1)}, bf16[8,64,128]{2,1,0:T(8,128)(2,1)S(1)}, u32[]{:S(2)}, u32[]{:S(2)}) collective-permute-start(bf16[8,64,128]{2,1,0:T(8,128)(2,1)S(1)} %get-tuple-element.56), channel_id=1, source_target_pairs={{4,8},{12,16},{20,24},{8,4},{16,12},{24,20},{5,9},{13,17},{21,25},... | collective-permute-start | bytes 393224 | tf_op jit(solution)/shard_map/ppermute | solution.py:228
  7.9 3.1 %collective-permute-start.1 = (bf16[2,8,64,128]{3,2,1,0:T(8,128)(2,1)S(1)}, bf16[2,8,64,128]{3,2,1,0:T(8,128)(2,1)S(1)}, u32[]{:S(2)}, u32[]{:S(2)}) collective-permute-start(bf16[2,8,64,128]{3,2,1,0:T(8,128)(2,1)S(1)} %bitcast.133), channel_id=1, source_target_pairs={{0,1},{1,0},{2,3},{3,2},{4,5},{5,4},{6,7},{7,6},{8,9},{9,8},{10,11... | collective-permute-start | bytes 786440 | tf_op jit(solution)/shard_map/ppermute | solution.py:222
  11.0 2.7 %collective-permute-start.4 = (bf16[2,8,64,128]{3,2,1,0:T(8,128)(2,1)S(1)}, bf16[2,8,64,128]{3,2,1,0:T(8,128)(2,1)S(1)}, u32[]{:S(2)}, u32[]{:S(2)}) collective-permute-start(bf16[2,8,64,128]{3,2,1,0:T(8,128)(2,1)S(1)} %collective-permute-done.own.far_own), channel_id=1, source_target_pairs={{0,1},{1,0},{2,3},{3,2},{4,5},{5,4},{6,7},{7,6},{8,9},{9,8},{10,11... | collective-permute-start | bytes 786440 | tf_op jit(solution)/shard_map/ppermute | solution.py:222
  18.1 11.2 %collective-permute-start.6 = (f16[4,28,8,128]{3,2,1,0:T(8,128)(2,1)}, f16[4,28,8,128]{3,2,1,0:T(8,128)(2,1)}, u32[]{:S(2)}, u32[]{:S(2)}) collective-permute-start(f16[4,28,8,128]{3,2,1,0:T(8,128)(2,1)} %get-tuple-element.68), channel_id=1, source_target_pairs={{0,4},{4,0},{8,12},{12,8},{16,20},{20,16},{24,28},{28,24},{1,5},{5... | collective-permute-start | bytes 688136 | tf_op jit(solution)/shard_map/ppermute | solution.py:222
  22.7 11.7 %collective-permute-start.5 = (f16[4,28,8,128]{3,2,1,0:T(8,128)(2,1)}, f16[4,28,8,128]{3,2,1,0:T(8,128)(2,1)S(1)}, u32[]{:S(2)}, u32[]{:S(2)}) collective-permute-start(f16[4,28,8,128]{3,2,1,0:T(8,128)(2,1)} %get-tuple-element.69), channel_id=1, source_target_pairs={{0,8},{4,12},{8,0},{12,4},{16,24},{20,28},{24,16},{28,20},{1,9},{5... | collective-permute-start | bytes 688136 | tf_op jit(solution)/shard_map/ppermute | solution.py:222
  27.3 8.2 %collective-permute-start.9 = (f32[2,2,8,64,128]{4,3,2,1,0:T(8,128)S(1)}, f32[2,2,8,64,128]{4,3,2,1,0:T(8,128)S(1)}, u32[]{:S(2)}, u32[]{:S(2)}) collective-permute-start(f32[2,2,8,64,128]{4,3,2,1,0:T(8,128)S(1)} %dynamic-slice_bitcast_fusion), channel_id=1, source_target_pairs={{0,1},{1,0},{2,3},{3,2},{4,5},{5,4},{6,7},{7,6},{8,9},{9,8},{10,11... | collective-permute-start | bytes 3145736 | tf_op jit(solution)/shard_map/ppermute | solution.py:222
  31.6 5.9 %collective-permute-start.8 = (f16[2,28,8,128]{3,2,1,0:T(8,128)(2,1)S(1)}, f16[2,28,8,128]{3,2,1,0:T(8,128)(2,1)S(1)}, u32[]{:S(2)}, u32[]{:S(2)}) collective-permute-start(f16[2,28,8,128]{3,2,1,0:T(8,128)(2,1)S(1)} %multiply_convert_fusion.3), channel_id=1, source_target_pairs={{0,8},{4,12},{8,0},{12,4},{16,24},{20,28},{24,16},{28,20},{1,9},{5... | collective-permute-start | bytes 344072 | tf_op jit(solution)/shard_map/ppermute | solution.py:222
  34.8 5.8 %collective-permute-start.7 = (f16[2,28,8,128]{3,2,1,0:T(8,128)(2,1)S(1)}, f16[2,28,8,128]{3,2,1,0:T(8,128)(2,1)S(1)}, u32[]{:S(2)}, u32[]{:S(2)}) collective-permute-start(f16[2,28,8,128]{3,2,1,0:T(8,128)(2,1)S(1)} %multiply_convert_fusion.2), channel_id=1, source_target_pairs={{0,4},{4,0},{8,12},{12,8},{16,20},{20,16},{24,28},{28,24},{1,5},{5... | collective-permute-start | bytes 344072 | tf_op jit(solution)/shard_map/ppermute | solution.py:222
  35.7 7.4 %copy-start.2 = (bf16[2,8,64,128]{3,2,1,0:T(8,128)(2,1)S(1)}, bf16[2,8,64,128]{3,2,1,0:T(8,128)(2,1)}, u32[]{:S(2)}) copy-start(bf16[2,8,64,128]{3,2,1,0:T(8,128)(2,1)} %copy-done.1) | copy-start | bytes 786436
  35.8 7.4 %copy-start.4 = (bf16[2,8,64,128]{3,2,1,0:T(8,128)(2,1)S(1)}, bf16[2,8,64,128]{3,2,1,0:T(8,128)(2,1)}, u32[]{:S(2)}) copy-start(bf16[2,8,64,128]{3,2,1,0:T(8,128)(2,1)} %copy-done.3) | copy-start | bytes 786436
  35.8 7.4 %copy-start.6 = (bf16[2,8,64,128]{3,2,1,0:T(8,128)(2,1)S(1)}, bf16[2,8,64,128]{3,2,1,0:T(8,128)(2,1)}, u32[]{:S(2)}) copy-start(bf16[2,8,64,128]{3,2,1,0:T(8,128)(2,1)} %copy-done.5) | copy-start | bytes 786436
  37.7 12.9 %collective-permute-start.12 = (f16[1,28,8,128]{3,2,1,0:T(8,128)(2,1)S(1)}, f16[1,28,8,128]{3,2,1,0:T(8,128)(2,1)S(1)}, u32[]{:S(2)}, u32[]{:S(2)}) collective-permute-start(f16[1,28,8,128]{3,2,1,0:T(8,128)(2,1)S(1)} %multiply_convert_fusion.7), channel_id=1, source_target_pairs={{0,16},{4,20},{8,24},{12,28},{16,0},{20,4},{24,8},{28,12},{1,17},{... | collective-permute-start | bytes 172040 | tf_op jit(solution)/shard_map/ppermute | solution.py:222
  40.9 12.5 %collective-permute-start.11 = (f16[1,28,8,128]{3,2,1,0:T(8,128)(2,1)S(1)}, f16[1,28,8,128]{3,2,1,0:T(8,128)(2,1)S(1)}, u32[]{:S(2)}, u32[]{:S(2)}) collective-permute-start(f16[1,28,8,128]{3,2,1,0:T(8,128)(2,1)S(1)} %multiply_convert_fusion.6), channel_id=1, source_target_pairs={{0,16},{4,20},{8,24},{12,28},{16,0},{20,4},{24,8},{28,12},{1,17},{... | collective-permute-start | bytes 172040 | tf_op jit(solution)/shard_map/ppermute | solution.py:222
  42.6 11.8 %collective-permute-start.15 = (f32[2,8,64,128]{3,1,2,0:T(8,128)S(1)}, f32[2,8,64,128]{3,1,2,0:T(8,128)S(1)}, u32[]{:S(2)}, u32[]{:S(2)}) collective-permute-start(f32[2,8,64,128]{3,1,2,0:T(8,128)S(1)} %bitcast.142), channel_id=1, source_target_pairs={{0,2},{1,3},{2,0},{3,1},{4,6},{5,7},{6,4},{7,5},{8,10},{9,11},{10,... | collective-permute-start | bytes 1572872 | tf_op jit(solution)/shard_map/ppermute | solution.py:222
  46.6 13.2 %collective-permute-start.10 = (f32[8,64,128]{2,1,0:T(8,128)S(1)}, f32[8,64,128]{2,1,0:T(8,128)S(1)}, u32[]{:S(2)}, u32[]{:S(2)}) collective-permute-start(f32[8,64,128]{2,1,0:T(8,128)S(1)} %get-tuple-element.38), channel_id=1, source_target_pairs={{4,8},{12,16},{20,24},{8,4},{16,12},{24,20},{5,9},{13,17},{21,25},... | collective-permute-start | bytes 786440 | tf_op jit(solution)/shard_map/ppermute | solution.py:228
  47.5 12.3 %collective-permute-start.16 = (f32[8,64,128]{2,1,0:T(8,128)S(1)}, f32[8,64,128]{2,1,0:T(8,128)S(1)}, u32[]{:S(2)}, u32[]{:S(2)}) collective-permute-start(f32[8,64,128]{2,1,0:T(8,128)S(1)} %get-tuple-element.45), channel_id=1, source_target_pairs={{0,4},{4,0},{8,12},{12,8},{16,20},{20,16},{24,28},{28,24},{1,5},{5... | collective-permute-start | bytes 786440 | tf_op jit(solution)/shard_map/ppermute | solution.py:222
  50.9 8.1 %collective-permute-start.14 = (f16[1,28,8,128]{3,2,1,0:T(8,128)(2,1)S(1)}, f16[1,28,8,128]{3,2,1,0:T(8,128)(2,1)S(1)}, u32[]{:S(2)}, u32[]{:S(2)}) collective-permute-start(f16[1,28,8,128]{3,2,1,0:T(8,128)(2,1)S(1)} %multiply_convert_fusion.5), channel_id=1, source_target_pairs={{0,16},{4,20},{8,24},{12,28},{16,0},{20,4},{24,8},{28,12},{1,17},{... | collective-permute-start | bytes 172040 | tf_op jit(solution)/shard_map/ppermute | solution.py:222
  53.6 6.0 %collective-permute-start.13 = (f16[1,28,8,128]{3,2,1,0:T(8,128)(2,1)S(1)}, f16[1,28,8,128]{3,2,1,0:T(8,128)(2,1)S(1)}, u32[]{:S(2)}, u32[]{:S(2)}) collective-permute-start(f16[1,28,8,128]{3,2,1,0:T(8,128)(2,1)S(1)} %multiply_convert_fusion.4), channel_id=1, source_target_pairs={{0,16},{4,20},{8,24},{12,28},{16,0},{20,4},{24,8},{28,12},{1,17},{... | collective-permute-start | bytes 172040 | tf_op jit(solution)/shard_map/ppermute | solution.py:222
  59.1 4.9 %collective-permute-start.17 = (f16[2,28,8,128]{3,2,1,0:T(8,128)(2,1)S(1)}, f16[2,28,8,128]{3,2,1,0:T(8,128)(2,1)S(1)}, u32[]{:S(2)}, u32[]{:S(2)}) collective-permute-start(f16[2,28,8,128]{3,2,1,0:T(8,128)(2,1)S(1)} %pad_maximum_fusion.2), channel_id=1, source_target_pairs={{0,8},{4,12},{8,0},{12,4},{16,24},{20,28},{24,16},{28,20},{1,9},{5... | collective-permute-start | bytes 344072 | tf_op jit(solution)/shard_map/ppermute | solution.py:222
  59.7 6.0 %collective-permute-start.19 = (f16[2,28,8,128]{3,2,1,0:T(8,128)(2,1)S(1)}, f16[2,28,8,128]{3,2,1,0:T(8,128)(2,1)S(1)}, u32[]{:S(2)}, u32[]{:S(2)}) collective-permute-start(f16[2,28,8,128]{3,2,1,0:T(8,128)(2,1)S(1)} %pad_maximum_fusion.3), channel_id=1, source_target_pairs={{0,4},{4,0},{8,12},{12,8},{16,20},{20,16},{24,28},{28,24},{1,5},{5... | collective-permute-start | bytes 344072 | tf_op jit(solution)/shard_map/ppermute | solution.py:222
  64.0 7.9 %collective-permute-start.18 = (f16[4,28,8,128]{3,2,1,0:T(8,128)(2,1)S(1)}, f16[4,28,8,128]{3,2,1,0:T(8,128)(2,1)S(1)}, u32[]{:S(2)}, u32[]{:S(2)}) collective-permute-start(f16[4,28,8,128]{3,2,1,0:T(8,128)(2,1)S(1)} %get-tuple-element.62), channel_id=1, source_target_pairs={{0,4},{4,0},{8,12},{12,8},{16,20},{20,16},{24,28},{28,24},{1,5},{5... | collective-permute-start | bytes 688136 | tf_op jit(solution)/shard_map/ppermute | solution.py:222
  65.7 6.1 %collective-permute-start.20 = (f16[4,28,8,128]{3,2,1,0:T(8,128)(2,1)S(1)}, f16[4,28,8,128]{3,2,1,0:T(8,128)(2,1)S(1)}, u32[]{:S(2)}, u32[]{:S(2)}) collective-permute-start(f16[4,28,8,128]{3,2,1,0:T(8,128)(2,1)S(1)} %get-tuple-element.60), channel_id=1, source_target_pairs={{0,8},{4,12},{8,0},{12,4},{16,24},{20,28},{24,16},{28,20},{1,9},{5... | collective-permute-start | bytes 688136 | tf_op jit(solution)/shard_map/ppermute | solution.py:222
  (4 other events, 13.3 us)

commit v3 on v2

--- a/solution.py
+++ b/solution.py
@@ -190,7 +190,7 @@
             part = jnp.dot(weights[...], jnp.concatenate(halves, axis=1), preferred_element_type=jnp.float32)
             for k in range(2):
                 for block in range(total // chans):
-                    out_ref[block // 2, block % 2, plane, row + k] = part[
+                    out_ref[block % 2, block // 2, plane, row + k] = part[
                         block * chans : (block + 1) * chans, k * width : (k + 1) * width
                     ]
 
@@ -213,6 +213,10 @@
     )(place, grad, beside, across, taps)
 
 
+def entry(values, at):
+    return lax.dynamic_index_in_dim(values, at, 0, keepdims=False)
+
+
 def after(value, *others):
     return lax.optimization_barrier((value,) + others)[0]
 
@@ -316,42 +320,45 @@
     near = kernel_grad_part(
         place, own, other, grad, grad_beside, grad_across, scale, shard_places(near_bits)
     )
+    chains = [Chain(near, near_bits)]
     far = kernel_grad_part(
-        place, after(far_own, near), far_other, grad, grad_beside, grad_across, scale, shard_places(far_bits)
-    )
-    chains = [Chain(after(near, far), near_bits), Chain(far, far_bits)]
-    last = after(chains[0].sent, chains[1].sent)
-
-    terms = input_grad_part(place, after(grad, last), grad_beside, grad_across, kernel, chans)
-    kept = lax.dynamic_index_in_dim(terms, place[0], 1, keepdims=False)
-    away = lax.dynamic_index_in_dim(terms, 1 - place[0], 1, keepdims=False)
-    received_terms = swap(away, "chan", 0)
-
-    due = {2: [away]}
-    for turn in range(2, 4 * edges):
-        chain = chains[turn % 2]
-        chain.step([last] + due.get(turn, []))
-        last = chain.sent
+        place, after(far_own, chains[0].sent), far_other, grad, grad_beside, grad_across, scale,
+        shard_places(far_bits),
+    )
+    chains.append(Chain(far, far_bits))
+    last = chains[1].sent
+
+    due = {}
+    for turn in range(1, 4 * edges):
+        if turn > 1:
+            chain = chains[turn % 2]
+            chain.step([last] + due.get(turn, []))
+            last = chain.sent
+        if turn == 1:
+            terms = input_grad_part(place, after(grad, last), grad_beside, grad_across, kernel, chans)
+            kept, away = entry(terms, place[0]), entry(terms, 1 - place[0])
+            received_terms = swap(away, "chan", 0)
+            due.setdefault(turn + 1, []).append(away)
         if turn == 3:
-            half_terms = kept + after(received_terms, last)
-            kept = lax.dynamic_index_in_dim(half_terms, place[1], 0, keepdims=False)
-            away = lax.dynamic_index_in_dim(half_terms, 1 - place[1], 0, keepdims=False)
+            terms = kept + after(received_terms, last)
+            kept, away = entry(terms, place[1]), entry(terms, 1 - place[1])
             received_terms = swap(away, "chan", 1)
-            due[turn + 1] = [away]
+            due.setdefault(turn + 1, []).append(away)
         if turn == 5:
             inner, beside, across = output_part(place, after(own, last), other, far_own, far_other, kernel)
-            beside, across = swap(beside, "space", 0), across_swap(across)
-            due[turn + 1] = [inner]
-        if turn == 2 * edges + 1:
+            due.setdefault(turn + 1, []).append(inner)
+        if turn == 7:
+            beside, across = swap(after(beside, last), "space", 0), across_swap(after(across, last))
+        if turn == 7:
             total = kept + after(received_terms, last)
             input_grad = jnp.transpose(total.astype(jnp.bfloat16), (0, 2, 1, 3))
-            due[turn + 1] = [input_grad]
-        if turn == 2 * edges + 3:
+            due.setdefault(turn + 1, []).append(input_grad)
+        if turn == 10:
             beside, across = after(beside, last), after(across, last)
             rims = [jnp.where(odd == 0, across, beside), jnp.where(odd == 0, beside, across)]
             rims = jnp.stack(rims[:1] + [jnp.zeros_like(beside)] * (depth - 2) + rims[1:])
             output_map = jnp.transpose((inner + rims).astype(jnp.bfloat16), (0, 2, 1, 3))
-            due[turn + 2] = [output_map]
+            due.setdefault(turn + 2, []).append(output_map)
     parts, flips = [], []
     for chain in chains:
         parts += [opened(chain.sent), opened(chain.received)]

time: 74.6 us -> 70.6 us (0.946)
  waiting for transfers between devices: 19.8 us -> 15.4 us
  starting transfers between devices: 29 us -> 32.8 us
  other arithmetic: 6.59 us -> 3.97 us
    ppermute x19, waiting for transfers between devices: 19.8 us -> 15.4 us  [swap(): return lax.ppermute(value, axis, [(i, i ^ 1 << bit) for i in range(count)])]
    ppermute x19, starting transfers between devices: 27.5 us -> 31.5 us  [swap(): return lax.ppermute(value, axis, [(i, i ^ 1 << bit) for i in range(count)])]
    select_n x6, other arithmetic: 1.75 us -> 0.81 us  [summed(): jnp.where(is_head(kept), jnp.maximum(kept, terms) + 1.0, kept + terms)]
    convert_element_type x8 -> x9, other arithmetic: 1.12 us -> 0.25 us  [opened(): shards = received.astype(jnp.float32)]
    unnamed x17 -> x5, local copies, waits for them, and re-layouts: 3.59 us -> 2.87 us
    convert_element_type x7 -> x8, other arithmetic: 1.6 us -> 0.89 us  [message(): return (shards * factor).astype(jnp.float16)]
  transfers between devices with their start and end apart: 21 -> 21, of which waited for: 10 -> 8; matrix products, arithmetic and copies ran while one was open for 10% -> 9% of each run, Pallas kernels for 12% -> 16%
where the time goes in v3:
time: 70.6 us; the launch traced here: 70.4 us
  starting transfers between devices  32.8 us (46%)
  waiting for transfers between devices  15.4 us (22%)
  Pallas kernels  13.5 us (19%)
  other arithmetic  3.97 us (6%)
  local copies, waits for them, and re-layouts  3.55 us (5%)
  between operations  1.16 us (2%)
    ppermute x19, starting transfers between devices, swap(): return lax.ppermute(value, axis, [(i, i ^ 1 << bit) for i in range(count)])  31.5 us
    ppermute x19, waiting for transfers between devices, swap(): return lax.ppermute(value, axis, [(i, i ^ 1 << bit) for i in range(count)])  15.4 us
    pallas_call x2, Pallas kernels, kernel_grad_part(): pl.pallas_call(functools.partial(kernel_grad_kernel, scale, order), out_s...  5.22 us
    pallas_call x1, Pallas kernels, output_part(): pl.pallas_call(output_kernel, out_shape=[jax.ShapeDtypeStruct((depth, hei...  3.44 us
    unnamed x5, local copies, waits for them, and re-layouts  2.87 us
    pallas_call x1, Pallas kernels, input_grad_part(): pl.pallas_call(input_grad_kernel, out_shape=jax.ShapeDtypeStruct((2, 2, d...  2.83 us
    pallas_call x1, Pallas kernels, assembled(): pl.pallas_call(functools.partial(assemble_kernel, flips), out_shape=jax.S...  2.02 us
  transfers between devices with their start and end apart: 21, of which 8 were waited for; matrix products, arithmetic and copies ran while one was open for 9% of the time, Pallas kernels for 16%

profile of v3, /device:TPU:0, one launch (start us, length us, event | category | flops | bytes accessed | tf_op | source)
XLA Modules:
  0.0 70.4 jit_solution(898436590221750915)
XLA Ops:
  2.1 2.6 %collective-permute-start = (bf16[2,8,64,128]{3,2,1,0:T(8,128)(2,1)S(1)}, bf16[2,8,64,128]{3,2,1,0:T(8,128)(2,1)S(1)}, u32[]{:S(2)}, u32[]{:S(2)}) collective-permute-start(bf16[2,8,64,128]{3,2,1,0:T(8,128)(2,1)S(1)} %bitcast.139), channel_id=1, source_target_pairs={{0,2},{1,3},{2,0},{3,1},{4,6},{5,7},{6,4},{7,5},{8,10},{9,11},{10,... | collective-permute-start | bytes 786440 | tf_op jit(solution)/shard_map/ppermute | solution.py:226
  5.8 1.6 %collective-permute-start.2 = (bf16[8,64,128]{2,1,0:T(8,128)(2,1)S(1)}, bf16[8,64,128]{2,1,0:T(8,128)(2,1)S(1)}, u32[]{:S(2)}, u32[]{:S(2)}) collective-permute-start(bf16[8,64,128]{2,1,0:T(8,128)(2,1)S(1)} %get-tuple-element.57), channel_id=1, source_target_pairs={{0,4},{4,0},{8,12},{12,8},{16,20},{20,16},{24,28},{28,24},{1,5},{5... | collective-permute-start | bytes 393224 | tf_op jit(solution)/shard_map/ppermute | solution.py:226
  8.1 3.3 %collective-permute-done.2.beside = bf16[8,64,128]{2,1,0:T(8,128)(2,1)S(1)} collective-permute-done((bf16[8,64,128]{2,1,0:T(8,128)(2,1)S(1)}, bf16[8,64,128]{2,1,0:T(8,128)(2,1)S(1)}, u32[]{:S(2)}, u32[]{:S(2)}) %collective-permute-start.2) | collective-permute-done | bytes 131104 | tf_op jit(solution)/shard_map/ppermute | solution.py:226
  11.6 2.6 %kernel_grad.2 = f32[8,28,8,128]{3,2,1,0:T(8,128)S(1)} custom-call(s32[3]{0:T(128)S(1)} %pad_add_fusion.place, bf16[2,8,64,128]{3,2,1,0:T(8,128)(2,1)S(1)} %bitcast.140, bf16[2,8,64,128]{3,2,1,0:T(8,128)(2,1)S(1)} %collective-permute-done.1.other, bf16[2,8,64,128]{3,2,1,0:T(8,128)(2,1)S(1)} %bitcast.129, ...), custom_call_target="tpu_custom_call" | custom-call | flops 1 | bytes 1 | tf_op jit(solution)/shard_map/kernel_grad/pallas_call | solution.py:93
  14.5 4.4 %collective-permute-start.6 = (f16[4,28,8,128]{3,2,1,0:T(8,128)(2,1)S(1)}, f16[4,28,8,128]{3,2,1,0:T(8,128)(2,1)S(1)}, u32[]{:S(2)}, u32[]{:S(2)}) collective-permute-start(f16[4,28,8,128]{3,2,1,0:T(8,128)(2,1)S(1)} %multiply_convert_fusion.1), channel_id=1, source_target_pairs={{0,4},{4,0},{8,12},{12,8},{16,20},{20,16},{24,28},{28,24},{1,5},{5... | collective-permute-start | bytes 688136 | tf_op jit(solution)/shard_map/ppermute | solution.py:226
  18.9 2.6 %kernel_grad.3 = f32[8,28,8,128]{3,2,1,0:T(8,128)S(1)} custom-call(s32[3]{0:T(128)S(1)} %pad_add_fusion.place, bf16[2,8,64,128]{3,2,1,0:T(8,128)(2,1)S(1)} %collective-permute-done.own.far_own, bf16[2,8,64,128]{3,2,1,0:T(8,128)(2,1)S(1)} %collective-permute-done.4.other.far_other, bf16[2,8,64,128]{3,2,1,0:T(8,128)(2,1)S(1)} %bitcast.130, ...), custom_call_target="tpu_custom_call" | custom-call | flops 1 | bytes 1 | tf_op jit(solution)/shard_map/kernel_grad/pallas_call | solution.py:93
  21.7 1.6 %collective-permute-start.5 = (f16[4,28,8,128]{3,2,1,0:T(8,128)(2,1)S(1)}, f16[4,28,8,128]{3,2,1,0:T(8,128)(2,1)S(1)}, u32[]{:S(2)}, u32[]{:S(2)}) collective-permute-start(f16[4,28,8,128]{3,2,1,0:T(8,128)(2,1)S(1)} %multiply_convert_fusion), channel_id=1, source_target_pairs={{0,8},{4,12},{8,0},{12,4},{16,24},{20,28},{24,16},{28,20},{1,9},{5... | collective-permute-start | bytes 688136 | tf_op jit(solution)/shard_map/ppermute | solution.py:226
  23.3 2.8 %input_grad.1 = f32[2,2,2,8,64,128]{5,4,3,2,1,0:T(8,128)S(1)} custom-call(s32[3]{0:T(128)S(1)} %pad_add_fusion.place, bf16[2,8,64,128]{3,2,1,0:T(8,128)(2,1)S(1)} %bitcast.131, bf16[8,64,128]{2,1,0:T(8,128)(2,1)S(1)} %collective-permute-done.2.beside, bf16[8,64,128]{2,1,0:T(8,128)(2,1)S(1)} %collective-permute-done.3.across, bf16[27,64,256]{2,1,0:T(8,128)(2,1)S(1)} %copy-done), custom_call_target="tpu_custom_call" | custom-call | flops 1 | bytes 1 | tf_op jit(solution)/shard_map/input_grad/pallas_call | solution.py:201
  26.8 1.6 %collective-permute-start.8 = (f16[2,28,8,128]{3,2,1,0:T(8,128)(2,1)S(1)}, f16[2,28,8,128]{3,2,1,0:T(8,128)(2,1)S(1)}, u32[]{:S(2)}, u32[]{:S(2)}) collective-permute-start(f16[2,28,8,128]{3,2,1,0:T(8,128)(2,1)S(1)} %multiply_convert_fusion.3), channel_id=1, source_target_pairs={{0,8},{4,12},{8,0},{12,4},{16,24},{20,28},{24,16},{28,20},{1,9},{5... | collective-permute-start | bytes 344072 | tf_op jit(solution)/shard_map/ppermute | solution.py:226
  29.9 1.4 %collective-permute-start.7 = (f16[2,28,8,128]{3,2,1,0:T(8,128)(2,1)S(1)}, f16[2,28,8,128]{3,2,1,0:T(8,128)(2,1)S(1)}, u32[]{:S(2)}, u32[]{:S(2)}) collective-permute-start(f16[2,28,8,128]{3,2,1,0:T(8,128)(2,1)S(1)} %multiply_convert_fusion.2), channel_id=1, source_target_pairs={{0,4},{4,0},{8,12},{12,8},{16,20},{20,16},{24,28},{28,24},{1,5},{5... | collective-permute-start | bytes 344072 | tf_op jit(solution)/shard_map/ppermute | solution.py:226
  32.7 2.3 %collective-permute-start.11 = (f16[1,28,8,128]{3,2,1,0:T(8,128)(2,1)S(1)}, f16[1,28,8,128]{3,2,1,0:T(8,128)(2,1)S(1)}, u32[]{:S(2)}, u32[]{:S(2)}) collective-permute-start(f16[1,28,8,128]{3,2,1,0:T(8,128)(2,1)S(1)} %multiply_convert_fusion.7), channel_id=1, source_target_pairs={{0,16},{4,20},{8,24},{12,28},{16,0},{20,4},{24,8},{28,12},{1,17},{... | collective-permute-start | bytes 172040 | tf_op jit(solution)/shard_map/ppermute | solution.py:226
  35.3 2.4 %collective-permute-start.10 = (f16[1,28,8,128]{3,2,1,0:T(8,128)(2,1)S(1)}, f16[1,28,8,128]{3,2,1,0:T(8,128)(2,1)S(1)}, u32[]{:S(2)}, u32[]{:S(2)}) collective-permute-start(f16[1,28,8,128]{3,2,1,0:T(8,128)(2,1)S(1)} %multiply_convert_fusion.6), channel_id=1, source_target_pairs={{0,16},{4,20},{8,24},{12,28},{16,0},{20,4},{24,8},{28,12},{1,17},{... | collective-permute-start | bytes 172040 | tf_op jit(solution)/shard_map/ppermute | solution.py:226
  38.2 3.4 %output_map.1 = (f32[2,8,64,128]{3,2,1,0:T(8,128)S(1)}, f32[8,64,128]{2,1,0:T(8,128)S(1)}, f32[8,64,128]{2,1,0:T(8,128)S(1)}) custom-call(s32[3]{0:T(128)S(1)} %pad_add_fusion.place, bf16[2,8,64,128]{3,2,1,0:T(8,128)(2,1)S(1)} %bitcast.141, bf16[2,8,64,128]{3,2,1,0:T(8,128)(2,1)S(1)} %collective-permute-done.1.other, ...), custom_call_target="tpu_custom_call" | custom-call | flops 1 | bytes 1 | tf_op jit(solution)/shard_map/output_map/pallas_call | solution.py:150
  42.9 2.4 %collective-permute-start.16 = (f16[1,28,8,128]{3,2,1,0:T(8,128)(2,1)S(1)}, f16[1,28,8,128]{3,2,1,0:T(8,128)(2,1)S(1)}, u32[]{:S(2)}, u32[]{:S(2)}) collective-permute-start(f16[1,28,8,128]{3,2,1,0:T(8,128)(2,1)S(1)} %multiply_convert_fusion.4), channel_id=1, source_target_pairs={{0,16},{4,20},{8,24},{12,28},{16,0},{20,4},{24,8},{28,12},{1,17},{... | collective-permute-start | bytes 172040 | tf_op jit(solution)/shard_map/ppermute | solution.py:226
  45.2 1.5 %collective-permute-start.17 = (f32[8,64,128]{2,1,0:T(8,128)S(1)}, f32[8,64,128]{2,1,0:T(8,128)S(1)}, u32[]{:S(2)}, u32[]{:S(2)}) collective-permute-start(f32[8,64,128]{2,1,0:T(8,128)S(1)} %get-tuple-element.46), channel_id=1, source_target_pairs={{0,4},{4,0},{8,12},{12,8},{16,20},{20,16},{24,28},{28,24},{1,5},{5... | collective-permute-start | bytes 786440 | tf_op jit(solution)/shard_map/ppermute | solution.py:226
  47.4 2.1 %collective-permute-done.14 = f32[2,8,64,128]{3,1,2,0:T(8,128)S(1)} collective-permute-done((f32[2,8,64,128]{3,1,2,0:T(8,128)S(1)}, f32[2,8,64,128]{3,1,2,0:T(8,128)S(1)}, u32[]{:S(2)}, u32[]{:S(2)}) %collective-permute-start.14) | collective-permute-done | bytes 524320 | tf_op jit(solution)/shard_map/ppermute | solution.py:226
  50.6 1.8 %collective-permute-start.15 = (f16[2,28,8,128]{3,2,1,0:T(8,128)(2,1)S(1)}, f16[2,28,8,128]{3,2,1,0:T(8,128)(2,1)S(1)}, u32[]{:S(2)}, u32[]{:S(2)}) collective-permute-start(f16[2,28,8,128]{3,2,1,0:T(8,128)(2,1)S(1)} %pad_maximum_fusion.2), channel_id=1, source_target_pairs={{0,8},{4,12},{8,0},{12,4},{16,24},{20,28},{24,16},{28,20},{1,9},{5... | collective-permute-start | bytes 344072 | tf_op jit(solution)/shard_map/ppermute | solution.py:226
  52.4 1.4 %collective-permute-start.19 = (f16[2,28,8,128]{3,2,1,0:T(8,128)(2,1)S(1)}, f16[2,28,8,128]{3,2,1,0:T(8,128)(2,1)S(1)}, u32[]{:S(2)}, u32[]{:S(2)}) collective-permute-start(f16[2,28,8,128]{3,2,1,0:T(8,128)(2,1)S(1)} %pad_maximum_fusion.3), channel_id=1, source_target_pairs={{0,4},{4,0},{8,12},{12,8},{16,20},{20,16},{24,28},{28,24},{1,5},{5... | collective-permute-start | bytes 344072 | tf_op jit(solution)/shard_map/ppermute | solution.py:226
  53.8 2.8 %collective-permute-done.15 = f16[2,28,8,128]{3,2,1,0:T(8,128)(2,1)S(1)} collective-permute-done((f16[2,28,8,128]{3,2,1,0:T(8,128)(2,1)S(1)}, f16[2,28,8,128]{3,2,1,0:T(8,128)(2,1)S(1)}, u32[]{:S(2)}, u32[]{:S(2)}) %collective-permute-start.15) | collective-permute-done | bytes 114720 | tf_op jit(solution)/shard_map/ppermute | solution.py:226
  56.6 1.7 %collective-permute-start.18 = (f16[4,28,8,128]{3,2,1,0:T(8,128)(2,1)S(1)}, f16[4,28,8,128]{3,2,1,0:T(8,128)(2,1)S(1)}, u32[]{:S(2)}, u32[]{:S(2)}) collective-permute-start(f16[4,28,8,128]{3,2,1,0:T(8,128)(2,1)S(1)} %get-tuple-element.63), channel_id=1, source_target_pairs={{0,4},{4,0},{8,12},{12,8},{16,20},{20,16},{24,28},{28,24},{1,5},{5... | collective-permute-start | bytes 688136 | tf_op jit(solution)/shard_map/ppermute | solution.py:226
  58.3 2.4 %collective-permute-done.19 = f16[2,28,8,128]{3,2,1,0:T(8,128)(2,1)S(1)} collective-permute-done((f16[2,28,8,128]{3,2,1,0:T(8,128)(2,1)S(1)}, f16[2,28,8,128]{3,2,1,0:T(8,128)(2,1)S(1)}, u32[]{:S(2)}, u32[]{:S(2)}) %collective-permute-start.19) | collective-permute-done | bytes 114720 | tf_op jit(solution)/shard_map/ppermute | solution.py:226
  60.8 3.1 %collective-permute-start.20 = (f16[4,28,8,128]{3,2,1,0:T(8,128)(2,1)S(1)}, f16[4,28,8,128]{3,2,1,0:T(8,128)(2,1)S(1)}, u32[]{:S(2)}, u32[]{:S(2)}) collective-permute-start(f16[4,28,8,128]{3,2,1,0:T(8,128)(2,1)S(1)} %get-tuple-element.60), channel_id=1, source_target_pairs={{0,8},{4,12},{8,0},{12,4},{16,24},{20,28},{24,16},{28,20},{1,9},{5... | collective-permute-start | bytes 688136 | tf_op jit(solution)/shard_map/ppermute | solution.py:226
  65.0 3.0 %collective-permute-done.20 = f16[4,28,8,128]{3,2,1,0:T(8,128)(2,1)S(1)} collective-permute-done((f16[4,28,8,128]{3,2,1,0:T(8,128)(2,1)S(1)}, f16[4,28,8,128]{3,2,1,0:T(8,128)(2,1)S(1)}, u32[]{:S(2)}, u32[]{:S(2)}) %collective-permute-start.20) | collective-permute-done | bytes 229408 | tf_op jit(solution)/shard_map/ppermute | solution.py:226
  68.4 2.0 %assemble.1 = f32[27,64,256]{2,1,0:T(8,128)} custom-call(s32[3]{0:T(128)S(1)} %pad_add_fusion.place, f32[4,28,8,128]{3,2,1,0:T(8,128)S(1)} %get-tuple-element.66.refs_0_, f32[4,28,8,128]{3,2,1,0:T(8,128)S(1)} %get-tuple-element.67.refs_1_, f32[4,28,8,128]{3,2,1,0:T(8,128)S(1)} %get-tuple-element.65.refs_2_, f32[4,28,8,128]{3,2,1,0:T(8,128)S(1)} %get-tuple-element.64.refs_3_), custom_call_target="tpu_custom_call" | custom-call | flops 1 | bytes 1 | tf_op jit(solution)/shard_map/assemble/pallas_call | solution.py:286
  (86 shorter events, 12.5 us)
Async XLA Ops:
  1.6 10.0 %collective-permute-start.1 = (bf16[2,8,64,128]{3,2,1,0:T(8,128)(2,1)S(1)}, bf16[2,8,64,128]{3,2,1,0:T(8,128)(2,1)S(1)}, u32[]{:S(2)}, u32[]{:S(2)}) collective-permute-start(bf16[2,8,64,128]{3,2,1,0:T(8,128)(2,1)S(1)} %bitcast.138), channel_id=1, source_target_pairs={{0,1},{1,0},{2,3},{3,2},{4,5},{5,4},{6,7},{7,6},{8,9},{9,8},{10,11... | collective-permute-start | bytes 786440 | tf_op jit(solution)/shard_map/ppermute | solution.py:226
  2.1 9.5 %collective-permute-start = (bf16[2,8,64,128]{3,2,1,0:T(8,128)(2,1)S(1)}, bf16[2,8,64,128]{3,2,1,0:T(8,128)(2,1)S(1)}, u32[]{:S(2)}, u32[]{:S(2)}) collective-permute-start(bf16[2,8,64,128]{3,2,1,0:T(8,128)(2,1)S(1)} %bitcast.139), channel_id=1, source_target_pairs={{0,2},{1,3},{2,0},{3,1},{4,6},{5,7},{6,4},{7,5},{8,10},{9,11},{10,... | collective-permute-start | bytes 786440 | tf_op jit(solution)/shard_map/ppermute | solution.py:226
  5.8 5.6 %collective-permute-start.2 = (bf16[8,64,128]{2,1,0:T(8,128)(2,1)S(1)}, bf16[8,64,128]{2,1,0:T(8,128)(2,1)S(1)}, u32[]{:S(2)}, u32[]{:S(2)}) collective-permute-start(bf16[8,64,128]{2,1,0:T(8,128)(2,1)S(1)} %get-tuple-element.57), channel_id=1, source_target_pairs={{0,4},{4,0},{8,12},{12,8},{16,20},{20,16},{24,28},{28,24},{1,5},{5... | collective-permute-start | bytes 393224 | tf_op jit(solution)/shard_map/ppermute | solution.py:226
  7.3 4.1 %collective-permute-start.3 = (bf16[8,64,128]{2,1,0:T(8,128)(2,1)S(1)}, bf16[8,64,128]{2,1,0:T(8,128)(2,1)S(1)}, u32[]{:S(2)}, u32[]{:S(2)}) collective-permute-start(bf16[8,64,128]{2,1,0:T(8,128)(2,1)S(1)} %get-tuple-element.56), channel_id=1, source_target_pairs={{4,8},{12,16},{20,24},{8,4},{16,12},{24,20},{5,9},{13,17},{21,25},... | collective-permute-start | bytes 393224 | tf_op jit(solution)/shard_map/ppermute | solution.py:232
  11.6 7.2 %collective-permute-start.4 = (bf16[2,8,64,128]{3,2,1,0:T(8,128)(2,1)S(1)}, bf16[2,8,64,128]{3,2,1,0:T(8,128)(2,1)S(1)}, u32[]{:S(2)}, u32[]{:S(2)}) collective-permute-start(bf16[2,8,64,128]{3,2,1,0:T(8,128)(2,1)S(1)} %collective-permute-done.own.far_own), channel_id=1, source_target_pairs={{0,1},{1,0},{2,3},{3,2},{4,5},{5,4},{6,7},{7,6},{8,9},{9,8},{10,11... | collective-permute-start | bytes 786440 | tf_op jit(solution)/shard_map/ppermute | solution.py:226
  14.3 9.0 %copy-start = (bf16[27,64,256]{2,1,0:T(8,128)(2,1)S(1)}, bf16[27,64,256]{2,1,0:T(8,128)(2,1)}, u32[]{:S(2)}) copy-start(bf16[27,64,256]{2,1,0:T(8,128)(2,1)} %taps.3) | copy-start | bytes 2654212
  14.5 11.9 %collective-permute-start.6 = (f16[4,28,8,128]{3,2,1,0:T(8,128)(2,1)S(1)}, f16[4,28,8,128]{3,2,1,0:T(8,128)(2,1)S(1)}, u32[]{:S(2)}, u32[]{:S(2)}) collective-permute-start(f16[4,28,8,128]{3,2,1,0:T(8,128)(2,1)S(1)} %multiply_convert_fusion.1), channel_id=1, source_target_pairs={{0,4},{4,0},{8,12},{12,8},{16,20},{20,16},{24,28},{28,24},{1,5},{5... | collective-permute-start | bytes 688136 | tf_op jit(solution)/shard_map/ppermute | solution.py:226
  21.7 7.8 %collective-permute-start.5 = (f16[4,28,8,128]{3,2,1,0:T(8,128)(2,1)S(1)}, f16[4,28,8,128]{3,2,1,0:T(8,128)(2,1)S(1)}, u32[]{:S(2)}, u32[]{:S(2)}) collective-permute-start(f16[4,28,8,128]{3,2,1,0:T(8,128)(2,1)S(1)} %multiply_convert_fusion), channel_id=1, source_target_pairs={{0,8},{4,12},{8,0},{12,4},{16,24},{20,28},{24,16},{28,20},{1,9},{5... | collective-permute-start | bytes 688136 | tf_op jit(solution)/shard_map/ppermute | solution.py:226
  26.3 5.0 %collective-permute-start.9 = (f32[2,2,8,64,128]{4,3,2,1,0:T(8,128)S(1)}, f32[2,2,8,64,128]{4,3,2,1,0:T(8,128)S(1)}, u32[]{:S(2)}, u32[]{:S(2)}) collective-permute-start(f32[2,2,8,64,128]{4,3,2,1,0:T(8,128)S(1)} %dynamic-slice_bitcast_fusion), channel_id=1, source_target_pairs={{0,1},{1,0},{2,3},{3,2},{4,5},{5,4},{6,7},{7,6},{8,9},{9,8},{10,11... | collective-permute-start | bytes 3145736 | tf_op jit(solution)/shard_map/ppermute | solution.py:226
  26.8 5.6 %collective-permute-start.8 = (f16[2,28,8,128]{3,2,1,0:T(8,128)(2,1)S(1)}, f16[2,28,8,128]{3,2,1,0:T(8,128)(2,1)S(1)}, u32[]{:S(2)}, u32[]{:S(2)}) collective-permute-start(f16[2,28,8,128]{3,2,1,0:T(8,128)(2,1)S(1)} %multiply_convert_fusion.3), channel_id=1, source_target_pairs={{0,8},{4,12},{8,0},{12,4},{16,24},{20,28},{24,16},{28,20},{1,9},{5... | collective-permute-start | bytes 344072 | tf_op jit(solution)/shard_map/ppermute | solution.py:226
  29.9 5.1 %collective-permute-start.7 = (f16[2,28,8,128]{3,2,1,0:T(8,128)(2,1)S(1)}, f16[2,28,8,128]{3,2,1,0:T(8,128)(2,1)S(1)}, u32[]{:S(2)}, u32[]{:S(2)}) collective-permute-start(f16[2,28,8,128]{3,2,1,0:T(8,128)(2,1)S(1)} %multiply_convert_fusion.2), channel_id=1, source_target_pairs={{0,4},{4,0},{8,12},{12,8},{16,20},{20,16},{24,28},{28,24},{1,5},{5... | collective-permute-start | bytes 344072 | tf_op jit(solution)/shard_map/ppermute | solution.py:226
  32.7 9.0 %collective-permute-start.11 = (f16[1,28,8,128]{3,2,1,0:T(8,128)(2,1)S(1)}, f16[1,28,8,128]{3,2,1,0:T(8,128)(2,1)S(1)}, u32[]{:S(2)}, u32[]{:S(2)}) collective-permute-start(f16[1,28,8,128]{3,2,1,0:T(8,128)(2,1)S(1)} %multiply_convert_fusion.7), channel_id=1, source_target_pairs={{0,16},{4,20},{8,24},{12,28},{16,0},{20,4},{24,8},{28,12},{1,17},{... | collective-permute-start | bytes 172040 | tf_op jit(solution)/shard_map/ppermute | solution.py:226
  35.3 7.3 %collective-permute-start.10 = (f16[1,28,8,128]{3,2,1,0:T(8,128)(2,1)S(1)}, f16[1,28,8,128]{3,2,1,0:T(8,128)(2,1)S(1)}, u32[]{:S(2)}, u32[]{:S(2)}) collective-permute-start(f16[1,28,8,128]{3,2,1,0:T(8,128)(2,1)S(1)} %multiply_convert_fusion.6), channel_id=1, source_target_pairs={{0,16},{4,20},{8,24},{12,28},{16,0},{20,4},{24,8},{28,12},{1,17},{... | collective-permute-start | bytes 172040 | tf_op jit(solution)/shard_map/ppermute | solution.py:226
  37.7 11.8 %collective-permute-start.14 = (f32[2,8,64,128]{3,1,2,0:T(8,128)S(1)}, f32[2,8,64,128]{3,1,2,0:T(8,128)S(1)}, u32[]{:S(2)}, u32[]{:S(2)}) collective-permute-start(f32[2,8,64,128]{3,1,2,0:T(8,128)S(1)} %bitcast.148), channel_id=1, source_target_pairs={{0,2},{1,3},{2,0},{3,1},{4,6},{5,7},{6,4},{7,5},{8,10},{9,11},{10,... | collective-permute-start | bytes 1572872 | tf_op jit(solution)/shard_map/ppermute | solution.py:226
  41.9 8.6 %collective-permute-start.13 = (f16[1,28,8,128]{3,2,1,0:T(8,128)(2,1)S(1)}, f16[1,28,8,128]{3,2,1,0:T(8,128)(2,1)S(1)}, u32[]{:S(2)}, u32[]{:S(2)}) collective-permute-start(f16[1,28,8,128]{3,2,1,0:T(8,128)(2,1)S(1)} %multiply_convert_fusion.5), channel_id=1, source_target_pairs={{0,16},{4,20},{8,24},{12,28},{16,0},{20,4},{24,8},{28,12},{1,17},{... | collective-permute-start | bytes 172040 | tf_op jit(solution)/shard_map/ppermute | solution.py:226
  42.9 9.4 %collective-permute-start.16 = (f16[1,28,8,128]{3,2,1,0:T(8,128)(2,1)S(1)}, f16[1,28,8,128]{3,2,1,0:T(8,128)(2,1)S(1)}, u32[]{:S(2)}, u32[]{:S(2)}) collective-permute-start(f16[1,28,8,128]{3,2,1,0:T(8,128)(2,1)S(1)} %multiply_convert_fusion.4), channel_id=1, source_target_pairs={{0,16},{4,20},{8,24},{12,28},{16,0},{20,4},{24,8},{28,12},{1,17},{... | collective-permute-start | bytes 172040 | tf_op jit(solution)/shard_map/ppermute | solution.py:226
  45.2 18.7 %collective-permute-start.17 = (f32[8,64,128]{2,1,0:T(8,128)S(1)}, f32[8,64,128]{2,1,0:T(8,128)S(1)}, u32[]{:S(2)}, u32[]{:S(2)}) collective-permute-start(f32[8,64,128]{2,1,0:T(8,128)S(1)} %get-tuple-element.46), channel_id=1, source_target_pairs={{0,4},{4,0},{8,12},{12,8},{16,20},{20,16},{24,28},{28,24},{1,5},{5... | collective-permute-start | bytes 786440 | tf_op jit(solution)/shard_map/ppermute | solution.py:226
  46.7 17.2 %collective-permute-start.12 = (f32[8,64,128]{2,1,0:T(8,128)S(1)}, f32[8,64,128]{2,1,0:T(8,128)S(1)}, u32[]{:S(2)}, u32[]{:S(2)}) collective-permute-start(f32[8,64,128]{2,1,0:T(8,128)S(1)} %get-tuple-element.39), channel_id=1, source_target_pairs={{4,8},{12,16},{20,24},{8,4},{16,12},{24,20},{5,9},{13,17},{21,25},... | collective-permute-start | bytes 786440 | tf_op jit(solution)/shard_map/ppermute | solution.py:232
  50.6 6.0 %collective-permute-start.15 = (f16[2,28,8,128]{3,2,1,0:T(8,128)(2,1)S(1)}, f16[2,28,8,128]{3,2,1,0:T(8,128)(2,1)S(1)}, u32[]{:S(2)}, u32[]{:S(2)}) collective-permute-start(f16[2,28,8,128]{3,2,1,0:T(8,128)(2,1)S(1)} %pad_maximum_fusion.2), channel_id=1, source_target_pairs={{0,8},{4,12},{8,0},{12,4},{16,24},{20,28},{24,16},{28,20},{1,9},{5... | collective-permute-start | bytes 344072 | tf_op jit(solution)/shard_map/ppermute | solution.py:226
  52.4 8.4 %collective-permute-start.19 = (f16[2,28,8,128]{3,2,1,0:T(8,128)(2,1)S(1)}, f16[2,28,8,128]{3,2,1,0:T(8,128)(2,1)S(1)}, u32[]{:S(2)}, u32[]{:S(2)}) collective-permute-start(f16[2,28,8,128]{3,2,1,0:T(8,128)(2,1)S(1)} %pad_maximum_fusion.3), channel_id=1, source_target_pairs={{0,4},{4,0},{8,12},{12,8},{16,20},{20,16},{24,28},{28,24},{1,5},{5... | collective-permute-start | bytes 344072 | tf_op jit(solution)/shard_map/ppermute | solution.py:226
  56.6 11.4 %collective-permute-start.18 = (f16[4,28,8,128]{3,2,1,0:T(8,128)(2,1)S(1)}, f16[4,28,8,128]{3,2,1,0:T(8,128)(2,1)S(1)}, u32[]{:S(2)}, u32[]{:S(2)}) collective-permute-start(f16[4,28,8,128]{3,2,1,0:T(8,128)(2,1)S(1)} %get-tuple-element.63), channel_id=1, source_target_pairs={{0,4},{4,0},{8,12},{12,8},{16,20},{20,16},{24,28},{28,24},{1,5},{5... | collective-permute-start | bytes 688136 | tf_op jit(solution)/shard_map/ppermute | solution.py:226
  60.8 7.1 %collective-permute-start.20 = (f16[4,28,8,128]{3,2,1,0:T(8,128)(2,1)S(1)}, f16[4,28,8,128]{3,2,1,0:T(8,128)(2,1)S(1)}, u32[]{:S(2)}, u32[]{:S(2)}) collective-permute-start(f16[4,28,8,128]{3,2,1,0:T(8,128)(2,1)S(1)} %get-tuple-element.60), channel_id=1, source_target_pairs={{0,8},{4,12},{8,0},{12,4},{16,24},{20,28},{24,16},{28,20},{1,9},{5... | collective-permute-start | bytes 688136 | tf_op jit(solution)/shard_map/ppermute | solution.py:226

commit v4 on v3

--- a/solution.py
+++ b/solution.py
@@ -347,8 +347,10 @@
         if turn == 5:
             inner, beside, across = output_part(place, after(own, last), other, far_own, far_other, kernel)
             due.setdefault(turn + 1, []).append(inner)
+        if turn == 8:
+            beside = swap(after(beside, last), "space", 0)
         if turn == 7:
-            beside, across = swap(after(beside, last), "space", 0), across_swap(after(across, last))
+            across = across_swap(after(across, last))
         if turn == 7:
             total = kept + after(received_terms, last)
             input_grad = jnp.transpose(total.astype(jnp.bfloat16), (0, 2, 1, 3))

time: 70.6 us -> 68.5 us (0.970)
  starting transfers between devices: 32.8 us -> 28.9 us
  waiting for transfers between devices: 15.4 us -> 17.2 us
    ppermute x19, starting transfers between devices: 31.5 us -> 27.6 us  [swap(): return lax.ppermute(value, axis, [(i, i ^ 1 << bit) for i in range(count)])]
    ppermute x19, waiting for transfers between devices: 15.4 us -> 17.2 us  [swap(): return lax.ppermute(value, axis, [(i, i ^ 1 << bit) for i in range(count)])]
  transfers between devices with their start and end apart: 21 -> 21, of which waited for: 8 -> 10; matrix products, arithmetic and copies ran while one was open for 9% -> 9% of each run, Pallas kernels for 16% -> 17%
where the time goes in v4:
time: 68.5 us; the launch traced here: 68.3 us
  starting transfers between devices  28.9 us (42%)
  waiting for transfers between devices  17.2 us (25%)
  Pallas kernels  13.5 us (20%)
  other arithmetic  3.97 us (6%)
  local copies, waits for them, and re-layouts  3.55 us (5%)
  between operations  1.14 us (2%)
    ppermute x19, starting transfers between devices, swap(): return lax.ppermute(value, axis, [(i, i ^ 1 << bit) for i in range(count)])  27.6 us
    ppermute x19, waiting for transfers between devices, swap(): return lax.ppermute(value, axis, [(i, i ^ 1 << bit) for i in range(count)])  17.2 us
    pallas_call x2, Pallas kernels, kernel_grad_part(): pl.pallas_call(functools.partial(kernel_grad_kernel, scale, order), out_s...  5.22 us
    pallas_call x1, Pallas kernels, output_part(): pl.pallas_call(output_kernel, out_shape=[jax.ShapeDtypeStruct((depth, hei...  3.44 us
    unnamed x5, local copies, waits for them, and re-layouts  2.87 us
    pallas_call x1, Pallas kernels, input_grad_part(): pl.pallas_call(input_grad_kernel, out_shape=jax.ShapeDtypeStruct((2, 2, d...  2.83 us
    pallas_call x1, Pallas kernels, assembled(): pl.pallas_call(functools.partial(assemble_kernel, flips), out_shape=jax.S...  2.02 us
  transfers between devices with their start and end apart: 21, of which 10 were waited for; matrix products, arithmetic and copies ran while one was open for 9% of the time, Pallas kernels for 17%

profile of v4, /device:TPU:0, one launch (start us, length us, event | category | flops | bytes accessed | tf_op | source)
XLA Modules:
  0.0 68.3 jit_solution(4621477725109751860)
XLA Ops:
  2.1 2.6 %collective-permute-start = (bf16[2,8,64,128]{3,2,1,0:T(8,128)(2,1)S(1)}, bf16[2,8,64,128]{3,2,1,0:T(8,128)(2,1)S(1)}, u32[]{:S(2)}, u32[]{:S(2)}) collective-permute-start(bf16[2,8,64,128]{3,2,1,0:T(8,128)(2,1)S(1)} %bitcast.139), channel_id=1, source_target_pairs={{0,2},{1,3},{2,0},{3,1},{4,6},{5,7},{6,4},{7,5},{8,10},{9,11},{10,... | collective-permute-start | bytes 786440 | tf_op jit(solution)/shard_map/ppermute | solution.py:226
  5.8 1.6 %collective-permute-start.2 = (bf16[8,64,128]{2,1,0:T(8,128)(2,1)S(1)}, bf16[8,64,128]{2,1,0:T(8,128)(2,1)S(1)}, u32[]{:S(2)}, u32[]{:S(2)}) collective-permute-start(bf16[8,64,128]{2,1,0:T(8,128)(2,1)S(1)} %get-tuple-element.57), channel_id=1, source_target_pairs={{0,4},{4,0},{8,12},{12,8},{16,20},{20,16},{24,28},{28,24},{1,5},{5... | collective-permute-start | bytes 393224 | tf_op jit(solution)/shard_map/ppermute | solution.py:226
  8.1 3.3 %collective-permute-done.2.beside = bf16[8,64,128]{2,1,0:T(8,128)(2,1)S(1)} collective-permute-done((bf16[8,64,128]{2,1,0:T(8,128)(2,1)S(1)}, bf16[8,64,128]{2,1,0:T(8,128)(2,1)S(1)}, u32[]{:S(2)}, u32[]{:S(2)}) %collective-permute-start.2) | collective-permute-done | bytes 131104 | tf_op jit(solution)/shard_map/ppermute | solution.py:226
  11.6 2.6 %kernel_grad.2 = f32[8,28,8,128]{3,2,1,0:T(8,128)S(1)} custom-call(s32[3]{0:T(128)S(1)} %pad_add_fusion.place, bf16[2,8,64,128]{3,2,1,0:T(8,128)(2,1)S(1)} %bitcast.140, bf16[2,8,64,128]{3,2,1,0:T(8,128)(2,1)S(1)} %collective-permute-done.1.other, bf16[2,8,64,128]{3,2,1,0:T(8,128)(2,1)S(1)} %bitcast.129, ...), custom_call_target="tpu_custom_call" | custom-call | flops 1 | bytes 1 | tf_op jit(solution)/shard_map/kernel_grad/pallas_call | solution.py:93
  14.5 4.4 %collective-permute-start.6 = (f16[4,28,8,128]{3,2,1,0:T(8,128)(2,1)S(1)}, f16[4,28,8,128]{3,2,1,0:T(8,128)(2,1)S(1)}, u32[]{:S(2)}, u32[]{:S(2)}) collective-permute-start(f16[4,28,8,128]{3,2,1,0:T(8,128)(2,1)S(1)} %multiply_convert_fusion.1), channel_id=1, source_target_pairs={{0,4},{4,0},{8,12},{12,8},{16,20},{20,16},{24,28},{28,24},{1,5},{5... | collective-permute-start | bytes 688136 | tf_op jit(solution)/shard_map/ppermute | solution.py:226
  18.9 2.6 %kernel_grad.3 = f32[8,28,8,128]{3,2,1,0:T(8,128)S(1)} custom-call(s32[3]{0:T(128)S(1)} %pad_add_fusion.place, bf16[2,8,64,128]{3,2,1,0:T(8,128)(2,1)S(1)} %collective-permute-done.own.far_own, bf16[2,8,64,128]{3,2,1,0:T(8,128)(2,1)S(1)} %collective-permute-done.4.other.far_other, bf16[2,8,64,128]{3,2,1,0:T(8,128)(2,1)S(1)} %bitcast.130, ...), custom_call_target="tpu_custom_call" | custom-call | flops 1 | bytes 1 | tf_op jit(solution)/shard_map/kernel_grad/pallas_call | solution.py:93
  21.7 1.6 %collective-permute-start.5 = (f16[4,28,8,128]{3,2,1,0:T(8,128)(2,1)S(1)}, f16[4,28,8,128]{3,2,1,0:T(8,128)(2,1)S(1)}, u32[]{:S(2)}, u32[]{:S(2)}) collective-permute-start(f16[4,28,8,128]{3,2,1,0:T(8,128)(2,1)S(1)} %multiply_convert_fusion), channel_id=1, source_target_pairs={{0,8},{4,12},{8,0},{12,4},{16,24},{20,28},{24,16},{28,20},{1,9},{5... | collective-permute-start | bytes 688136 | tf_op jit(solution)/shard_map/ppermute | solution.py:226
  23.3 2.8 %input_grad.1 = f32[2,2,2,8,64,128]{5,4,3,2,1,0:T(8,128)S(1)} custom-call(s32[3]{0:T(128)S(1)} %pad_add_fusion.place, bf16[2,8,64,128]{3,2,1,0:T(8,128)(2,1)S(1)} %bitcast.131, bf16[8,64,128]{2,1,0:T(8,128)(2,1)S(1)} %collective-permute-done.2.beside, bf16[8,64,128]{2,1,0:T(8,128)(2,1)S(1)} %collective-permute-done.3.across, bf16[27,64,256]{2,1,0:T(8,128)(2,1)S(1)} %copy-done), custom_call_target="tpu_custom_call" | custom-call | flops 1 | bytes 1 | tf_op jit(solution)/shard_map/input_grad/pallas_call | solution.py:201
  26.8 1.6 %collective-permute-start.8 = (f16[2,28,8,128]{3,2,1,0:T(8,128)(2,1)S(1)}, f16[2,28,8,128]{3,2,1,0:T(8,128)(2,1)S(1)}, u32[]{:S(2)}, u32[]{:S(2)}) collective-permute-start(f16[2,28,8,128]{3,2,1,0:T(8,128)(2,1)S(1)} %multiply_convert_fusion.3), channel_id=1, source_target_pairs={{0,8},{4,12},{8,0},{12,4},{16,24},{20,28},{24,16},{28,20},{1,9},{5... | collective-permute-start | bytes 344072 | tf_op jit(solution)/shard_map/ppermute | solution.py:226
  28.4 1.1 %collective-permute-done.5 = f16[4,28,8,128]{3,2,1,0:T(8,128)(2,1)S(1)} collective-permute-done((f16[4,28,8,128]{3,2,1,0:T(8,128)(2,1)S(1)}, f16[4,28,8,128]{3,2,1,0:T(8,128)(2,1)S(1)}, u32[]{:S(2)}, u32[]{:S(2)}) %collective-permute-start.5) | collective-permute-done | bytes 229408 | tf_op jit(solution)/shard_map/ppermute | solution.py:226
  29.9 1.4 %collective-permute-start.7 = (f16[2,28,8,128]{3,2,1,0:T(8,128)(2,1)S(1)}, f16[2,28,8,128]{3,2,1,0:T(8,128)(2,1)S(1)}, u32[]{:S(2)}, u32[]{:S(2)}) collective-permute-start(f16[2,28,8,128]{3,2,1,0:T(8,128)(2,1)S(1)} %multiply_convert_fusion.2), channel_id=1, source_target_pairs={{0,4},{4,0},{8,12},{12,8},{16,20},{20,16},{24,28},{28,24},{1,5},{5... | collective-permute-start | bytes 344072 | tf_op jit(solution)/shard_map/ppermute | solution.py:226
  32.7 2.3 %collective-permute-start.11 = (f16[1,28,8,128]{3,2,1,0:T(8,128)(2,1)S(1)}, f16[1,28,8,128]{3,2,1,0:T(8,128)(2,1)S(1)}, u32[]{:S(2)}, u32[]{:S(2)}) collective-permute-start(f16[1,28,8,128]{3,2,1,0:T(8,128)(2,1)S(1)} %multiply_convert_fusion.7), channel_id=1, source_target_pairs={{0,16},{4,20},{8,24},{12,28},{16,0},{20,4},{24,8},{28,12},{1,17},{... | collective-permute-start | bytes 172040 | tf_op jit(solution)/shard_map/ppermute | solution.py:226
  35.3 2.4 %collective-permute-start.10 = (f16[1,28,8,128]{3,2,1,0:T(8,128)(2,1)S(1)}, f16[1,28,8,128]{3,2,1,0:T(8,128)(2,1)S(1)}, u32[]{:S(2)}, u32[]{:S(2)}) collective-permute-start(f16[1,28,8,128]{3,2,1,0:T(8,128)(2,1)S(1)} %multiply_convert_fusion.6), channel_id=1, source_target_pairs={{0,16},{4,20},{8,24},{12,28},{16,0},{20,4},{24,8},{28,12},{1,17},{... | collective-permute-start | bytes 172040 | tf_op jit(solution)/shard_map/ppermute | solution.py:226
  38.2 3.4 %output_map.1 = (f32[2,8,64,128]{3,2,1,0:T(8,128)S(1)}, f32[8,64,128]{2,1,0:T(8,128)S(1)}, f32[8,64,128]{2,1,0:T(8,128)S(1)}) custom-call(s32[3]{0:T(128)S(1)} %pad_add_fusion.place, bf16[2,8,64,128]{3,2,1,0:T(8,128)(2,1)S(1)} %bitcast.141, bf16[2,8,64,128]{3,2,1,0:T(8,128)(2,1)S(1)} %collective-permute-done.1.other, ...), custom_call_target="tpu_custom_call" | custom-call | flops 1 | bytes 1 | tf_op jit(solution)/shard_map/output_map/pallas_call | solution.py:150
  42.9 2.4 %collective-permute-start.16 = (f16[1,28,8,128]{3,2,1,0:T(8,128)(2,1)S(1)}, f16[1,28,8,128]{3,2,1,0:T(8,128)(2,1)S(1)}, u32[]{:S(2)}, u32[]{:S(2)}) collective-permute-start(f16[1,28,8,128]{3,2,1,0:T(8,128)(2,1)S(1)} %multiply_convert_fusion.4), channel_id=1, source_target_pairs={{0,16},{4,20},{8,24},{12,28},{16,0},{20,4},{24,8},{28,12},{1,17},{... | collective-permute-start | bytes 172040 | tf_op jit(solution)/shard_map/ppermute | solution.py:226
  45.9 3.6 %collective-permute-done.14 = f32[2,8,64,128]{3,1,2,0:T(8,128)S(1)} collective-permute-done((f32[2,8,64,128]{3,1,2,0:T(8,128)S(1)}, f32[2,8,64,128]{3,1,2,0:T(8,128)S(1)}, u32[]{:S(2)}, u32[]{:S(2)}) %collective-permute-start.14) | collective-permute-done | bytes 524320 | tf_op jit(solution)/shard_map/ppermute | solution.py:226
  49.5 1.0 %fusion.6 = bf16[2,64,8,128]{3,2,1,0:T(8,128)(2,1)} fusion(f32[2,8,64,128]{3,1,2,0:T(8,128)S(1)} %collective-permute-done.14, f32[1,2,8,64,128]{4,3,2,1,0:T(8,128)S(1)} %get-tuple-element.52), kind=kLoop, calls=%fused_computation.23 | loop fusion | flops 262144 | bytes 1310720 | tf_op jit(solution)/shard_map/transpose | solution.py:356
  50.6 1.8 %collective-permute-start.15 = (f16[2,28,8,128]{3,2,1,0:T(8,128)(2,1)S(1)}, f16[2,28,8,128]{3,2,1,0:T(8,128)(2,1)S(1)}, u32[]{:S(2)}, u32[]{:S(2)}) collective-permute-start(f16[2,28,8,128]{3,2,1,0:T(8,128)(2,1)S(1)} %pad_maximum_fusion.2), channel_id=1, source_target_pairs={{0,8},{4,12},{8,0},{12,4},{16,24},{20,28},{24,16},{28,20},{1,9},{5... | collective-permute-start | bytes 344072 | tf_op jit(solution)/shard_map/ppermute | solution.py:226
  52.4 1.4 %collective-permute-start.19 = (f16[2,28,8,128]{3,2,1,0:T(8,128)(2,1)S(1)}, f16[2,28,8,128]{3,2,1,0:T(8,128)(2,1)S(1)}, u32[]{:S(2)}, u32[]{:S(2)}) collective-permute-start(f16[2,28,8,128]{3,2,1,0:T(8,128)(2,1)S(1)} %pad_maximum_fusion.3), channel_id=1, source_target_pairs={{0,4},{4,0},{8,12},{12,8},{16,20},{20,16},{24,28},{28,24},{1,5},{5... | collective-permute-start | bytes 344072 | tf_op jit(solution)/shard_map/ppermute | solution.py:226
  54.4 1.8 %collective-permute-done.15 = f16[2,28,8,128]{3,2,1,0:T(8,128)(2,1)S(1)} collective-permute-done((f16[2,28,8,128]{3,2,1,0:T(8,128)(2,1)S(1)}, f16[2,28,8,128]{3,2,1,0:T(8,128)(2,1)S(1)}, u32[]{:S(2)}, u32[]{:S(2)}) %collective-permute-start.15) | collective-permute-done | bytes 114720 | tf_op jit(solution)/shard_map/ppermute | solution.py:226
  57.0 1.5 %collective-permute-done.19 = f16[2,28,8,128]{3,2,1,0:T(8,128)(2,1)S(1)} collective-permute-done((f16[2,28,8,128]{3,2,1,0:T(8,128)(2,1)S(1)}, f16[2,28,8,128]{3,2,1,0:T(8,128)(2,1)S(1)}, u32[]{:S(2)}, u32[]{:S(2)}) %collective-permute-start.19) | collective-permute-done | bytes 114720 | tf_op jit(solution)/shard_map/ppermute | solution.py:226
  59.6 3.4 %collective-permute-done.17 = f32[8,64,128]{2,1,0:T(8,128)S(1)} collective-permute-done((f32[8,64,128]{2,1,0:T(8,128)S(1)}, f32[8,64,128]{2,1,0:T(8,128)S(1)}, u32[]{:S(2)}, u32[]{:S(2)}) %collective-permute-start.17) | collective-permute-done | bytes 262176 | tf_op jit(solution)/shard_map/ppermute | solution.py:226
  64.7 1.1 %collective-permute-done.18 = f16[4,28,8,128]{3,2,1,0:T(8,128)(2,1)S(1)} collective-permute-done((f16[4,28,8,128]{3,2,1,0:T(8,128)(2,1)S(1)}, f16[4,28,8,128]{3,2,1,0:T(8,128)(2,1)S(1)}, u32[]{:S(2)}, u32[]{:S(2)}) %collective-permute-start.18) | collective-permute-done | bytes 229408 | tf_op jit(solution)/shard_map/ppermute | solution.py:226
  66.2 2.0 %assemble.1 = f32[27,64,256]{2,1,0:T(8,128)} custom-call(s32[3]{0:T(128)S(1)} %pad_add_fusion.place, f32[4,28,8,128]{3,2,1,0:T(8,128)S(1)} %get-tuple-element.66.refs_0_, f32[4,28,8,128]{3,2,1,0:T(8,128)S(1)} %get-tuple-element.67.refs_1_, f32[4,28,8,128]{3,2,1,0:T(8,128)S(1)} %get-tuple-element.65.refs_2_, f32[4,28,8,128]{3,2,1,0:T(8,128)S(1)} %get-tuple-element.64.refs_3_), custom_call_target="tpu_custom_call" | custom-call | flops 1 | bytes 1 | tf_op jit(solution)/shard_map/assemble/pallas_call | solution.py:286
  (86 shorter events, 13.4 us)
Async XLA Ops:
  1.6 10.0 %collective-permute-start.1 = (bf16[2,8,64,128]{3,2,1,0:T(8,128)(2,1)S(1)}, bf16[2,8,64,128]{3,2,1,0:T(8,128)(2,1)S(1)}, u32[]{:S(2)}, u32[]{:S(2)}) collective-permute-start(bf16[2,8,64,128]{3,2,1,0:T(8,128)(2,1)S(1)} %bitcast.138), channel_id=1, source_target_pairs={{0,1},{1,0},{2,3},{3,2},{4,5},{5,4},{6,7},{7,6},{8,9},{9,8},{10,11... | collective-permute-start | bytes 786440 | tf_op jit(solution)/shard_map/ppermute | solution.py:226
  2.1 9.5 %collective-permute-start = (bf16[2,8,64,128]{3,2,1,0:T(8,128)(2,1)S(1)}, bf16[2,8,64,128]{3,2,1,0:T(8,128)(2,1)S(1)}, u32[]{:S(2)}, u32[]{:S(2)}) collective-permute-start(bf16[2,8,64,128]{3,2,1,0:T(8,128)(2,1)S(1)} %bitcast.139), channel_id=1, source_target_pairs={{0,2},{1,3},{2,0},{3,1},{4,6},{5,7},{6,4},{7,5},{8,10},{9,11},{10,... | collective-permute-start | bytes 786440 | tf_op jit(solution)/shard_map/ppermute | solution.py:226
  5.8 5.6 %collective-permute-start.2 = (bf16[8,64,128]{2,1,0:T(8,128)(2,1)S(1)}, bf16[8,64,128]{2,1,0:T(8,128)(2,1)S(1)}, u32[]{:S(2)}, u32[]{:S(2)}) collective-permute-start(bf16[8,64,128]{2,1,0:T(8,128)(2,1)S(1)} %get-tuple-element.57), channel_id=1, source_target_pairs={{0,4},{4,0},{8,12},{12,8},{16,20},{20,16},{24,28},{28,24},{1,5},{5... | collective-permute-start | bytes 393224 | tf_op jit(solution)/shard_map/ppermute | solution.py:226
  7.3 4.1 %collective-permute-start.3 = (bf16[8,64,128]{2,1,0:T(8,128)(2,1)S(1)}, bf16[8,64,128]{2,1,0:T(8,128)(2,1)S(1)}, u32[]{:S(2)}, u32[]{:S(2)}) collective-permute-start(bf16[8,64,128]{2,1,0:T(8,128)(2,1)S(1)} %get-tuple-element.56), channel_id=1, source_target_pairs={{4,8},{12,16},{20,24},{8,4},{16,12},{24,20},{5,9},{13,17},{21,25},... | collective-permute-start | bytes 393224 | tf_op jit(solution)/shard_map/ppermute | solution.py:232
  11.6 7.2 %collective-permute-start.4 = (bf16[2,8,64,128]{3,2,1,0:T(8,128)(2,1)S(1)}, bf16[2,8,64,128]{3,2,1,0:T(8,128)(2,1)S(1)}, u32[]{:S(2)}, u32[]{:S(2)}) collective-permute-start(bf16[2,8,64,128]{3,2,1,0:T(8,128)(2,1)S(1)} %collective-permute-done.own.far_own), channel_id=1, source_target_pairs={{0,1},{1,0},{2,3},{3,2},{4,5},{5,4},{6,7},{7,6},{8,9},{9,8},{10,11... | collective-permute-start | bytes 786440 | tf_op jit(solution)/shard_map/ppermute | solution.py:226
  14.3 9.0 %copy-start = (bf16[27,64,256]{2,1,0:T(8,128)(2,1)S(1)}, bf16[27,64,256]{2,1,0:T(8,128)(2,1)}, u32[]{:S(2)}) copy-start(bf16[27,64,256]{2,1,0:T(8,128)(2,1)} %taps.3) | copy-start | bytes 2654212
  14.5 11.9 %collective-permute-start.6 = (f16[4,28,8,128]{3,2,1,0:T(8,128)(2,1)S(1)}, f16[4,28,8,128]{3,2,1,0:T(8,128)(2,1)S(1)}, u32[]{:S(2)}, u32[]{:S(2)}) collective-permute-start(f16[4,28,8,128]{3,2,1,0:T(8,128)(2,1)S(1)} %multiply_convert_fusion.1), channel_id=1, source_target_pairs={{0,4},{4,0},{8,12},{12,8},{16,20},{20,16},{24,28},{28,24},{1,5},{5... | collective-permute-start | bytes 688136 | tf_op jit(solution)/shard_map/ppermute | solution.py:226
  21.7 7.8 %collective-permute-start.5 = (f16[4,28,8,128]{3,2,1,0:T(8,128)(2,1)S(1)}, f16[4,28,8,128]{3,2,1,0:T(8,128)(2,1)S(1)}, u32[]{:S(2)}, u32[]{:S(2)}) collective-permute-start(f16[4,28,8,128]{3,2,1,0:T(8,128)(2,1)S(1)} %multiply_convert_fusion), channel_id=1, source_target_pairs={{0,8},{4,12},{8,0},{12,4},{16,24},{20,28},{24,16},{28,20},{1,9},{5... | collective-permute-start | bytes 688136 | tf_op jit(solution)/shard_map/ppermute | solution.py:226
  26.3 5.0 %collective-permute-start.9 = (f32[2,2,8,64,128]{4,3,2,1,0:T(8,128)S(1)}, f32[2,2,8,64,128]{4,3,2,1,0:T(8,128)S(1)}, u32[]{:S(2)}, u32[]{:S(2)}) collective-permute-start(f32[2,2,8,64,128]{4,3,2,1,0:T(8,128)S(1)} %dynamic-slice_bitcast_fusion), channel_id=1, source_target_pairs={{0,1},{1,0},{2,3},{3,2},{4,5},{5,4},{6,7},{7,6},{8,9},{9,8},{10,11... | collective-permute-start | bytes 3145736 | tf_op jit(solution)/shard_map/ppermute | solution.py:226
  26.8 5.6 %collective-permute-start.8 = (f16[2,28,8,128]{3,2,1,0:T(8,128)(2,1)S(1)}, f16[2,28,8,128]{3,2,1,0:T(8,128)(2,1)S(1)}, u32[]{:S(2)}, u32[]{:S(2)}) collective-permute-start(f16[2,28,8,128]{3,2,1,0:T(8,128)(2,1)S(1)} %multiply_convert_fusion.3), channel_id=1, source_target_pairs={{0,8},{4,12},{8,0},{12,4},{16,24},{20,28},{24,16},{28,20},{1,9},{5... | collective-permute-start | bytes 344072 | tf_op jit(solution)/shard_map/ppermute | solution.py:226
  29.9 5.1 %collective-permute-start.7 = (f16[2,28,8,128]{3,2,1,0:T(8,128)(2,1)S(1)}, f16[2,28,8,128]{3,2,1,0:T(8,128)(2,1)S(1)}, u32[]{:S(2)}, u32[]{:S(2)}) collective-permute-start(f16[2,28,8,128]{3,2,1,0:T(8,128)(2,1)S(1)} %multiply_convert_fusion.2), channel_id=1, source_target_pairs={{0,4},{4,0},{8,12},{12,8},{16,20},{20,16},{24,28},{28,24},{1,5},{5... | collective-permute-start | bytes 344072 | tf_op jit(solution)/shard_map/ppermute | solution.py:226
  32.7 9.0 %collective-permute-start.11 = (f16[1,28,8,128]{3,2,1,0:T(8,128)(2,1)S(1)}, f16[1,28,8,128]{3,2,1,0:T(8,128)(2,1)S(1)}, u32[]{:S(2)}, u32[]{:S(2)}) collective-permute-start(f16[1,28,8,128]{3,2,1,0:T(8,128)(2,1)S(1)} %multiply_convert_fusion.7), channel_id=1, source_target_pairs={{0,16},{4,20},{8,24},{12,28},{16,0},{20,4},{24,8},{28,12},{1,17},{... | collective-permute-start | bytes 172040 | tf_op jit(solution)/shard_map/ppermute | solution.py:226
  35.3 7.3 %collective-permute-start.10 = (f16[1,28,8,128]{3,2,1,0:T(8,128)(2,1)S(1)}, f16[1,28,8,128]{3,2,1,0:T(8,128)(2,1)S(1)}, u32[]{:S(2)}, u32[]{:S(2)}) collective-permute-start(f16[1,28,8,128]{3,2,1,0:T(8,128)(2,1)S(1)} %multiply_convert_fusion.6), channel_id=1, source_target_pairs={{0,16},{4,20},{8,24},{12,28},{16,0},{20,4},{24,8},{28,12},{1,17},{... | collective-permute-start | bytes 172040 | tf_op jit(solution)/shard_map/ppermute | solution.py:226
  37.7 11.8 %collective-permute-start.14 = (f32[2,8,64,128]{3,1,2,0:T(8,128)S(1)}, f32[2,8,64,128]{3,1,2,0:T(8,128)S(1)}, u32[]{:S(2)}, u32[]{:S(2)}) collective-permute-start(f32[2,8,64,128]{3,1,2,0:T(8,128)S(1)} %bitcast.148), channel_id=1, source_target_pairs={{0,2},{1,3},{2,0},{3,1},{4,6},{5,7},{6,4},{7,5},{8,10},{9,11},{10,... | collective-permute-start | bytes 1572872 | tf_op jit(solution)/shard_map/ppermute | solution.py:226
  41.9 8.6 %collective-permute-start.13 = (f16[1,28,8,128]{3,2,1,0:T(8,128)(2,1)S(1)}, f16[1,28,8,128]{3,2,1,0:T(8,128)(2,1)S(1)}, u32[]{:S(2)}, u32[]{:S(2)}) collective-permute-start(f16[1,28,8,128]{3,2,1,0:T(8,128)(2,1)S(1)} %multiply_convert_fusion.5), channel_id=1, source_target_pairs={{0,16},{4,20},{8,24},{12,28},{16,0},{20,4},{24,8},{28,12},{1,17},{... | collective-permute-start | bytes 172040 | tf_op jit(solution)/shard_map/ppermute | solution.py:226
  42.9 9.4 %collective-permute-start.16 = (f16[1,28,8,128]{3,2,1,0:T(8,128)(2,1)S(1)}, f16[1,28,8,128]{3,2,1,0:T(8,128)(2,1)S(1)}, u32[]{:S(2)}, u32[]{:S(2)}) collective-permute-start(f16[1,28,8,128]{3,2,1,0:T(8,128)(2,1)S(1)} %multiply_convert_fusion.4), channel_id=1, source_target_pairs={{0,16},{4,20},{8,24},{12,28},{16,0},{20,4},{24,8},{28,12},{1,17},{... | collective-permute-start | bytes 172040 | tf_op jit(solution)/shard_map/ppermute | solution.py:226
  45.2 14.3 %collective-permute-start.12 = (f32[8,64,128]{2,1,0:T(8,128)S(1)}, f32[8,64,128]{2,1,0:T(8,128)S(1)}, u32[]{:S(2)}, u32[]{:S(2)}) collective-permute-start(f32[8,64,128]{2,1,0:T(8,128)S(1)} %get-tuple-element.39), channel_id=1, source_target_pairs={{4,8},{12,16},{20,24},{8,4},{16,12},{24,20},{5,9},{13,17},{21,25},... | collective-permute-start | bytes 786440 | tf_op jit(solution)/shard_map/ppermute | solution.py:232
  50.6 5.7 %collective-permute-start.15 = (f16[2,28,8,128]{3,2,1,0:T(8,128)(2,1)S(1)}, f16[2,28,8,128]{3,2,1,0:T(8,128)(2,1)S(1)}, u32[]{:S(2)}, u32[]{:S(2)}) collective-permute-start(f16[2,28,8,128]{3,2,1,0:T(8,128)(2,1)S(1)} %pad_maximum_fusion.2), channel_id=1, source_target_pairs={{0,8},{4,12},{8,0},{12,4},{16,24},{20,28},{24,16},{28,20},{1,9},{5... | collective-permute-start | bytes 344072 | tf_op jit(solution)/shard_map/ppermute | solution.py:226
  52.4 6.1 %collective-permute-start.19 = (f16[2,28,8,128]{3,2,1,0:T(8,128)(2,1)S(1)}, f16[2,28,8,128]{3,2,1,0:T(8,128)(2,1)S(1)}, u32[]{:S(2)}, u32[]{:S(2)}) collective-permute-start(f16[2,28,8,128]{3,2,1,0:T(8,128)(2,1)S(1)} %pad_maximum_fusion.3), channel_id=1, source_target_pairs={{0,4},{4,0},{8,12},{12,8},{16,20},{20,16},{24,28},{28,24},{1,5},{5... | collective-permute-start | bytes 344072 | tf_op jit(solution)/shard_map/ppermute | solution.py:226
  53.8 9.2 %collective-permute-start.17 = (f32[8,64,128]{2,1,0:T(8,128)S(1)}, f32[8,64,128]{2,1,0:T(8,128)S(1)}, u32[]{:S(2)}, u32[]{:S(2)}) collective-permute-start(f32[8,64,128]{2,1,0:T(8,128)S(1)} %get-tuple-element.46), channel_id=1, source_target_pairs={{0,4},{4,0},{8,12},{12,8},{16,20},{20,16},{24,28},{28,24},{1,5},{5... | collective-permute-start | bytes 786440 | tf_op jit(solution)/shard_map/ppermute | solution.py:226
  56.3 9.5 %collective-permute-start.18 = (f16[4,28,8,128]{3,2,1,0:T(8,128)(2,1)S(1)}, f16[4,28,8,128]{3,2,1,0:T(8,128)(2,1)S(1)}, u32[]{:S(2)}, u32[]{:S(2)}) collective-permute-start(f16[4,28,8,128]{3,2,1,0:T(8,128)(2,1)S(1)} %get-tuple-element.63), channel_id=1, source_target_pairs={{0,4},{4,0},{8,12},{12,8},{16,20},{20,16},{24,28},{28,24},{1,5},{5... | collective-permute-start | bytes 688136 | tf_op jit(solution)/shard_map/ppermute | solution.py:226
  58.6 6.1 %collective-permute-start.20 = (f16[4,28,8,128]{3,2,1,0:T(8,128)(2,1)S(1)}, f16[4,28,8,128]{3,2,1,0:T(8,128)(2,1)S(1)}, u32[]{:S(2)}, u32[]{:S(2)}) collective-permute-start(f16[4,28,8,128]{3,2,1,0:T(8,128)(2,1)S(1)} %get-tuple-element.60), channel_id=1, source_target_pairs={{0,8},{4,12},{8,0},{12,4},{16,24},{20,28},{24,16},{28,20},{1,9},{5... | collective-permute-start | bytes 688136 | tf_op jit(solution)/shard_map/ppermute | solution.py:226

commit v5 on v4

--- a/solution.py
+++ b/solution.py
@@ -346,12 +346,12 @@
             due.setdefault(turn + 1, []).append(away)
         if turn == 5:
             inner, beside, across = output_part(place, after(own, last), other, far_own, far_other, kernel)
-            due.setdefault(turn + 1, []).append(inner)
+            due.setdefault(turn + 2, []).append(inner)
         if turn == 8:
             beside = swap(after(beside, last), "space", 0)
         if turn == 7:
             across = across_swap(after(across, last))
-        if turn == 7:
+        if turn == 9:
             total = kept + after(received_terms, last)
             input_grad = jnp.transpose(total.astype(jnp.bfloat16), (0, 2, 1, 3))
             due.setdefault(turn + 1, []).append(input_grad)

time: 68.5 us -> 68.3 us (level)
  waiting for transfers between devices: 17.2 us -> 14.7 us
  starting transfers between devices: 28.9 us -> 31.3 us
    ppermute x19, waiting for transfers between devices: 17.2 us -> 14.7 us  [swap(): return lax.ppermute(value, axis, [(i, i ^ 1 << bit) for i in range(count)])]
    ppermute x19, starting transfers between devices: 27.6 us -> 30 us  [swap(): return lax.ppermute(value, axis, [(i, i ^ 1 << bit) for i in range(count)])]
  transfers between devices with their start and end apart: 21 -> 21, of which waited for: 10 -> 9; matrix products, arithmetic and copies ran while one was open for 9% -> 9% of each run, Pallas kernels for 17% -> 17%
where the time goes in v5:
time: 68.3 us; the launch traced here: 68.1 us
  starting transfers between devices  31.3 us (46%)
  waiting for transfers between devices  14.7 us (22%)
  Pallas kernels  13.5 us (20%)
  other arithmetic  3.97 us (6%)
  local copies, waits for them, and re-layouts  3.55 us (5%)
  between operations  1.15 us (2%)
    ppermute x19, starting transfers between devices, swap(): return lax.ppermute(value, axis, [(i, i ^ 1 << bit) for i in range(count)])  30 us
    ppermute x19, waiting for transfers between devices, swap(): return lax.ppermute(value, axis, [(i, i ^ 1 << bit) for i in range(count)])  14.7 us
    pallas_call x2, Pallas kernels, kernel_grad_part(): pl.pallas_call(functools.partial(kernel_grad_kernel, scale, order), out_s...  5.22 us
    pallas_call x1, Pallas kernels, output_part(): pl.pallas_call(output_kernel, out_shape=[jax.ShapeDtypeStruct((depth, hei...  3.44 us
    unnamed x5, local copies, waits for them, and re-layouts  2.87 us
    pallas_call x1, Pallas kernels, input_grad_part(): pl.pallas_call(input_grad_kernel, out_shape=jax.ShapeDtypeStruct((2, 2, d...  2.83 us
    pallas_call x1, Pallas kernels, assembled(): pl.pallas_call(functools.partial(assemble_kernel, flips), out_shape=jax.S...  2.02 us
  transfers between devices with their start and end apart: 21, of which 9 were waited for; matrix products, arithmetic and copies ran while one was open for 9% of the time, Pallas kernels for 17%

profile of v5, /device:TPU:0, one launch (start us, length us, event | category | flops | bytes accessed | tf_op | source)
XLA Modules:
  0.0 68.1 jit_solution(17162377856300602949)
XLA Ops:
  2.1 2.6 %collective-permute-start = (bf16[2,8,64,128]{3,2,1,0:T(8,128)(2,1)S(1)}, bf16[2,8,64,128]{3,2,1,0:T(8,128)(2,1)S(1)}, u32[]{:S(2)}, u32[]{:S(2)}) collective-permute-start(bf16[2,8,64,128]{3,2,1,0:T(8,128)(2,1)S(1)} %bitcast.139), channel_id=1, source_target_pairs={{0,2},{1,3},{2,0},{3,1},{4,6},{5,7},{6,4},{7,5},{8,10},{9,11},{10,... | collective-permute-start | bytes 786440 | tf_op jit(solution)/shard_map/ppermute | solution.py:226
  5.8 1.6 %collective-permute-start.2 = (bf16[8,64,128]{2,1,0:T(8,128)(2,1)S(1)}, bf16[8,64,128]{2,1,0:T(8,128)(2,1)S(1)}, u32[]{:S(2)}, u32[]{:S(2)}) collective-permute-start(bf16[8,64,128]{2,1,0:T(8,128)(2,1)S(1)} %get-tuple-element.57), channel_id=1, source_target_pairs={{0,4},{4,0},{8,12},{12,8},{16,20},{20,16},{24,28},{28,24},{1,5},{5... | collective-permute-start | bytes 393224 | tf_op jit(solution)/shard_map/ppermute | solution.py:226
  8.1 3.3 %collective-permute-done.2.beside = bf16[8,64,128]{2,1,0:T(8,128)(2,1)S(1)} collective-permute-done((bf16[8,64,128]{2,1,0:T(8,128)(2,1)S(1)}, bf16[8,64,128]{2,1,0:T(8,128)(2,1)S(1)}, u32[]{:S(2)}, u32[]{:S(2)}) %collective-permute-start.2) | collective-permute-done | bytes 131104 | tf_op jit(solution)/shard_map/ppermute | solution.py:226
  11.6 2.6 %kernel_grad.2 = f32[8,28,8,128]{3,2,1,0:T(8,128)S(1)} custom-call(s32[3]{0:T(128)S(1)} %pad_add_fusion.place, bf16[2,8,64,128]{3,2,1,0:T(8,128)(2,1)S(1)} %bitcast.140, bf16[2,8,64,128]{3,2,1,0:T(8,128)(2,1)S(1)} %collective-permute-done.1.other, bf16[2,8,64,128]{3,2,1,0:T(8,128)(2,1)S(1)} %bitcast.129, ...), custom_call_target="tpu_custom_call" | custom-call | flops 1 | bytes 1 | tf_op jit(solution)/shard_map/kernel_grad/pallas_call | solution.py:93
  14.5 4.4 %collective-permute-start.6 = (f16[4,28,8,128]{3,2,1,0:T(8,128)(2,1)S(1)}, f16[4,28,8,128]{3,2,1,0:T(8,128)(2,1)S(1)}, u32[]{:S(2)}, u32[]{:S(2)}) collective-permute-start(f16[4,28,8,128]{3,2,1,0:T(8,128)(2,1)S(1)} %multiply_convert_fusion.1), channel_id=1, source_target_pairs={{0,4},{4,0},{8,12},{12,8},{16,20},{20,16},{24,28},{28,24},{1,5},{5... | collective-permute-start | bytes 688136 | tf_op jit(solution)/shard_map/ppermute | solution.py:226
  18.9 2.6 %kernel_grad.3 = f32[8,28,8,128]{3,2,1,0:T(8,128)S(1)} custom-call(s32[3]{0:T(128)S(1)} %pad_add_fusion.place, bf16[2,8,64,128]{3,2,1,0:T(8,128)(2,1)S(1)} %collective-permute-done.own.far_own, bf16[2,8,64,128]{3,2,1,0:T(8,128)(2,1)S(1)} %collective-permute-done.4.other.far_other, bf16[2,8,64,128]{3,2,1,0:T(8,128)(2,1)S(1)} %bitcast.130, ...), custom_call_target="tpu_custom_call" | custom-call | flops 1 | bytes 1 | tf_op jit(solution)/shard_map/kernel_grad/pallas_call | solution.py:93
  21.7 1.6 %collective-permute-start.5 = (f16[4,28,8,128]{3,2,1,0:T(8,128)(2,1)S(1)}, f16[4,28,8,128]{3,2,1,0:T(8,128)(2,1)S(1)}, u32[]{:S(2)}, u32[]{:S(2)}) collective-permute-start(f16[4,28,8,128]{3,2,1,0:T(8,128)(2,1)S(1)} %multiply_convert_fusion), channel_id=1, source_target_pairs={{0,8},{4,12},{8,0},{12,4},{16,24},{20,28},{24,16},{28,20},{1,9},{5... | collective-permute-start | bytes 688136 | tf_op jit(solution)/shard_map/ppermute | solution.py:226
  23.3 2.8 %input_grad.1 = f32[2,2,2,8,64,128]{5,4,3,2,1,0:T(8,128)S(1)} custom-call(s32[3]{0:T(128)S(1)} %pad_add_fusion.place, bf16[2,8,64,128]{3,2,1,0:T(8,128)(2,1)S(1)} %bitcast.131, bf16[8,64,128]{2,1,0:T(8,128)(2,1)S(1)} %collective-permute-done.2.beside, bf16[8,64,128]{2,1,0:T(8,128)(2,1)S(1)} %collective-permute-done.3.across, bf16[27,64,256]{2,1,0:T(8,128)(2,1)S(1)} %copy-done), custom_call_target="tpu_custom_call" | custom-call | flops 1 | bytes 1 | tf_op jit(solution)/shard_map/input_grad/pallas_call | solution.py:201
  26.8 1.6 %collective-permute-start.8 = (f16[2,28,8,128]{3,2,1,0:T(8,128)(2,1)S(1)}, f16[2,28,8,128]{3,2,1,0:T(8,128)(2,1)S(1)}, u32[]{:S(2)}, u32[]{:S(2)}) collective-permute-start(f16[2,28,8,128]{3,2,1,0:T(8,128)(2,1)S(1)} %multiply_convert_fusion.3), channel_id=1, source_target_pairs={{0,8},{4,12},{8,0},{12,4},{16,24},{20,28},{24,16},{28,20},{1,9},{5... | collective-permute-start | bytes 344072 | tf_op jit(solution)/shard_map/ppermute | solution.py:226
  28.4 1.1 %collective-permute-done.5 = f16[4,28,8,128]{3,2,1,0:T(8,128)(2,1)S(1)} collective-permute-done((f16[4,28,8,128]{3,2,1,0:T(8,128)(2,1)S(1)}, f16[4,28,8,128]{3,2,1,0:T(8,128)(2,1)S(1)}, u32[]{:S(2)}, u32[]{:S(2)}) %collective-permute-start.5) | collective-permute-done | bytes 229408 | tf_op jit(solution)/shard_map/ppermute | solution.py:226
  29.9 1.4 %collective-permute-start.7 = (f16[2,28,8,128]{3,2,1,0:T(8,128)(2,1)S(1)}, f16[2,28,8,128]{3,2,1,0:T(8,128)(2,1)S(1)}, u32[]{:S(2)}, u32[]{:S(2)}) collective-permute-start(f16[2,28,8,128]{3,2,1,0:T(8,128)(2,1)S(1)} %multiply_convert_fusion.2), channel_id=1, source_target_pairs={{0,4},{4,0},{8,12},{12,8},{16,20},{20,16},{24,28},{28,24},{1,5},{5... | collective-permute-start | bytes 344072 | tf_op jit(solution)/shard_map/ppermute | solution.py:226
  32.7 2.3 %collective-permute-start.11 = (f16[1,28,8,128]{3,2,1,0:T(8,128)(2,1)S(1)}, f16[1,28,8,128]{3,2,1,0:T(8,128)(2,1)S(1)}, u32[]{:S(2)}, u32[]{:S(2)}) collective-permute-start(f16[1,28,8,128]{3,2,1,0:T(8,128)(2,1)S(1)} %multiply_convert_fusion.7), channel_id=1, source_target_pairs={{0,16},{4,20},{8,24},{12,28},{16,0},{20,4},{24,8},{28,12},{1,17},{... | collective-permute-start | bytes 172040 | tf_op jit(solution)/shard_map/ppermute | solution.py:226
  35.3 2.4 %collective-permute-start.10 = (f16[1,28,8,128]{3,2,1,0:T(8,128)(2,1)S(1)}, f16[1,28,8,128]{3,2,1,0:T(8,128)(2,1)S(1)}, u32[]{:S(2)}, u32[]{:S(2)}) collective-permute-start(f16[1,28,8,128]{3,2,1,0:T(8,128)(2,1)S(1)} %multiply_convert_fusion.6), channel_id=1, source_target_pairs={{0,16},{4,20},{8,24},{12,28},{16,0},{20,4},{24,8},{28,12},{1,17},{... | collective-permute-start | bytes 172040 | tf_op jit(solution)/shard_map/ppermute | solution.py:226
  38.2 3.4 %output_map.1 = (f32[2,8,64,128]{3,2,1,0:T(8,128)S(1)}, f32[8,64,128]{2,1,0:T(8,128)S(1)}, f32[8,64,128]{2,1,0:T(8,128)S(1)}) custom-call(s32[3]{0:T(128)S(1)} %pad_add_fusion.place, bf16[2,8,64,128]{3,2,1,0:T(8,128)(2,1)S(1)} %bitcast.141, bf16[2,8,64,128]{3,2,1,0:T(8,128)(2,1)S(1)} %collective-permute-done.1.other, ...), custom_call_target="tpu_custom_call" | custom-call | flops 1 | bytes 1 | tf_op jit(solution)/shard_map/output_map/pallas_call | solution.py:150
  42.9 2.4 %collective-permute-start.15 = (f16[1,28,8,128]{3,2,1,0:T(8,128)(2,1)S(1)}, f16[1,28,8,128]{3,2,1,0:T(8,128)(2,1)S(1)}, u32[]{:S(2)}, u32[]{:S(2)}) collective-permute-start(f16[1,28,8,128]{3,2,1,0:T(8,128)(2,1)S(1)} %multiply_convert_fusion.4), channel_id=1, source_target_pairs={{0,16},{4,20},{8,24},{12,28},{16,0},{20,4},{24,8},{28,12},{1,17},{... | collective-permute-start | bytes 172040 | tf_op jit(solution)/shard_map/ppermute | solution.py:226
  45.9 1.2 %collective-permute-done.13 = f16[1,28,8,128]{3,2,1,0:T(8,128)(2,1)S(1)} collective-permute-done((f16[1,28,8,128]{3,2,1,0:T(8,128)(2,1)S(1)}, f16[1,28,8,128]{3,2,1,0:T(8,128)(2,1)S(1)}, u32[]{:S(2)}, u32[]{:S(2)}) %collective-permute-start.13) | collective-permute-done | bytes 57376 | tf_op jit(solution)/shard_map/ppermute | solution.py:226
  47.1 3.1 %collective-permute-start.14 = (f16[2,28,8,128]{3,2,1,0:T(8,128)(2,1)S(1)}, f16[2,28,8,128]{3,2,1,0:T(8,128)(2,1)S(1)}, u32[]{:S(2)}, u32[]{:S(2)}) collective-permute-start(f16[2,28,8,128]{3,2,1,0:T(8,128)(2,1)S(1)} %pad_maximum_fusion.2), channel_id=1, source_target_pairs={{0,8},{4,12},{8,0},{12,4},{16,24},{20,28},{24,16},{28,20},{1,9},{5... | collective-permute-start | bytes 344072 | tf_op jit(solution)/shard_map/ppermute | solution.py:226
  51.0 1.3 %collective-permute-start.17 = (f32[8,64,128]{2,1,0:T(8,128)S(1)}, f32[8,64,128]{2,1,0:T(8,128)S(1)}, u32[]{:S(2)}, u32[]{:S(2)}) collective-permute-start(f32[8,64,128]{2,1,0:T(8,128)S(1)} %get-tuple-element.46), channel_id=1, source_target_pairs={{0,4},{4,0},{8,12},{12,8},{16,20},{20,16},{24,28},{28,24},{1,5},{5... | collective-permute-start | bytes 786440 | tf_op jit(solution)/shard_map/ppermute | solution.py:226
  52.3 1.0 %fusion.6 = bf16[2,64,8,128]{3,2,1,0:T(8,128)(2,1)} fusion(f32[2,8,64,128]{3,1,2,0:T(8,128)S(1)} %collective-permute-done.16, f32[1,2,8,64,128]{4,3,2,1,0:T(8,128)S(1)} %get-tuple-element.52), kind=kLoop, calls=%fused_computation.23 | loop fusion | flops 262144 | bytes 1310720 | tf_op jit(solution)/shard_map/transpose | solution.py:356
  53.4 2.9 %collective-permute-done.14 = f16[2,28,8,128]{3,2,1,0:T(8,128)(2,1)S(1)} collective-permute-done((f16[2,28,8,128]{3,2,1,0:T(8,128)(2,1)S(1)}, f16[2,28,8,128]{3,2,1,0:T(8,128)(2,1)S(1)}, u32[]{:S(2)}, u32[]{:S(2)}) %collective-permute-start.14) | collective-permute-done | bytes 114720 | tf_op jit(solution)/shard_map/ppermute | solution.py:226
  56.7 2.6 %collective-permute-start.20 = (f16[4,28,8,128]{3,2,1,0:T(8,128)(2,1)S(1)}, f16[4,28,8,128]{3,2,1,0:T(8,128)(2,1)S(1)}, u32[]{:S(2)}, u32[]{:S(2)}) collective-permute-start(f16[4,28,8,128]{3,2,1,0:T(8,128)(2,1)S(1)} %get-tuple-element.60), channel_id=1, source_target_pairs={{0,8},{4,12},{8,0},{12,4},{16,24},{20,28},{24,16},{28,20},{1,9},{5... | collective-permute-start | bytes 688136 | tf_op jit(solution)/shard_map/ppermute | solution.py:226
  59.2 3.0 %collective-permute-done.17 = f32[8,64,128]{2,1,0:T(8,128)S(1)} collective-permute-done((f32[8,64,128]{2,1,0:T(8,128)S(1)}, f32[8,64,128]{2,1,0:T(8,128)S(1)}, u32[]{:S(2)}, u32[]{:S(2)}) %collective-permute-start.17) | collective-permute-done | bytes 262176 | tf_op jit(solution)/shard_map/ppermute | solution.py:226
  63.3 2.4 %collective-permute-done.18 = f16[4,28,8,128]{3,2,1,0:T(8,128)(2,1)S(1)} collective-permute-done((f16[4,28,8,128]{3,2,1,0:T(8,128)(2,1)S(1)}, f16[4,28,8,128]{3,2,1,0:T(8,128)(2,1)S(1)}, u32[]{:S(2)}, u32[]{:S(2)}) %collective-permute-start.18) | collective-permute-done | bytes 229408 | tf_op jit(solution)/shard_map/ppermute | solution.py:226
  66.1 2.0 %assemble.1 = f32[27,64,256]{2,1,0:T(8,128)} custom-call(s32[3]{0:T(128)S(1)} %pad_add_fusion.place, f32[4,28,8,128]{3,2,1,0:T(8,128)S(1)} %get-tuple-element.66.refs_0_, f32[4,28,8,128]{3,2,1,0:T(8,128)S(1)} %get-tuple-element.67.refs_1_, f32[4,28,8,128]{3,2,1,0:T(8,128)S(1)} %get-tuple-element.65.refs_2_, f32[4,28,8,128]{3,2,1,0:T(8,128)S(1)} %get-tuple-element.64.refs_3_), custom_call_target="tpu_custom_call" | custom-call | flops 1 | bytes 1 | tf_op jit(solution)/shard_map/assemble/pallas_call | solution.py:286
  (86 shorter events, 11.4 us)
Async XLA Ops:
  1.6 10.0 %collective-permute-start.1 = (bf16[2,8,64,128]{3,2,1,0:T(8,128)(2,1)S(1)}, bf16[2,8,64,128]{3,2,1,0:T(8,128)(2,1)S(1)}, u32[]{:S(2)}, u32[]{:S(2)}) collective-permute-start(bf16[2,8,64,128]{3,2,1,0:T(8,128)(2,1)S(1)} %bitcast.138), channel_id=1, source_target_pairs={{0,1},{1,0},{2,3},{3,2},{4,5},{5,4},{6,7},{7,6},{8,9},{9,8},{10,11... | collective-permute-start | bytes 786440 | tf_op jit(solution)/shard_map/ppermute | solution.py:226
  2.1 9.5 %collective-permute-start = (bf16[2,8,64,128]{3,2,1,0:T(8,128)(2,1)S(1)}, bf16[2,8,64,128]{3,2,1,0:T(8,128)(2,1)S(1)}, u32[]{:S(2)}, u32[]{:S(2)}) collective-permute-start(bf16[2,8,64,128]{3,2,1,0:T(8,128)(2,1)S(1)} %bitcast.139), channel_id=1, source_target_pairs={{0,2},{1,3},{2,0},{3,1},{4,6},{5,7},{6,4},{7,5},{8,10},{9,11},{10,... | collective-permute-start | bytes 786440 | tf_op jit(solution)/shard_map/ppermute | solution.py:226
  5.8 5.6 %collective-permute-start.2 = (bf16[8,64,128]{2,1,0:T(8,128)(2,1)S(1)}, bf16[8,64,128]{2,1,0:T(8,128)(2,1)S(1)}, u32[]{:S(2)}, u32[]{:S(2)}) collective-permute-start(bf16[8,64,128]{2,1,0:T(8,128)(2,1)S(1)} %get-tuple-element.57), channel_id=1, source_target_pairs={{0,4},{4,0},{8,12},{12,8},{16,20},{20,16},{24,28},{28,24},{1,5},{5... | collective-permute-start | bytes 393224 | tf_op jit(solution)/shard_map/ppermute | solution.py:226
  7.3 4.1 %collective-permute-start.3 = (bf16[8,64,128]{2,1,0:T(8,128)(2,1)S(1)}, bf16[8,64,128]{2,1,0:T(8,128)(2,1)S(1)}, u32[]{:S(2)}, u32[]{:S(2)}) collective-permute-start(bf16[8,64,128]{2,1,0:T(8,128)(2,1)S(1)} %get-tuple-element.56), channel_id=1, source_target_pairs={{4,8},{12,16},{20,24},{8,4},{16,12},{24,20},{5,9},{13,17},{21,25},... | collective-permute-start | bytes 393224 | tf_op jit(solution)/shard_map/ppermute | solution.py:232
  11.6 7.2 %collective-permute-start.4 = (bf16[2,8,64,128]{3,2,1,0:T(8,128)(2,1)S(1)}, bf16[2,8,64,128]{3,2,1,0:T(8,128)(2,1)S(1)}, u32[]{:S(2)}, u32[]{:S(2)}) collective-permute-start(bf16[2,8,64,128]{3,2,1,0:T(8,128)(2,1)S(1)} %collective-permute-done.own.far_own), channel_id=1, source_target_pairs={{0,1},{1,0},{2,3},{3,2},{4,5},{5,4},{6,7},{7,6},{8,9},{9,8},{10,11... | collective-permute-start | bytes 786440 | tf_op jit(solution)/shard_map/ppermute | solution.py:226
  14.3 9.0 %copy-start = (bf16[27,64,256]{2,1,0:T(8,128)(2,1)S(1)}, bf16[27,64,256]{2,1,0:T(8,128)(2,1)}, u32[]{:S(2)}) copy-start(bf16[27,64,256]{2,1,0:T(8,128)(2,1)} %taps.3) | copy-start | bytes 2654212
  14.5 11.9 %collective-permute-start.6 = (f16[4,28,8,128]{3,2,1,0:T(8,128)(2,1)S(1)}, f16[4,28,8,128]{3,2,1,0:T(8,128)(2,1)S(1)}, u32[]{:S(2)}, u32[]{:S(2)}) collective-permute-start(f16[4,28,8,128]{3,2,1,0:T(8,128)(2,1)S(1)} %multiply_convert_fusion.1), channel_id=1, source_target_pairs={{0,4},{4,0},{8,12},{12,8},{16,20},{20,16},{24,28},{28,24},{1,5},{5... | collective-permute-start | bytes 688136 | tf_op jit(solution)/shard_map/ppermute | solution.py:226
  21.7 7.8 %collective-permute-start.5 = (f16[4,28,8,128]{3,2,1,0:T(8,128)(2,1)S(1)}, f16[4,28,8,128]{3,2,1,0:T(8,128)(2,1)S(1)}, u32[]{:S(2)}, u32[]{:S(2)}) collective-permute-start(f16[4,28,8,128]{3,2,1,0:T(8,128)(2,1)S(1)} %multiply_convert_fusion), channel_id=1, source_target_pairs={{0,8},{4,12},{8,0},{12,4},{16,24},{20,28},{24,16},{28,20},{1,9},{5... | collective-permute-start | bytes 688136 | tf_op jit(solution)/shard_map/ppermute | solution.py:226
  26.3 5.0 %collective-permute-start.9 = (f32[2,2,8,64,128]{4,3,2,1,0:T(8,128)S(1)}, f32[2,2,8,64,128]{4,3,2,1,0:T(8,128)S(1)}, u32[]{:S(2)}, u32[]{:S(2)}) collective-permute-start(f32[2,2,8,64,128]{4,3,2,1,0:T(8,128)S(1)} %dynamic-slice_bitcast_fusion), channel_id=1, source_target_pairs={{0,1},{1,0},{2,3},{3,2},{4,5},{5,4},{6,7},{7,6},{8,9},{9,8},{10,11... | collective-permute-start | bytes 3145736 | tf_op jit(solution)/shard_map/ppermute | solution.py:226
  26.8 5.6 %collective-permute-start.8 = (f16[2,28,8,128]{3,2,1,0:T(8,128)(2,1)S(1)}, f16[2,28,8,128]{3,2,1,0:T(8,128)(2,1)S(1)}, u32[]{:S(2)}, u32[]{:S(2)}) collective-permute-start(f16[2,28,8,128]{3,2,1,0:T(8,128)(2,1)S(1)} %multiply_convert_fusion.3), channel_id=1, source_target_pairs={{0,8},{4,12},{8,0},{12,4},{16,24},{20,28},{24,16},{28,20},{1,9},{5... | collective-permute-start | bytes 344072 | tf_op jit(solution)/shard_map/ppermute | solution.py:226
  29.9 5.1 %collective-permute-start.7 = (f16[2,28,8,128]{3,2,1,0:T(8,128)(2,1)S(1)}, f16[2,28,8,128]{3,2,1,0:T(8,128)(2,1)S(1)}, u32[]{:S(2)}, u32[]{:S(2)}) collective-permute-start(f16[2,28,8,128]{3,2,1,0:T(8,128)(2,1)S(1)} %multiply_convert_fusion.2), channel_id=1, source_target_pairs={{0,4},{4,0},{8,12},{12,8},{16,20},{20,16},{24,28},{28,24},{1,5},{5... | collective-permute-start | bytes 344072 | tf_op jit(solution)/shard_map/ppermute | solution.py:226
  32.7 9.0 %collective-permute-start.11 = (f16[1,28,8,128]{3,2,1,0:T(8,128)(2,1)S(1)}, f16[1,28,8,128]{3,2,1,0:T(8,128)(2,1)S(1)}, u32[]{:S(2)}, u32[]{:S(2)}) collective-permute-start(f16[1,28,8,128]{3,2,1,0:T(8,128)(2,1)S(1)} %multiply_convert_fusion.7), channel_id=1, source_target_pairs={{0,16},{4,20},{8,24},{12,28},{16,0},{20,4},{24,8},{28,12},{1,17},{... | collective-permute-start | bytes 172040 | tf_op jit(solution)/shard_map/ppermute | solution.py:226
  35.3 7.3 %collective-permute-start.10 = (f16[1,28,8,128]{3,2,1,0:T(8,128)(2,1)S(1)}, f16[1,28,8,128]{3,2,1,0:T(8,128)(2,1)S(1)}, u32[]{:S(2)}, u32[]{:S(2)}) collective-permute-start(f16[1,28,8,128]{3,2,1,0:T(8,128)(2,1)S(1)} %multiply_convert_fusion.6), channel_id=1, source_target_pairs={{0,16},{4,20},{8,24},{12,28},{16,0},{20,4},{24,8},{28,12},{1,17},{... | collective-permute-start | bytes 172040 | tf_op jit(solution)/shard_map/ppermute | solution.py:226
  37.7 14.7 %collective-permute-start.16 = (f32[2,8,64,128]{3,1,2,0:T(8,128)S(1)}, f32[2,8,64,128]{3,1,2,0:T(8,128)S(1)}, u32[]{:S(2)}, u32[]{:S(2)}) collective-permute-start(f32[2,8,64,128]{3,1,2,0:T(8,128)S(1)} %bitcast.148), channel_id=1, source_target_pairs={{0,2},{1,3},{2,0},{3,1},{4,6},{5,7},{6,4},{7,5},{8,10},{9,11},{10,... | collective-permute-start | bytes 1572872 | tf_op jit(solution)/shard_map/ppermute | solution.py:226
  41.9 5.1 %collective-permute-start.13 = (f16[1,28,8,128]{3,2,1,0:T(8,128)(2,1)S(1)}, f16[1,28,8,128]{3,2,1,0:T(8,128)(2,1)S(1)}, u32[]{:S(2)}, u32[]{:S(2)}) collective-permute-start(f16[1,28,8,128]{3,2,1,0:T(8,128)(2,1)S(1)} %multiply_convert_fusion.5), channel_id=1, source_target_pairs={{0,16},{4,20},{8,24},{12,28},{16,0},{20,4},{24,8},{28,12},{1,17},{... | collective-permute-start | bytes 172040 | tf_op jit(solution)/shard_map/ppermute | solution.py:226
  42.9 7.3 %collective-permute-start.15 = (f16[1,28,8,128]{3,2,1,0:T(8,128)(2,1)S(1)}, f16[1,28,8,128]{3,2,1,0:T(8,128)(2,1)S(1)}, u32[]{:S(2)}, u32[]{:S(2)}) collective-permute-start(f16[1,28,8,128]{3,2,1,0:T(8,128)(2,1)S(1)} %multiply_convert_fusion.4), channel_id=1, source_target_pairs={{0,16},{4,20},{8,24},{12,28},{16,0},{20,4},{24,8},{28,12},{1,17},{... | collective-permute-start | bytes 172040 | tf_op jit(solution)/shard_map/ppermute | solution.py:226
  45.2 17.0 %collective-permute-start.12 = (f32[8,64,128]{2,1,0:T(8,128)S(1)}, f32[8,64,128]{2,1,0:T(8,128)S(1)}, u32[]{:S(2)}, u32[]{:S(2)}) collective-permute-start(f32[8,64,128]{2,1,0:T(8,128)S(1)} %get-tuple-element.39), channel_id=1, source_target_pairs={{4,8},{12,16},{20,24},{8,4},{16,12},{24,20},{5,9},{13,17},{21,25},... | collective-permute-start | bytes 786440 | tf_op jit(solution)/shard_map/ppermute | solution.py:232
  47.1 9.2 %collective-permute-start.14 = (f16[2,28,8,128]{3,2,1,0:T(8,128)(2,1)S(1)}, f16[2,28,8,128]{3,2,1,0:T(8,128)(2,1)S(1)}, u32[]{:S(2)}, u32[]{:S(2)}) collective-permute-start(f16[2,28,8,128]{3,2,1,0:T(8,128)(2,1)S(1)} %pad_maximum_fusion.2), channel_id=1, source_target_pairs={{0,8},{4,12},{8,0},{12,4},{16,24},{20,28},{24,16},{28,20},{1,9},{5... | collective-permute-start | bytes 344072 | tf_op jit(solution)/shard_map/ppermute | solution.py:226
  50.2 6.3 %collective-permute-start.19 = (f16[2,28,8,128]{3,2,1,0:T(8,128)(2,1)S(1)}, f16[2,28,8,128]{3,2,1,0:T(8,128)(2,1)S(1)}, u32[]{:S(2)}, u32[]{:S(2)}) collective-permute-start(f16[2,28,8,128]{3,2,1,0:T(8,128)(2,1)S(1)} %pad_maximum_fusion.3), channel_id=1, source_target_pairs={{0,4},{4,0},{8,12},{12,8},{16,20},{20,16},{24,28},{28,24},{1,5},{5... | collective-permute-start | bytes 344072 | tf_op jit(solution)/shard_map/ppermute | solution.py:226
  51.0 11.1 %collective-permute-start.17 = (f32[8,64,128]{2,1,0:T(8,128)S(1)}, f32[8,64,128]{2,1,0:T(8,128)S(1)}, u32[]{:S(2)}, u32[]{:S(2)}) collective-permute-start(f32[8,64,128]{2,1,0:T(8,128)S(1)} %get-tuple-element.46), channel_id=1, source_target_pairs={{0,4},{4,0},{8,12},{12,8},{16,20},{20,16},{24,28},{28,24},{1,5},{5... | collective-permute-start | bytes 786440 | tf_op jit(solution)/shard_map/ppermute | solution.py:226
  56.3 9.4 %collective-permute-start.18 = (f16[4,28,8,128]{3,2,1,0:T(8,128)(2,1)S(1)}, f16[4,28,8,128]{3,2,1,0:T(8,128)(2,1)S(1)}, u32[]{:S(2)}, u32[]{:S(2)}) collective-permute-start(f16[4,28,8,128]{3,2,1,0:T(8,128)(2,1)S(1)} %get-tuple-element.63), channel_id=1, source_target_pairs={{0,4},{4,0},{8,12},{12,8},{16,20},{20,16},{24,28},{28,24},{1,5},{5... | collective-permute-start | bytes 688136 | tf_op jit(solution)/shard_map/ppermute | solution.py:226
  56.7 6.6 %collective-permute-start.20 = (f16[4,28,8,128]{3,2,1,0:T(8,128)(2,1)S(1)}, f16[4,28,8,128]{3,2,1,0:T(8,128)(2,1)S(1)}, u32[]{:S(2)}, u32[]{:S(2)}) collective-permute-start(f16[4,28,8,128]{3,2,1,0:T(8,128)(2,1)S(1)} %get-tuple-element.60), channel_id=1, source_target_pairs={{0,8},{4,12},{8,0},{12,4},{16,24},{20,28},{24,16},{28,20},{1,9},{5... | collective-permute-start | bytes 688136 | tf_op jit(solution)/shard_map/ppermute | solution.py:226
